TPU v7x, 512 devices: a whole 4x4x16 slice. The times are simulated.
512 devices in a mesh: dom: 16 (over z_hi, y, core), edge: 32 (over z_lo, x).
Axes of the slice: x: 4, y: 4, z: 16 (z_hi: 2, z_lo: 8; z = z_hi * 8 + z_lo), core: 2. Of those that a mesh axis runs over, the one named last changes fastest.
Arguments:
- entities: float32 [65536, 400], P(('dom', 'edge')), may hold values from -2 to 2
- entity_state: float32 [65536], P(('dom', 'edge')), may hold values from 0.0001 to 0.1
- relations: float32 [672, 400], replicated, may hold values from -4 to 4
- relation_state: float32 [672, 400], replicated, may hold values from 0.01 to 1
- live_blocks: int32 [2, 512], P(None, ('dom', 'edge')), may hold values from 1 to 10, as said below
- dst_blocks: int32 [2, 5120], P(None, ('dom', 'edge')), may hold values from 0 to 31
- relation_ids: int32 [2, 5120], P(None, ('dom', 'edge')), may hold values from 0 to 671
- source_rows: int32 [2, 5120, 128], P(None, ('dom', 'edge')), may hold values from 0 to 127
- target_rows: int32 [2, 5120, 128], P(None, ('dom', 'edge')), may hold values from 0 to 127
- negative_blocks: int32 [2, 5120, 4], P(None, ('dom', 'edge')), may hold values from 0 to 31
Outputs:
- new_entities: float32 [65536, 400], P(('dom', 'edge'))
- new_entity_state: float32 [65536], P(('dom', 'edge'))
- new_relations: float32 [672, 400], replicated
- new_relation_state: float32 [672, 400], replicated
Inputs may be any that keep to these rules, and one draw needn't show every extreme that they name: live_blocks[r, v] slots of device v are used in round r; in every round some device uses all 10 of them.
All inputs are finite; a program needn't handle non-finite values.
Results may differ from a plain program's by a relative error of at most 0.008.
Values may be sent and summed in bfloat16 or wider, within the bound.
No kernel may reach another device: no remote copies, remote signals or barrier semaphores. Data moves between devices by JAX's collectives and lax.ppermute only.
A program may use at most 128 MiB of HBM per device.

v0:
```python
import jax
import jax.numpy as jnp
from jax import lax
from jax.sharding import PartitionSpec as P

ROUNDS = 2


ENT_RATE = 0.25
REL_RATE = 0.25


def shifted(value, axis, steps):
    count = lax.axis_size(axis)
    pairs = [(source, (source + steps) % count) for source in range(count)]
    return lax.ppermute(value, axis, pairs)


def edge_block(own_rows, part3, relations, rel, src, tgt, dst, negs):
    block, width = own_rows.shape
    half = width // 2
    places = jnp.arange(block, dtype=jnp.int32)
    src_hot = (src[:, None] == places[None, :]).astype(jnp.bfloat16)
    tgt_hot = (tgt[:, None] == places[None, :]).astype(jnp.bfloat16)
    heads = jnp.dot(src_hot, own_rows, preferred_element_type=jnp.float32)
    target_block = lax.dynamic_index_in_dim(part3, dst, 0, keepdims=False)
    tails = jnp.dot(tgt_hot, target_block, preferred_element_type=jnp.float32)
    operator = lax.dynamic_index_in_dim(relations, rel, 0, keepdims=False)
    h_re, h_im = (heads[:, :half], heads[:, half:])
    r_re, r_im = (operator[:half], operator[half:])
    query = jnp.concatenate([h_re * r_re - h_im * r_im, h_re * r_im + h_im * r_re], 1).astype(
        jnp.bfloat16
    )
    query_f = query.astype(jnp.float32)
    positive = jnp.sum(query_f * tails, 1)
    negatives = jnp.take(part3, negs, axis=0).reshape(-1, width)
    scores = lax.dot_general(
        query, negatives, (((1,), (1,)), ((), ())), preferred_element_type=jnp.float32
    )
    pos_weight = -jax.nn.sigmoid(-positive)
    neg_weight = (jax.nn.sigmoid(scores) / scores.shape[1]).astype(jnp.bfloat16)
    grad_query = pos_weight[:, None] * tails + jnp.dot(
        neg_weight, negatives, preferred_element_type=jnp.float32
    )
    tgt_add = jnp.zeros((block, width), jnp.float32).at[tgt].add(pos_weight[:, None] * query_f)
    neg_add = lax.dot_general(
        neg_weight, query, (((0,), (0,)), ((), ())), preferred_element_type=jnp.float32
    )
    neg_add = neg_add.reshape(negs.shape[0], block, width)
    g_re, g_im = (grad_query[:, :half], grad_query[:, half:])
    head_grad = jnp.concatenate([g_re * r_re + g_im * r_im, g_im * r_re - g_re * r_im], 1)
    lhs_add = jnp.zeros((block, width), jnp.float32).at[src].add(head_grad)
    rel_add = jnp.concatenate(
        [jnp.sum(g_re * h_re + g_im * h_im, 0), jnp.sum(g_im * h_re - g_re * h_im, 0)]
    )
    return (lhs_add, tgt_add, neg_add, rel_add)


def run_blocks(own_rows, part3, relations, lists, start, stop, mapper):
    dst_all, rel_all, src_all, tgt_all, neg_all = lists
    width = part3.shape[2]

    def step(k, carry):
        rhs_part, lhs_part, rel_rows = carry
        slot, side = mapper(k)
        rows = lax.dynamic_index_in_dim(own_rows, side, 0, keepdims=False)
        lhs_add, tgt_add, neg_add, rel_add = edge_block(
            rows,
            part3,
            relations,
            rel_all[slot],
            src_all[slot],
            tgt_all[slot],
            dst_all[slot],
            neg_all[slot],
        )
        rhs_part = rhs_part.at[dst_all[slot]].add(tgt_add)
        rhs_part = rhs_part.at[neg_all[slot]].add(neg_add)
        lhs_part = lhs_part.at[side].add(lhs_add)
        rel_rows = rel_rows.at[slot].set(rel_add)
        return (rhs_part, lhs_part, rel_rows)

    init = (
        jnp.zeros(part3.shape, jnp.float32),
        jnp.zeros(own_rows.shape, jnp.float32),
        jnp.zeros((dst_all.shape[0], width), jnp.float32),
    )
    return lax.fori_loop(start, stop, step, init)


def shards(
    entities,
    entity_state,
    relations,
    relation_state,
    live_blocks,
    dst_blocks,
    relation_ids,
    source_rows,
    target_rows,
    negative_blocks,
):
    weights, state, rel, rel_state = (entities, entity_state, relations, relation_state)
    block, width = weights.shape
    parts = lax.axis_size("edge")
    for r in range(ROUNDS):
        own_b = weights.astype(jnp.bfloat16)
        if r > 0:
            visiting = shifted(own_b, "dom", -r)
        else:
            visiting = own_b
        part3 = lax.all_gather(visiting, "edge", axis=0, tiled=True).reshape(parts, block, width)
        mine = (dst_blocks[r], relation_ids[r], source_rows[r], target_rows[r], negative_blocks[r])
        count = live_blocks[r, 0]

        def mapper(k):
            return (k, 0)

        rhs_part, lhs_part, rel_rows = run_blocks(own_b[None], part3, rel, mine, 0, count, mapper)
        lhs_grad = lhs_part[0]
        rel_ids = relation_ids[r]
        partial_value = rhs_part.astype(jnp.bfloat16)
        pieces = lax.all_to_all(partial_value, "edge", split_axis=0, concat_axis=0, tiled=True)
        rhs_grad = jnp.sum(pieces, axis=0, dtype=jnp.float32)
        if r > 0:
            rhs_grad = shifted(rhs_grad.astype(jnp.bfloat16), "dom", r).astype(rhs_grad.dtype)
        grads = lhs_grad + rhs_grad
        state = state + jnp.mean(grads * grads, axis=1)
        weights = weights - ENT_RATE * grads / jnp.sqrt(state)[:, None]
        rel_grad = jnp.zeros(rel.shape, jnp.float32).at[rel_ids].add(rel_rows)
        rel_grad = lax.psum(rel_grad, ("dom", "edge"))
        rel_state = rel_state + rel_grad * rel_grad
        rel = rel - REL_RATE * rel_grad / jnp.sqrt(rel_state)
    return (weights, state, rel, rel_state)


def solution(mesh):
    placed = (
        P(("dom", "edge"), None),
        P(("dom", "edge")),
        P(),
        P(),
        P(None, ("dom", "edge")),
        P(None, ("dom", "edge")),
        P(None, ("dom", "edge")),
        P(None, ("dom", "edge"), None),
        P(None, ("dom", "edge"), None),
        P(None, ("dom", "edge"), None),
    )
    return jax.shard_map(
        shards,
        mesh=mesh,
        in_specs=placed,
        out_specs=(P(("dom", "edge"), None), P(("dom", "edge")), P(), P()),
        check_vma=False,
    )
```

profile of v0, /device:TPU:1, one launch (start us, length us, event | category | flops | bytes accessed | tf_op | source)
XLA Modules:
  0.0 2081.2 jit_solution(1264024629895854190)
XLA Ops:
  7.2 1.7 copy.40
  9.0 2.9 copy.41
  14.3 209.8 %all-gather.3.cloned.1.call-done = bf16[4096,400]{1,0:T(8,128)(2,1)} async-done(((bf16[128,400]{1,0:T(8,128)(2,1)}), bf16[4096,400]{1,0:T(8,128)(2,1)}) %all-gather.3.cloned.1.call-update) | async-done | bytes 3276816 | tf_op jit(solution)/shard_map/all_gather | solution.py:112
  224.2 3.2 broadcast.474.clone
  227.4 97.3 %while.40 = (s32[]{:T(128)}, f32[32,128,400]{1,2,0:T(8,128)}, f32[1,128,400]{2,1,0:T(8,128)S(1)}, f32[10,400]{1,0:T(8,128)S(1)}, s32[]{:T(128)}, /*index=5*/s32[...) while((s32[]{:T(128)}, f32[32,128,400]{1,2,0:T(8,128)}, ...), condition=%wide.region_9.11_spmd, body=%wide.region_0.10_spmd.sunk | while | flops 186218976 | bytes 27180840 | solution.py:88
  236.0 1.4 scatter_custom_fusion.26
  237.4 8.5 copy.80
  246.7 1.6 add_select_fusion.4
  249.2 2.8 gather_fusion
  252.8 3.1 scatter_fusion
  256.5 1.4 scatter_custom_fusion.28
  268.3 1.4 scatter_custom_fusion.26
  269.7 8.5 copy.80
  278.9 1.6 add_select_fusion.4
  281.4 2.8 gather_fusion
  285.0 3.0 scatter_fusion
  288.7 1.4 scatter_custom_fusion.28
  300.5 1.4 scatter_custom_fusion.26
  301.9 8.5 copy.80
  311.2 1.6 add_select_fusion.4
  313.6 2.8 gather_fusion
  317.2 3.1 scatter_fusion
  321.0 1.4 scatter_custom_fusion.28
  324.8 5.0 convert_element_type.63
  329.8 147.8 %all-to-all-start = ((bf16[32,128,400]{1,2,0:T(8,128)(2,1)}), bf16[32,128,400]{1,2,0:T(8,128)(2,1)S(1)}, u32[]{:S(2)}, u32[]{:S(2)}) async-start(bf16[32,128,400]{1,2,0:T(8,128)(2,1)} %convert_element_type.63), calls=%async_computation | async-start | bytes 6553600 | tf_op jit(solution)/shard_map/all_to_all | solution.py:123
  479.7 2.0 scatter_custom_fusion.6
  481.8 138.4 %all-to-all-done = bf16[32,128,400]{1,2,0:T(8,128)(2,1)S(1)} async-done(((bf16[32,128,400]{1,2,0:T(8,128)(2,1)}), bf16[32,128,400]{1,2,0:T(8,128)(2,1)S(1)}, u32[]{:S(2)}, u32[]{:S(2)}) %all-to-all-start) | async-done | bytes 3276832 | tf_op jit(solution)/shard_map/all_to_all | solution.py:123
  621.8 9.5 collective-permute-start
  632.9 1.7 copy.46
  634.8 403.4 %all-reduce.3.cloned.1.call-done = f32[672,400]{1,0:T(8,128)} async-done(((f32[672,400]{1,0:T(8,128)}), f32[672,400]{1,0:T(8,128)}) %all-reduce.3.cloned.1.call-update) | async-done | bytes 1075216 | tf_op jit(solution)/shard_map/psum | solution.py:131
  1038.2 2.9 multiply_subtract_fusion.3
  1041.3 169.1 %all-gather.5.cloned.1.call-done = bf16[4096,400]{0,1:T(8,128)(2,1)} async-done(((bf16[128,400]{0,1:T(8,128)(2,1)}), bf16[4096,400]{0,1:T(8,128)(2,1)}) %all-gather.5.cloned.1.call-update) | async-done | bytes 3276816 | tf_op jit(solution)/shard_map/all_gather | solution.py:112
  1210.4 6.0 copy.54
  1216.4 3.2 broadcast.474
  1219.7 128.2 %while.41 = (s32[]{:T(128)}, f32[32,128,400]{1,2,0:T(8,128)}, f32[1,128,400]{2,1,0:T(8,128)S(1)}, f32[10,400]{1,0:T(8,128)S(1)}, s32[]{:T(128)}, /*index=5*/s32[...) while((s32[]{:T(128)}, f32[32,128,400]{1,2,0:T(8,128)}, ...), condition=%wide.region_23.25_spmd, body=%wide.region_14.24_spmd.sunk | while | flops 186218976 | bytes 27180840 | solution.py:88
  1228.3 1.4 scatter_custom_fusion.31
  1229.7 8.5 copy.85
  1238.9 1.6 add_select_fusion.5
  1241.4 2.8 gather_fusion.1
  1245.0 3.0 scatter_fusion.1
  1248.8 1.4 scatter_custom_fusion.33
  1261.6 8.5 copy.85
  1270.8 1.6 add_select_fusion.5
  1273.3 2.8 gather_fusion.1
  1276.9 3.1 scatter_fusion.1
  1280.7 1.4 scatter_custom_fusion.33
  1293.5 8.5 copy.85
  1302.7 1.6 add_select_fusion.5
  1305.2 2.8 gather_fusion.1
  1308.8 3.0 scatter_fusion.1
  1325.3 8.5 copy.85
  1334.5 1.6 add_select_fusion.5
  1337.0 2.8 gather_fusion.1
  1340.6 3.0 scatter_fusion.1
  1344.3 1.4 scatter_custom_fusion.33
  1347.9 5.0 convert_element_type.66
  1352.9 137.1 %all-to-all-start.1 = ((bf16[32,128,400]{1,2,0:T(8,128)(2,1)}), bf16[32,128,400]{1,2,0:T(8,128)(2,1)S(1)}, u32[]{:S(2)}, u32[]{:S(2)}) async-start(bf16[32,128,400]{1,2,0:T(8,128)(2,1)} %convert_element_type.66), calls=%async_computation.1 | async-start | bytes 6553600 | tf_op jit(solution)/shard_map/all_to_all | solution.py:123
  1490.0 2.0 scatter_custom_fusion.7
  1492.9 129.9 %all-to-all-done.1 = bf16[32,128,400]{1,2,0:T(8,128)(2,1)S(1)} async-done(((bf16[32,128,400]{1,2,0:T(8,128)(2,1)}), bf16[32,128,400]{1,2,0:T(8,128)(2,1)S(1)}, u32[]{:S(2)}, u32[]{:S(2)}) %all-to-all-start.1) | async-done | bytes 3276832 | tf_op jit(solution)/shard_map/all_to_all | solution.py:123
  1623.3 34.4 %collective-permute-start.1 = (bf16[128,400]{0,1:T(8,128)(2,1)S(1)}, bf16[128,400]{0,1:T(8,128)(2,1)S(1)}, u32[]{:S(2)}, u32[]{:S(2)}) collective-permute-start(bf16[128,400]{0,1:T(8,128)(2,1)S(1)} %reduce_sum.119), channel_id=1, source_target_pairs={{0,32},{32,64},{64,96},{96,128},{128,160},{160,192},{192,224},{224... | collective-permute-start | bytes 307208 | tf_op jit(solution)/shard_map/ppermute | solution.py:16
  1657.8 409.4 %all-reduce.5.cloned.1.call-done = f32[672,400]{1,0:T(8,128)} async-done(((f32[672,400]{1,0:T(8,128)}), f32[672,400]{1,0:T(8,128)}) %all-reduce.5.cloned.1.call-update) | async-done | bytes 1075216 | tf_op jit(solution)/shard_map/psum | solution.py:131
  2067.2 3.3 multiply_subtract_fusion.2
  2070.4 1.5 copy.52
  2071.9 1.5 copy.53
  (301 shorter events, 76.7 us)
Async XLA Ops:
  7.2 217.0 %all-gather.3.cloned.1.call-start = ((), (), s32[]{:S(2)}) async-start(), calls=%async_computation.2 | async-start | bytes 4325376 | tf_op jit(solution)/shard_map/all_gather | solution.py:112
  8.9 2.9 copy-start.16
  8.9 3.6 copy-start.20
  8.9 4.2 copy-start.17
  8.9 4.2 copy-start.21
  8.9 4.8 copy-start.13
  8.9 4.8 copy-start.14
  224.2 3.2 copy-start.1
  224.2 3.2 copy-start.10
  224.2 3.3 copy-start.11
  324.8 5.0 copy-start.8
  329.8 290.4 %all-to-all-start = ((bf16[32,128,400]{1,2,0:T(8,128)(2,1)}), bf16[32,128,400]{1,2,0:T(8,128)(2,1)S(1)}, u32[]{:S(2)}, u32[]{:S(2)}) async-start(bf16[32,128,400]{1,2,0:T(8,128)(2,1)} %convert_element_type.63), calls=%async_computation | async-start | bytes 6553600 | tf_op jit(solution)/shard_map/all_to_all | solution.py:123
  477.6 560.6 %all-reduce.3.cloned.1.call-start = ((), (), s32[]{:S(2)}) async-start(), calls=%async_computation.3 | async-start | bytes 2752512 | tf_op jit(solution)/shard_map/psum | solution.py:131
  481.7 138.9 %copy-start.4 = (f32[1,128,400]{1,2,0:T(8,128)S(1)}, f32[1,128,400]{1,2,0:T(8,128)}, u32[]{:S(2)}) copy-start(f32[1,128,400]{1,2,0:T(8,128)} %copy.43) | copy-start | bytes 614404
  481.8 139.0 %copy-start.22 = (f32[128]{0:T(128)S(1)}, f32[128]{0:T(128)}, u32[]{:S(2)}) copy-start(f32[128]{0:T(128)} %param.29) | copy-start | bytes 1540
  481.8 728.6 %all-gather.5.cloned.1.call-start = ((), (), s32[]{:S(2)}) async-start(), calls=%async_computation.4 | async-start | bytes 3379200 | tf_op jit(solution)/shard_map/all_gather | solution.py:112
  620.2 0.9 copy-start.6
  620.7 13.9 copy-start.18
  621.8 12.8 copy-start.15
  621.8 12.9 copy-start.12
  621.8 10.4 collective-permute-start
  632.3 0.6 copy-start.7
  632.3 405.9 %copy-start.2 = (f32[672,400]{1,0:T(8,128)S(1)}, f32[672,400]{1,0:T(8,128)}, u32[]{:S(2)}) copy-start(f32[672,400]{1,0:T(8,128)} %get-tuple-element.1027) | copy-start | bytes 3225604
  634.6 406.5 %copy-start = (f32[672,400]{1,0:T(8,128)}, f32[672,400]{1,0:T(8,128)S(1)}, u32[]{:S(2)}) copy-start(f32[672,400]{1,0:T(8,128)S(1)} %copy.46) | copy-start | bytes 3225604
  1216.4 3.2 copy-start.24
  1216.4 3.2 copy-start.25
  1347.9 5.0 copy-start.9
  1352.9 270.0 %all-to-all-start.1 = ((bf16[32,128,400]{1,2,0:T(8,128)(2,1)}), bf16[32,128,400]{1,2,0:T(8,128)(2,1)S(1)}, u32[]{:S(2)}, u32[]{:S(2)}) async-start(bf16[32,128,400]{1,2,0:T(8,128)(2,1)} %convert_element_type.66), calls=%async_computation.1 | async-start | bytes 6553600 | tf_op jit(solution)/shard_map/all_to_all | solution.py:123
  1490.0 577.2 %all-reduce.5.cloned.1.call-start = ((), (), s32[]{:S(2)}) async-start(), calls=%async_computation.5 | async-start | bytes 2752512 | tf_op jit(solution)/shard_map/psum | solution.py:131
  1623.3 450.0 %collective-permute-start.1 = (bf16[128,400]{0,1:T(8,128)(2,1)S(1)}, bf16[128,400]{0,1:T(8,128)(2,1)S(1)}, u32[]{:S(2)}, u32[]{:S(2)}) collective-permute-start(bf16[128,400]{0,1:T(8,128)(2,1)S(1)} %reduce_sum.119), channel_id=1, source_target_pairs={{0,32},{32,64},{64,96},{96,128},{128,160},{160,192},{192,224},{224... | collective-permute-start | bytes 307208 | tf_op jit(solution)/shard_map/ppermute | solution.py:16
  2071.9 1.5 copy-start.3
  2071.9 1.6 copy-start.19
  2071.9 1.6 copy-start.23
  2071.9 2.1 copy-start.5
Sparse Core Ops, SparseCore 0:
  10.7 213.4 all-gather.2
  483.8 554.3 all-reduce.2
  1040.8 169.5 all-gather.4
  1495.9 571.1 all-reduce.4
where the time goes:
time: 2090 us; the launch traced here: 2080 us
  waiting for transfers between devices  1460 us (70%)
  starting transfers between devices  329 us (16%)
  local copies, waits for them, and re-layouts  129 us (6%)
  other arithmetic  96.7 us (5%)
  loops' own time  34.6 us (2%)
    psum x2, waiting for transfers between devices, shards(): rel_grad = lax.psum(rel_grad, ('dom', 'edge'))  813 us
    all_gather x2, waiting for transfers between devices, shards(): lax.all_gather(visiting, 'edge', axis=0, tiled=True)  379 us
    all_to_all x2, starting transfers between devices, shards(): lax.all_to_all(partial_value, 'edge', split_axis=0, concat_axis=0, tiled=...  285 us
    all_to_all x2, waiting for transfers between devices, shards(): lax.all_to_all(partial_value, 'edge', split_axis=0, concat_axis=0, tiled=...  268 us
    another operation x20, local copies, waits for them, and re-layouts  66.7 us
    ppermute x2, starting transfers between devices, shifted(): return lax.ppermute(value, axis, pairs)  43.9 us
  transfers between devices with their start and end apart: 8, of which 7 were waited for; matrix products, arithmetic and copies ran while one was open for 1% of the time, Pallas kernels for 0%

commit v1 on v0

v1 whole, which is shorter than its diff:
```python
import jax
import jax.numpy as jnp
from jax import lax
from jax.experimental import pallas as pl
from jax.experimental.pallas import tpu as pltpu
from jax.sharding import PartitionSpec as P

AXES = ("dom", "edge")
N_DOM, N_EDGE = 16, 32
ENT_RATE = 0.25
REL_RATE = 0.25
F32, BF16 = jnp.float32, jnp.bfloat16
GROUP = 16
PIECE = 80
FOLD = 112
DIGIT = 32
LISTS = 32
MIB = 1024 * 1024


def coords(v):
    dom, edge = v // N_EDGE, v % N_EDGE
    return edge % 4, (dom // 2) % 4, dom // 8, edge // 4, dom % 2


def place(x, y, z_hi, z_lo, core):
    return ((z_hi * 4 + y) * 2 + core) * N_EDGE + z_lo * 4 + x


def turn(v):
    x, y, z_hi, z_lo, core = coords(v)
    return place(x, z_lo % 4, z_hi, y + 4 * core, z_lo // 4)


def ahead(v):
    dom, edge = v // N_EDGE, v % N_EDGE
    return turn((dom + 1) % N_DOM * N_EDGE + edge)


ALL = range(N_DOM * N_EDGE)
TURN = [(v, turn(v)) for v in ALL]
AHEAD = [(v, ahead(v)) for v in ALL]
BACK = [(ahead(v), v) for v in ALL]
NEXT = [(turn(v), ahead(v)) for v in ALL]


OTHER = []
for v in ALL:
    x, y, z_hi, z_lo, core = coords(v)
    OTHER.append((v, place(x, y, z_hi, z_lo, 1 - core)))

PLANES = [[place(c % 4, c // 4 % 4, z // 8, z % 8, c // 16) for c in range(32)] for z in range(16)]
SHEETS = [plane[16 * core : 16 * core + 16] for plane in PLANES for core in range(2)]


def z_pairs(step):
    pairs = []
    for v in ALL:
        x, y, z_hi, z_lo, core = coords(v)
        z = (z_hi * 8 + z_lo) ^ step
        pairs.append((v, place(x, y, z // 8, z % 8, core)))
    return pairs


def send(value, pairs):
    return lax.ppermute(value, AXES, pairs)


def exchange(value, groups):
    return lax.all_to_all(value, AXES, 0, 0, axis_index_groups=groups, tiled=True)


def gather_sheet(own):
    return exchange(jnp.broadcast_to(own, (16,) + own.shape), SHEETS)


def together(*values):
    return lax.optimization_barrier(values)


def nt(a, b):
    return lax.dot_general(a, b, (((1,), (1,)), ((), ())), preferred_element_type=F32)


def nn(a, b):
    return jnp.dot(a, b, preferred_element_type=F32)


def blocks_kernel(
    scal, here, lists, own, rel, half, other, mine_out, theirs_out, lhs_out, rel_out, table, acc, rel_acc, sems
):
    slots = 10
    width, block = own.shape
    mid = width // 2
    copies = [
        pltpu.make_async_copy(src, table.at[pl.ds(16 * i, 16)], sems.at[i])
        for i, src in enumerate((half, other))
    ]
    for copy in copies:
        copy.start()

    def clear(k, carry):
        acc[k] = jnp.zeros((width, block), F32)
        return carry

    lax.fori_loop(0, 32, clear, 0)
    rel_acc[...] = jnp.zeros(rel_acc.shape, F32)
    lhs_out[...] = jnp.zeros(lhs_out.shape, F32)
    for copy in copies:
        copy.wait()

    def near(b):
        return ((b >> 4) ^ here[0]) * 16 + (b & 15)

    rows = lax.broadcasted_iota(jnp.int32, (block, block), 0)
    lanes = lax.broadcasted_iota(jnp.int32, (block, block), 1)

    def step(j, carry):
        src_hot = jnp.where(rows == lists[pl.ds(j, 1), :], 1.0, 0.0).astype(BF16)
        tgt_hot = jnp.where(rows == lists[pl.ds(slots + j, 1), :], 1.0, 0.0).astype(BF16)
        dst, rel_id = near(scal[j]), scal[slots + j] * DIGIT + scal[2 * slots + j]
        negs = [near(scal[3 * slots + 4 * j + i]) for i in range(4)]
        rel_tile = pl.ds(pl.multiple_of((rel_id >> 7) * 128, 128), 128)
        rel_row = jnp.where(rows == (rel_id & 127), 1.0, 0.0).astype(BF16)
        rel_lane = jnp.where(lanes == (rel_id & 127), 1.0, 0.0).astype(BF16)
        heads = nn(own[...], src_hot)
        tails = nn(table[dst], tgt_hot)
        rel_value = rel[:, rel_tile]
        high = rel_value.astype(BF16)
        low = (rel_value - high.astype(F32)).astype(BF16)
        op = nn(high, rel_row) + nn(low, rel_row)
        h_re, h_im = heads[:mid], heads[mid:]
        r_re, r_im = op[:mid], op[mid:]
        query = jnp.concatenate([h_re * r_re - h_im * r_im, h_re * r_im + h_im * r_re], 0).astype(BF16)
        query_f = query.astype(F32)
        positive = jnp.sum(query_f * tails, 0, keepdims=True)
        neg_rows = jnp.concatenate([table[n] for n in negs], 1)
        scores = nn(query_f.T.astype(BF16), neg_rows)
        pos_weight = -jax.nn.sigmoid(-positive)
        neg_weight = (jax.nn.sigmoid(scores) * (1.0 / scores.shape[1])).astype(BF16)
        grad_query = pos_weight * tails + nt(neg_rows, neg_weight)
        neg_add = nn(query, neg_weight)
        for i, n in enumerate(negs):
            acc[n] += neg_add[:, block * i : block * (i + 1)]
        acc[dst] += nt((pos_weight * query_f).astype(BF16), tgt_hot)
        g_re, g_im = grad_query[:mid], grad_query[mid:]
        head_grad = jnp.concatenate([g_re * r_re + g_im * r_im, g_im * r_re - g_re * r_im], 0)
        lhs_out[...] += nt(head_grad.astype(BF16), src_hot)
        op_grad = jnp.concatenate([g_re * h_re + g_im * h_im, g_im * h_re - g_re * h_im], 0)
        rel_acc[:, rel_tile] += nn(op_grad.astype(BF16), rel_lane)
        return carry

    lax.fori_loop(0, scal[7 * slots], step, 0)

    def pack(k, carry):
        mine_out[k] = acc[k].astype(BF16)
        theirs_out[k] = acc[16 + k].astype(BF16)
        return carry

    lax.fori_loop(0, 16, pack, 0)
    tiles = rel_acc.shape[1] // block
    for t in range(tiles - 1):
        rel_out[width * t : width * (t + 1)] = rel_acc[:, block * t : block * (t + 1)].astype(BF16)
    tail = rel_acc[:, block * (tiles - 1) :]
    folded = tail[:FOLD]
    for q in range(1, 4):
        part = tail[FOLD * q : FOLD * (q + 1)]
        if part.shape[0] < FOLD:
            part = jnp.concatenate([part, jnp.zeros((FOLD - part.shape[0], block), F32)], 0)
        folded = folded + pltpu.roll(part, q * block // 4, 1)
    first = width * (tiles - 1)
    rel_out[first : first + FOLD] = folded.astype(BF16)
    rel_out[first + FOLD :] = jnp.zeros((rel_out.shape[0] - first - FOLD, block), BF16)


def run_blocks(lists, here, own, rel, half, other):
    width, block = own.shape
    rel_lanes = rel.shape[1]
    vmem = pl.BlockSpec(memory_space=pltpu.VMEM)
    smem = pl.BlockSpec(memory_space=pltpu.SMEM)
    hbm = pl.BlockSpec(memory_space=pl.ANY)
    return pl.pallas_call(
        blocks_kernel,
        out_shape=(
            jax.ShapeDtypeStruct((16, width, block), BF16),
            jax.ShapeDtypeStruct((16, width, block), BF16),
            jax.ShapeDtypeStruct((width, block), F32),
            jax.ShapeDtypeStruct((32 * PIECE, block), BF16),
        ),
        in_specs=[smem, smem, vmem, vmem, vmem, hbm, hbm],
        out_specs=(vmem, vmem, vmem, vmem),
        scratch_shapes=[
            pltpu.VMEM((32, width, block), BF16),
            pltpu.VMEM((32, width, block), F32),
            pltpu.VMEM((width, rel_lanes), F32),
            pltpu.SemaphoreType.DMA((2,)),
        ],
        compiler_params=pltpu.CompilerParams(vmem_limit_bytes=40 * MIB),
        cost_estimate=pl.CostEstimate(flops=2 * 10**9, bytes_accessed=10**7, transcendentals=10**6),
        name="edge_blocks",
    )(lists[20], here, lists, own, rel, half, other)


def adagrad(grads, kept):
    width = grads.shape[0]
    state = kept[width : width + 1] + jnp.sum(grads * grads, 0, keepdims=True) * (1.0 / width)
    weights = kept[:width] - grads * (ENT_RATE / jnp.sqrt(state))
    return weights, state


def add_pieces(pieces):
    def add(k, total):
        return total + pieces[k].astype(F32)

    return lax.fori_loop(1, pieces.shape[0], add, pieces[0].astype(F32))


def middle_kernel(pieces, lhs, kept, kept_out, table_out):
    width = lhs.shape[0]
    weights, state = adagrad(lhs[...] + add_pieces(pieces), kept[...])
    kept_out[:width] = weights
    kept_out[width:] = jnp.broadcast_to(state, (kept.shape[0] - width, state.shape[1]))
    table_out[...] = weights.astype(BF16)


def middle(pieces, lhs, kept):
    return pl.pallas_call(
        middle_kernel,
        out_shape=(jax.ShapeDtypeStruct(kept.shape, F32), jax.ShapeDtypeStruct(lhs.shape, BF16)),
        compiler_params=pltpu.CompilerParams(vmem_limit_bytes=16 * MIB),
        name="middle_update",
    )(pieces, lhs, kept)


def fold_kernel(pieces, out):
    out[...] = add_pieces(pieces).astype(out.dtype)


def fold(pieces, kind):
    return pl.pallas_call(
        fold_kernel,
        out_shape=jax.ShapeDtypeStruct(pieces.shape[1:], kind),
        compiler_params=pltpu.CompilerParams(vmem_limit_bytes=16 * MIB),
        name="fold_pieces",
    )(pieces)


def last_kernel(rhs, lhs, kept, weights_out, state_out):
    weights, state = adagrad(rhs[...].astype(F32) + lhs[...].astype(F32), kept[...])
    weights_out[...] = weights
    state_out[...] = state


def last(rhs, lhs, kept):
    width, block = lhs.shape
    return pl.pallas_call(
        last_kernel,
        out_shape=(
            jax.ShapeDtypeStruct((width, block), F32),
            jax.ShapeDtypeStruct((1, block), F32),
        ),
        name="last_update",
    )(rhs, lhs, kept)


def z_step(total, step, kind):
    mine = total.astype(kind)
    return mine.astype(F32) + send(mine, z_pairs(step)).astype(F32)


def exchange_terms(mine, theirs, rel_part):
    swapped = send(theirs, OTHER)
    rel_pieces = exchange(rel_part.reshape(32, PIECE, -1), PLANES)
    summed, rel_pieces = together(mine + swapped, rel_pieces)
    rel_mine = fold(rel_pieces, F32)
    for step, kind in ((1, F32), (2, F32), (4, BF16)):
        rel_mine = z_step(rel_mine, step, kind)
    return exchange(summed, SHEETS), rel_mine


def spread_relations(mine):
    mine = mine.astype(BF16)
    return exchange(jnp.broadcast_to(mine, (32,) + mine.shape), PLANES)


def relation_kernel(packed, rel, rel_state, rel_out, state_out):
    width, count = rel_state.shape
    block = packed.shape[1]
    tiles = -(-count // block)
    rest = count - block * (tiles - 1)

    def update(grads, rows, lanes):
        state = rel_state[rows, lanes] + grads * grads
        state_out[rows, lanes] = state
        rel_out[rows, lanes] = rel[rows, lanes] - REL_RATE * grads / jnp.sqrt(state)

    def full(p, carry):
        for t in range(tiles - 1):
            grads = packed[pl.ds(pl.multiple_of(width * t + p * GROUP, GROUP), GROUP), :].astype(F32)
            rows = pl.ds(pl.multiple_of(p * GROUP, GROUP), GROUP)
            update(grads, rows, slice(block * t, block * (t + 1)))
        return carry

    lax.fori_loop(0, width // GROUP, full, 0)
    first = width * (tiles - 1)
    folded = packed[first : first + FOLD, :].astype(F32)
    for q in range(4):
        stop = min(FOLD * (q + 1), width)
        grads = folded if q == 0 else pltpu.roll(folded, block - q * block // 4, 1)
        lanes = slice(block * (tiles - 1), count)
        update(grads[: stop - FOLD * q, :rest], slice(FOLD * q, stop), lanes)
    if rel_out.shape[1] > count:
        rel_out[:, count:] = jnp.zeros((width, rel_out.shape[1] - count), F32)


def relation_update(pieces, rel, rel_state, lanes):
    width = rel.shape[0]
    return pl.pallas_call(
        relation_kernel,
        out_shape=(
            jax.ShapeDtypeStruct((width, lanes), F32),
            jax.ShapeDtypeStruct(rel_state.shape, F32),
        ),
        compiler_params=pltpu.CompilerParams(vmem_limit_bytes=16 * MIB),
        name="relation_update",
    )(pieces.reshape(-1, pieces.shape[2]), rel, rel_state)


def shards(
    entities,
    entity_state,
    relations,
    relation_state,
    live_blocks,
    dst_blocks,
    relation_ids,
    source_rows,
    target_rows,
    negative_blocks,
):
    block, width = entities.shape
    dom = lax.axis_index("dom")
    here = (dom % 2).astype(jnp.int32)[None]

    def lists_of(r):
        ids = relation_ids[r]
        numbers = [dst_blocks[r], ids // DIGIT, ids % DIGIT, negative_blocks[r].reshape(-1), live_blocks[r]]
        numbers = jnp.concatenate(numbers)
        numbers = jnp.pad(numbers, (0, block - numbers.shape[0]))[None]
        rows = jnp.concatenate([source_rows[r], target_rows[r], numbers])
        return jnp.pad(rows, ((0, LISTS - rows.shape[0]), (0, 0))).astype(BF16)

    weights = entities.T
    own = send(weights.astype(BF16), TURN)
    lists = send(jnp.concatenate([lists_of(0), lists_of(1)]), TURN)
    kept = send(jnp.concatenate([weights, jnp.broadcast_to(entity_state[None], (8, block))]), TURN)

    count = relations.shape[0]
    lanes = -(-count // block) * block
    rel = jnp.pad(relations.T, ((0, 0), (0, lanes - count)))
    rel_state = relation_state.T

    half, lists, kept = together(gather_sheet(own), lists, kept)
    other = send(half, OTHER)
    mine, theirs, lhs, rel_part = run_blocks(lists[:LISTS].astype(jnp.int32), here, own, rel, half, other)
    pieces, rel_mine = together(*exchange_terms(mine, theirs, rel_part))
    kept, own = middle(pieces, lhs, kept)
    source = send(jnp.concatenate([own, lists[LISTS:]]), NEXT)
    kept = send(kept, TURN)
    half, source, rel_mine = together(gather_sheet(own), source, z_step(rel_mine, 8, BF16))
    other = send(half, OTHER)
    rel, rel_state = relation_update(spread_relations(rel_mine), rel, rel_state, lanes)
    other, kept = together(other, kept)

    lists = source[width:].astype(jnp.int32)
    mine, theirs, lhs, rel_part = run_blocks(lists, here, source[:width], rel, half, other)
    pieces, rel_mine = exchange_terms(mine, theirs, rel_part)
    rel_sum = spread_relations(z_step(rel_mine, 8, BF16))
    rhs, lhs = together(fold(pieces, BF16), lhs.astype(BF16))
    weights, state = last(send(rhs, TURN), send(lhs, BACK), kept)
    rel, rel_state = relation_update(rel_sum, rel, rel_state, count)
    return (weights.T, state[0], rel.T, rel_state.T)


def solution(mesh):
    placed = (
        P(AXES, None),
        P(AXES),
        P(),
        P(),
        P(None, AXES),
        P(None, AXES),
        P(None, AXES),
        P(None, AXES, None),
        P(None, AXES, None),
        P(None, AXES, None),
    )
    return jax.shard_map(
        shards,
        mesh=mesh,
        in_specs=placed,
        out_specs=(P(AXES, None), P(AXES), P(), P()),
        check_vma=False,
    )
```

time: 2090 us -> 308 us (0.15)
  the two profiles are of different devices: /device:TPU:1 before, /device:TPU:27 now
where the time goes in v1:
time: 308 us; the launch traced here: 306 us
  starting transfers between devices  197 us (64%)
  waiting for transfers between devices  55.6 us (18%)
  local copies, waits for them, and re-layouts  19.4 us (6%)
  Pallas kernels  19.1 us (6%)
  other arithmetic  13.3 us (4%)
    ppermute x19, starting transfers between devices, send(): return lax.ppermute(value, AXES, pairs)  122 us
    all_to_all x8, starting transfers between devices, exchange(): lax.all_to_all(value, AXES, 0, 0, axis_index_groups=groups, tiled=True)  75.4 us
    ppermute x19, waiting for transfers between devices, send(): return lax.ppermute(value, AXES, pairs)  42.6 us
    all_to_all x8, waiting for transfers between devices, exchange(): lax.all_to_all(value, AXES, 0, 0, axis_index_groups=groups, tiled=True)  13.1 us
    pallas_call x2, Pallas kernels, run_blocks(): pl.pallas_call(blocks_kernel, out_shape=(jax.ShapeDtypeStruct((16, width,...  11.9 us
    unnamed x34, local copies, waits for them, and re-layouts  10.2 us
  transfers between devices with their start and end apart: 27, of which 14 were waited for; matrix products, arithmetic and copies ran while one was open for 6% of the time, Pallas kernels for 2%

profile of v1, /device:TPU:27, one launch (start us, length us, event | category | flops | bytes accessed | tf_op | source)
XLA Modules:
  0.0 305.8 jit_solution(4924351841253418881)
XLA Ops:
  0.6 0.9 bitcast_convert_fusion
  1.6 13.1 %collective-permute-start = (bf16[400,128]{1,0:T(8,128)(2,1)S(1)}, bf16[400,128]{1,0:T(8,128)(2,1)S(1)}, u32[]{:S(2)}, u32[]{:S(2)}) collective-permute-start(bf16[400,128]{1,0:T(8,128)(2,1)S(1)} %bitcast_convert_fusion), channel_id=1, source_target_pairs={{0,0},{1,1},{2,2},{3,3},{4,64},{5,65},{6,66},{7,67},{8,128},{9,129... | collective-permute-start | bytes 307208 | tf_op jit(solution)/shard_map/ppermute | solution.py:66
  15.3 0.9 pad_maximum_fusion
  16.3 1.9 collective-permute-start.2
  22.8 1.4 broadcast_in_dim.29
  24.2 6.5 %all-to-all-start = ((bf16[16,400,128]{2,1,0:T(8,128)(2,1)}), bf16[16,400,128]{2,1,0:T(8,128)(2,1)S(1)}, u32[]{:S(2)}, u32[]{:S(2)}) async-start(bf16[16,400,128]{2,1,0:T(8,128)(2,1)} %broadcast_in_dim.29), calls=%async_computation | async-start | bytes 3276800 | tf_op jit(solution)/shard_map/all_to_all | solution.py:70
  32.4 17.3 %collective-permute-start.1 = (bf16[64,128]{1,0:T(8,128)(2,1)S(1)}, bf16[64,128]{1,0:T(8,128)(2,1)S(1)}, u32[]{:S(2)}, u32[]{:S(2)}) collective-permute-start(bf16[64,128]{1,0:T(8,128)(2,1)S(1)} %pad_maximum_fusion.2), channel_id=1, source_target_pairs={{0,0},{1,1},{2,2},{3,3},{4,64},{5,65},{6,66},{7,67},{8,128},{9,129... | collective-permute-start | bytes 49160 | tf_op jit(solution)/shard_map/ppermute | solution.py:66
  49.7 1.4 collective-permute-done.1
  51.8 1.9 collective-permute-start.3
  53.7 1.4 pad.26.rel
  55.1 2.2 collective-permute-done.3.other
  57.3 6.3 %edge_blocks.2 = (bf16[16,400,128]{2,1,0:T(8,128)(2,1)S(1)}, bf16[16,400,128]{2,1,0:T(8,128)(2,1)}, f32[400,128]{1,0:T(8,128)S(1)}, bf16[2560,128]{1,0:T(8,128)(2,1)S(1)}) custom-call(s32[128]{0:T(128)S(1)} %slice_bitcast_fusion.5.scal, s32[1]{0:T(128)} %bitcast.14.here, s32[32,128]{1,0:T(8,128)S(1)} %get-tuple-element.73.lists, ...), custom_call_target="tpu_custom_call" | custom-call | flops 2000000000 | bytes 10000000 | tf_op jit(solution)/shard_map/edge_blocks/pallas_call | solution.py:182
  63.6 1.2 copy-done
  64.8 0.8 copy-done.6
  66.3 1.9 collective-permute-start.4
  68.2 14.7 %all-to-all-start.1 = ((bf16[32,80,128]{2,1,0:T(8,128)(2,1)}), bf16[32,80,128]{2,1,0:T(8,128)(2,1)S(1)}, u32[]{:S(2)}, u32[]{:S(2)}) async-start(bf16[32,80,128]{2,1,0:T(8,128)(2,1)} %bitcast.66), calls=%async_computation.1 | async-start | bytes 1310720 | tf_op jit(solution)/shard_map/all_to_all | solution.py:70
  83.0 3.1 %add.59 = bf16[16,400,128]{2,1,0:T(8,128)(2,1)} add(bf16[16,400,128]{2,1,0:T(8,128)(2,1)} %copy-done, bf16[16,400,128]{2,1,0:T(8,128)(2,1)S(1)} %collective-permute-done.4) | non-fusion elementwise | flops 819200 | bytes 4915200 | tf_op jit(solution)/shard_map/add | solution.py:274
  86.0 6.5 %all-to-all-done.1.pieces = bf16[32,80,128]{2,1,0:T(8,128)(2,1)S(1)} async-done(((bf16[32,80,128]{2,1,0:T(8,128)(2,1)}), bf16[32,80,128]{2,1,0:T(8,128)(2,1)S(1)}, u32[]{:S(2)}, u32[]{:S(2)}) %all-to-all-start.1) | async-done | bytes 655392 | tf_op jit(solution)/shard_map/all_to_all | solution.py:70
  92.5 6.4 %all-to-all-start.2 = ((bf16[16,400,128]{2,1,0:T(8,128)(2,1)}), bf16[16,400,128]{2,1,0:T(8,128)(2,1)S(1)}, u32[]{:S(2)}, u32[]{:S(2)}) async-start(bf16[16,400,128]{2,1,0:T(8,128)(2,1)} %add.59), calls=%async_computation.2 | async-start | bytes 3276800 | tf_op jit(solution)/shard_map/all_to_all | solution.py:70
  99.1 2.0 collective-permute-start.5
  101.1 3.1 %collective-permute-done.5 = f32[80,128]{1,0:T(8,128)S(1)} collective-permute-done((f32[80,128]{1,0:T(8,128)S(1)}, f32[80,128]{1,0:T(8,128)S(1)}, u32[]{:S(2)}, u32[]{:S(2)}) %collective-permute-start.5) | collective-permute-done | bytes 40992 | tf_op jit(solution)/shard_map/ppermute | solution.py:66
  104.2 1.9 collective-permute-start.6
  106.1 4.2 %collective-permute-done.6 = f32[80,128]{1,0:T(8,128)S(1)} collective-permute-done((f32[80,128]{1,0:T(8,128)S(1)}, f32[80,128]{1,0:T(8,128)S(1)}, u32[]{:S(2)}, u32[]{:S(2)}) %collective-permute-start.6) | collective-permute-done | bytes 40992 | tf_op jit(solution)/shard_map/ppermute | solution.py:66
  110.3 7.4 %collective-permute-start.7 = (bf16[80,128]{1,0:T(8,128)(2,1)S(1)}, bf16[80,128]{1,0:T(8,128)(2,1)S(1)}, u32[]{:S(2)}, u32[]{:S(2)}) collective-permute-start(bf16[80,128]{1,0:T(8,128)(2,1)S(1)} %add_convert_fusion.3), channel_id=1, source_target_pairs={{0,16},{1,17},{2,18},{3,19},{4,20},{5,21},{6,22},{7,23},{8,24},{9,... | collective-permute-start | bytes 61448 | tf_op jit(solution)/shard_map/ppermute | solution.py:66
  117.7 1.2 collective-permute-done.7
  118.9 0.9 copy-done.8
  119.8 0.9 copy-done.11
  121.3 1.4 broadcast_in_dim.34
  122.7 8.2 %all-to-all-start.3 = ((bf16[16,400,128]{2,1,0:T(8,128)(2,1)}), bf16[16,400,128]{2,1,0:T(8,128)(2,1)}, u32[]{:S(2)}, u32[]{:S(2)}) async-start(bf16[16,400,128]{2,1,0:T(8,128)(2,1)} %broadcast_in_dim.34), calls=%async_computation.3 | async-start | bytes 3276800 | tf_op jit(solution)/shard_map/all_to_all | solution.py:70
  130.9 13.7 %collective-permute-start.9 = (bf16[80,128]{1,0:T(8,128)(2,1)S(1)}, bf16[80,128]{1,0:T(8,128)(2,1)S(1)}, u32[]{:S(2)}, u32[]{:S(2)}) collective-permute-start(bf16[80,128]{1,0:T(8,128)(2,1)S(1)} %convert_add_fusion.1), channel_id=1, source_target_pairs={{0,256},{1,257},{2,258},{3,259},{4,260},{5,261},{6,262},{7,263},{8... | collective-permute-start | bytes 61448 | tf_op jit(solution)/shard_map/ppermute | solution.py:66
  144.7 1.9 collective-permute-start.8
  146.6 4.7 %collective-permute-done.8 = bf16[432,128]{1,0:T(8,128)(2,1)S(1)} collective-permute-done((bf16[432,128]{1,0:T(8,128)(2,1)S(1)}, bf16[432,128]{1,0:T(8,128)(2,1)S(1)}, u32[]{:S(2)}, u32[]{:S(2)}) %collective-permute-start.8) | collective-permute-done | bytes 110624 | tf_op jit(solution)/shard_map/ppermute | solution.py:66
  151.4 6.4 %collective-permute-start.10 = (bf16[16,400,128]{2,1,0:T(8,128)(2,1)}, bf16[16,400,128]{2,1,0:T(8,128)(2,1)}, u32[]{:S(2)}, u32[]{:S(2)}) collective-permute-start(bf16[16,400,128]{2,1,0:T(8,128)(2,1)} %all-to-all-done.3.half), channel_id=1, source_target_pairs={{0,32},{1,33},{2,34},{3,35},{4,36},{5,37},{6,38},{7,39},{8,40},{9,... | collective-permute-start | bytes 4915208 | tf_op jit(solution)/shard_map/ppermute | solution.py:66
  157.8 0.9 broadcast_in_dim.35
  158.7 7.2 %all-to-all-start.4 = ((bf16[32,80,128]{2,1,0:T(8,128)(2,1)}), bf16[32,80,128]{2,1,0:T(8,128)(2,1)S(1)}, u32[]{:S(2)}, u32[]{:S(2)}) async-start(bf16[32,80,128]{2,1,0:T(8,128)(2,1)} %broadcast_in_dim.35), calls=%async_computation.4 | async-start | bytes 1310720 | tf_op jit(solution)/shard_map/all_to_all | solution.py:70
  165.8 10.0 %collective-permute-start.11 = (f32[408,128]{1,0:T(8,128)S(1)}, f32[408,128]{1,0:T(8,128)S(1)}, u32[]{:S(2)}, u32[]{:S(2)}) collective-permute-start(f32[408,128]{1,0:T(8,128)S(1)} %get-tuple-element.52), channel_id=1, source_target_pairs={{0,0},{1,1},{2,2},{3,3},{4,64},{5,65},{6,66},{7,67},{8,128},{9,129... | collective-permute-start | bytes 626696 | tf_op jit(solution)/shard_map/ppermute | solution.py:66
  176.0 1.3 copy-done.1
  177.2 0.9 relation_update.2
  178.2 1.0 copy-done.4
  179.2 3.5 %collective-permute-done.11.kept = f32[408,128]{1,0:T(8,128)S(1)} collective-permute-done((f32[408,128]{1,0:T(8,128)S(1)}, f32[408,128]{1,0:T(8,128)S(1)}, u32[]{:S(2)}, u32[]{:S(2)}) %collective-permute-start.11) | collective-permute-done | bytes 208928 | tf_op jit(solution)/shard_map/ppermute | solution.py:66
  182.7 5.5 %edge_blocks.3 = (bf16[16,400,128]{2,1,0:T(8,128)(2,1)S(1)}, bf16[16,400,128]{2,1,0:T(8,128)(2,1)}, f32[400,128]{1,0:T(8,128)S(1)}, bf16[2560,128]{1,0:T(8,128)(2,1)}) custom-call(s32[128]{0:T(128)S(1)} %slice_bitcast_fusion.4.scal, s32[1]{0:T(128)} %bitcast.14.here, s32[32,128]{1,0:T(8,128)S(1)} %slice_convert_fusion.lists, ...), custom_call_target="tpu_custom_call" | custom-call | flops 2000000000 | bytes 10000000 | tf_op jit(solution)/shard_map/edge_blocks/pallas_call | solution.py:182
  189.0 7.6 %collective-permute-start.12 = (bf16[16,400,128]{2,1,0:T(8,128)(2,1)}, bf16[16,400,128]{2,1,0:T(8,128)(2,1)}, u32[]{:S(2)}, u32[]{:S(2)}) collective-permute-start(bf16[16,400,128]{2,1,0:T(8,128)(2,1)} %get-tuple-element.55), channel_id=1, source_target_pairs={{0,32},{1,33},{2,34},{3,35},{4,36},{5,37},{6,38},{7,39},{8,40},{9,... | collective-permute-start | bytes 4915208 | tf_op jit(solution)/shard_map/ppermute | solution.py:66
  196.6 13.4 %all-to-all-start.5 = ((bf16[32,80,128]{2,1,0:T(8,128)(2,1)}), bf16[32,80,128]{2,1,0:T(8,128)(2,1)S(1)}, u32[]{:S(2)}, u32[]{:S(2)}) async-start(bf16[32,80,128]{2,1,0:T(8,128)(2,1)} %bitcast.20), calls=%async_computation.5 | async-start | bytes 1310720 | tf_op jit(solution)/shard_map/all_to_all | solution.py:70
  210.1 3.0 add.64
  213.1 6.5 %all-to-all-done.5.pieces = bf16[32,80,128]{2,1,0:T(8,128)(2,1)S(1)} async-done(((bf16[32,80,128]{2,1,0:T(8,128)(2,1)}), bf16[32,80,128]{2,1,0:T(8,128)(2,1)S(1)}, u32[]{:S(2)}, u32[]{:S(2)}) %all-to-all-start.5) | async-done | bytes 655392 | tf_op jit(solution)/shard_map/all_to_all | solution.py:70
  219.7 6.4 %all-to-all-start.6 = ((bf16[16,400,128]{2,1,0:T(8,128)(2,1)}), bf16[16,400,128]{2,1,0:T(8,128)(2,1)S(1)}, u32[]{:S(2)}, u32[]{:S(2)}) async-start(bf16[16,400,128]{2,1,0:T(8,128)(2,1)} %add.64), calls=%async_computation.6 | async-start | bytes 3276800 | tf_op jit(solution)/shard_map/all_to_all | solution.py:70
  226.2 1.9 collective-permute-start.15
  228.2 3.1 %collective-permute-done.15 = f32[80,128]{1,0:T(8,128)S(1)} collective-permute-done((f32[80,128]{1,0:T(8,128)S(1)}, f32[80,128]{1,0:T(8,128)S(1)}, u32[]{:S(2)}, u32[]{:S(2)}) %collective-permute-start.15) | collective-permute-done | bytes 40992 | tf_op jit(solution)/shard_map/ppermute | solution.py:66
  231.3 1.9 collective-permute-start.16
  233.2 4.2 %collective-permute-done.16 = f32[80,128]{1,0:T(8,128)S(1)} collective-permute-done((f32[80,128]{1,0:T(8,128)S(1)}, f32[80,128]{1,0:T(8,128)S(1)}, u32[]{:S(2)}, u32[]{:S(2)}) %collective-permute-start.16) | collective-permute-done | bytes 40992 | tf_op jit(solution)/shard_map/ppermute | solution.py:66
  237.4 7.4 %collective-permute-start.17 = (bf16[80,128]{1,0:T(8,128)(2,1)S(1)}, bf16[80,128]{1,0:T(8,128)(2,1)S(1)}, u32[]{:S(2)}, u32[]{:S(2)}) collective-permute-start(bf16[80,128]{1,0:T(8,128)(2,1)S(1)} %add_convert_fusion.2), channel_id=1, source_target_pairs={{0,16},{1,17},{2,18},{3,19},{4,20},{5,21},{6,22},{7,23},{8,24},{9,... | collective-permute-start | bytes 61448 | tf_op jit(solution)/shard_map/ppermute | solution.py:66
  244.8 1.2 collective-permute-done.17
  246.0 10.8 %collective-permute-start.18 = (bf16[80,128]{1,0:T(8,128)(2,1)S(1)}, bf16[80,128]{1,0:T(8,128)(2,1)S(1)}, u32[]{:S(2)}, u32[]{:S(2)}) collective-permute-start(bf16[80,128]{1,0:T(8,128)(2,1)S(1)} %add_convert_fusion.1), channel_id=1, source_target_pairs={{0,256},{1,257},{2,258},{3,259},{4,260},{5,261},{6,262},{7,263},{8... | collective-permute-start | bytes 61448 | tf_op jit(solution)/shard_map/ppermute | solution.py:66
  256.8 2.4 collective-permute-done.18
  259.2 1.0 broadcast_in_dim.36
  260.2 12.6 %all-to-all-start.7 = ((bf16[32,80,128]{2,1,0:T(8,128)(2,1)}), bf16[32,80,128]{2,1,0:T(8,128)(2,1)S(1)}, u32[]{:S(2)}, u32[]{:S(2)}) async-start(bf16[32,80,128]{2,1,0:T(8,128)(2,1)} %broadcast_in_dim.36), calls=%async_computation.7 | async-start | bytes 1310720 | tf_op jit(solution)/shard_map/all_to_all | solution.py:70
  272.8 1.6 convert_element_type.68
  274.4 1.1 fold_pieces.4
  275.6 10.7 %collective-permute-start.13 = (bf16[400,128]{1,0:T(8,128)(2,1)}, bf16[400,128]{1,0:T(8,128)(2,1)S(1)}, u32[]{:S(2)}, u32[]{:S(2)}) collective-permute-start(bf16[400,128]{1,0:T(8,128)(2,1)} %fold_pieces.4), channel_id=1, source_target_pairs={{0,0},{1,1},{2,2},{3,3},{4,64},{5,65},{6,66},{7,67},{8,128},{9,129... | collective-permute-start | bytes 307208 | tf_op jit(solution)/shard_map/ppermute | solution.py:66
  286.3 1.9 collective-permute-start.14
  288.2 1.3 copy-done.5
  289.5 2.4 relation_update.3
  291.9 11.4 %collective-permute-done.14.lhs = bf16[400,128]{1,0:T(8,128)(2,1)S(1)} collective-permute-done((bf16[400,128]{1,0:T(8,128)(2,1)}, bf16[400,128]{1,0:T(8,128)(2,1)S(1)}, u32[]{:S(2)}, u32[]{:S(2)}) %collective-permute-start.14) | collective-permute-done | bytes 102432 | tf_op jit(solution)/shard_map/ppermute | solution.py:66
  303.9 1.8 last_update.1
  (80 shorter events, 10.6 us)
Async XLA Ops:
  1.6 21.2 %collective-permute-start = (bf16[400,128]{1,0:T(8,128)(2,1)S(1)}, bf16[400,128]{1,0:T(8,128)(2,1)S(1)}, u32[]{:S(2)}, u32[]{:S(2)}) collective-permute-start(bf16[400,128]{1,0:T(8,128)(2,1)S(1)} %bitcast_convert_fusion), channel_id=1, source_target_pairs={{0,0},{1,1},{2,2},{3,3},{4,64},{5,65},{6,66},{7,67},{8,128},{9,129... | collective-permute-start | bytes 307208 | tf_op jit(solution)/shard_map/ppermute | solution.py:66
  16.3 34.8 %collective-permute-start.2 = (f32[408,128]{1,0:T(8,128)S(1)}, f32[408,128]{1,0:T(8,128)S(1)}, u32[]{:S(2)}, u32[]{:S(2)}) collective-permute-start(f32[408,128]{1,0:T(8,128)S(1)} %pad_maximum_fusion), channel_id=1, source_target_pairs={{0,0},{1,1},{2,2},{3,3},{4,64},{5,65},{6,66},{7,67},{8,128},{9,129... | collective-permute-start | bytes 626696 | tf_op jit(solution)/shard_map/ppermute | solution.py:66
  24.2 8.1 %copy-start.15 = (s32[2,10,128]{2,0,1:T(2,128)S(1)}, s32[2,10,128]{2,0,1:T(2,128)}, u32[]{:S(2)}) copy-start(s32[2,10,128]{2,0,1:T(2,128)} %param.17) | copy-start | bytes 30724
  24.2 8.1 %copy-start.16 = (s32[2,10,128]{2,0,1:T(2,128)S(1)}, s32[2,10,128]{2,0,1:T(2,128)}, u32[]{:S(2)}) copy-start(s32[2,10,128]{2,0,1:T(2,128)} %param.18) | copy-start | bytes 30724
  24.2 27.5 %all-to-all-start = ((bf16[16,400,128]{2,1,0:T(8,128)(2,1)}), bf16[16,400,128]{2,1,0:T(8,128)(2,1)S(1)}, u32[]{:S(2)}, u32[]{:S(2)}) async-start(bf16[16,400,128]{2,1,0:T(8,128)(2,1)} %broadcast_in_dim.29), calls=%async_computation | async-start | bytes 3276800 | tf_op jit(solution)/shard_map/all_to_all | solution.py:70
  32.4 18.7 %collective-permute-start.1 = (bf16[64,128]{1,0:T(8,128)(2,1)S(1)}, bf16[64,128]{1,0:T(8,128)(2,1)S(1)}, u32[]{:S(2)}, u32[]{:S(2)}) collective-permute-start(bf16[64,128]{1,0:T(8,128)(2,1)S(1)} %pad_maximum_fusion.2), channel_id=1, source_target_pairs={{0,0},{1,1},{2,2},{3,3},{4,64},{5,65},{6,66},{7,67},{8,128},{9,129... | collective-permute-start | bytes 49160 | tf_op jit(solution)/shard_map/ppermute | solution.py:66
  51.1 0.7 copy-start.7
  51.8 5.5 %collective-permute-start.3 = (bf16[16,400,128]{2,1,0:T(8,128)(2,1)S(1)}, bf16[16,400,128]{2,1,0:T(8,128)(2,1)}, u32[]{:S(2)}, u32[]{:S(2)}) collective-permute-start(bf16[16,400,128]{2,1,0:T(8,128)(2,1)S(1)} %all-to-all-done.half), channel_id=1, source_target_pairs={{0,32},{1,33},{2,34},{3,35},{4,36},{5,37},{6,38},{7,39},{8,40},{9,... | collective-permute-start | bytes 4915208 | tf_op jit(solution)/shard_map/ppermute | solution.py:66
  63.6 1.2 copy-start
  64.8 0.8 copy-start.6
  65.7 0.7 copy-start.10
  66.3 16.6 %collective-permute-start.4 = (bf16[16,400,128]{2,1,0:T(8,128)(2,1)}, bf16[16,400,128]{2,1,0:T(8,128)(2,1)S(1)}, u32[]{:S(2)}, u32[]{:S(2)}) collective-permute-start(bf16[16,400,128]{2,1,0:T(8,128)(2,1)} %get-tuple-element.39), channel_id=1, source_target_pairs={{0,32},{1,33},{2,34},{3,35},{4,36},{5,37},{6,38},{7,39},{8,40},{9,... | collective-permute-start | bytes 4915208 | tf_op jit(solution)/shard_map/ppermute | solution.py:66
  68.2 24.3 %all-to-all-start.1 = ((bf16[32,80,128]{2,1,0:T(8,128)(2,1)}), bf16[32,80,128]{2,1,0:T(8,128)(2,1)S(1)}, u32[]{:S(2)}, u32[]{:S(2)}) async-start(bf16[32,80,128]{2,1,0:T(8,128)(2,1)} %bitcast.66), calls=%async_computation.1 | async-start | bytes 1310720 | tf_op jit(solution)/shard_map/all_to_all | solution.py:70
  92.5 26.3 %all-to-all-start.2 = ((bf16[16,400,128]{2,1,0:T(8,128)(2,1)}), bf16[16,400,128]{2,1,0:T(8,128)(2,1)S(1)}, u32[]{:S(2)}, u32[]{:S(2)}) async-start(bf16[16,400,128]{2,1,0:T(8,128)(2,1)} %add.59), calls=%async_computation.2 | async-start | bytes 3276800 | tf_op jit(solution)/shard_map/all_to_all | solution.py:70
  99.1 5.0 %collective-permute-start.5 = (f32[80,128]{1,0:T(8,128)S(1)}, f32[80,128]{1,0:T(8,128)S(1)}, u32[]{:S(2)}, u32[]{:S(2)}) collective-permute-start(f32[80,128]{1,0:T(8,128)S(1)} %fold_pieces.3), channel_id=1, source_target_pairs={{0,4},{1,5},{2,6},{3,7},{4,0},{5,1},{6,2},{7,3},{8,12},{9,13},{10,... | collective-permute-start | bytes 122888 | tf_op jit(solution)/shard_map/ppermute | solution.py:66
  104.2 6.1 %collective-permute-start.6 = (f32[80,128]{1,0:T(8,128)S(1)}, f32[80,128]{1,0:T(8,128)S(1)}, u32[]{:S(2)}, u32[]{:S(2)}) collective-permute-start(f32[80,128]{1,0:T(8,128)S(1)} %add.60), channel_id=1, source_target_pairs={{0,8},{1,9},{2,10},{3,11},{4,12},{5,13},{6,14},{7,15},{8,0},{9,1},... | collective-permute-start | bytes 122888 | tf_op jit(solution)/shard_map/ppermute | solution.py:66
  110.3 8.5 %collective-permute-start.7 = (bf16[80,128]{1,0:T(8,128)(2,1)S(1)}, bf16[80,128]{1,0:T(8,128)(2,1)S(1)}, u32[]{:S(2)}, u32[]{:S(2)}) collective-permute-start(bf16[80,128]{1,0:T(8,128)(2,1)S(1)} %add_convert_fusion.3), channel_id=1, source_target_pairs={{0,16},{1,17},{2,18},{3,19},{4,20},{5,21},{6,22},{7,23},{8,24},{9,... | collective-permute-start | bytes 61448 | tf_op jit(solution)/shard_map/ppermute | solution.py:66
  118.9 0.9 copy-start.8
  119.8 0.9 copy-start.11
  122.7 28.6 %all-to-all-start.3 = ((bf16[16,400,128]{2,1,0:T(8,128)(2,1)}), bf16[16,400,128]{2,1,0:T(8,128)(2,1)}, u32[]{:S(2)}, u32[]{:S(2)}) async-start(bf16[16,400,128]{2,1,0:T(8,128)(2,1)} %broadcast_in_dim.34), calls=%async_computation.3 | async-start | bytes 3276800 | tf_op jit(solution)/shard_map/all_to_all | solution.py:70
  130.9 15.7 %collective-permute-start.9 = (bf16[80,128]{1,0:T(8,128)(2,1)S(1)}, bf16[80,128]{1,0:T(8,128)(2,1)S(1)}, u32[]{:S(2)}, u32[]{:S(2)}) collective-permute-start(bf16[80,128]{1,0:T(8,128)(2,1)S(1)} %convert_add_fusion.1), channel_id=1, source_target_pairs={{0,256},{1,257},{2,258},{3,259},{4,260},{5,261},{6,262},{7,263},{8... | collective-permute-start | bytes 61448 | tf_op jit(solution)/shard_map/ppermute | solution.py:66
  144.7 6.7 %collective-permute-start.8 = (bf16[432,128]{1,0:T(8,128)(2,1)S(1)}, bf16[432,128]{1,0:T(8,128)(2,1)S(1)}, u32[]{:S(2)}, u32[]{:S(2)}) collective-permute-start(bf16[432,128]{1,0:T(8,128)(2,1)S(1)} %pad_maximum_fusion.1), channel_id=1, source_target_pairs={{0,16},{1,17},{2,18},{3,19},{64,80},{65,81},{66,82},{67,83},{128,1... | collective-permute-start | bytes 331784 | tf_op jit(solution)/shard_map/ppermute | solution.py:66
  151.4 31.3 %collective-permute-start.10 = (bf16[16,400,128]{2,1,0:T(8,128)(2,1)}, bf16[16,400,128]{2,1,0:T(8,128)(2,1)}, u32[]{:S(2)}, u32[]{:S(2)}) collective-permute-start(bf16[16,400,128]{2,1,0:T(8,128)(2,1)} %all-to-all-done.3.half), channel_id=1, source_target_pairs={{0,32},{1,33},{2,34},{3,35},{4,36},{5,37},{6,38},{7,39},{8,40},{9,... | collective-permute-start | bytes 4915208 | tf_op jit(solution)/shard_map/ppermute | solution.py:66
  158.7 17.3 %all-to-all-start.4 = ((bf16[32,80,128]{2,1,0:T(8,128)(2,1)}), bf16[32,80,128]{2,1,0:T(8,128)(2,1)S(1)}, u32[]{:S(2)}, u32[]{:S(2)}) async-start(bf16[32,80,128]{2,1,0:T(8,128)(2,1)} %broadcast_in_dim.35), calls=%async_computation.4 | async-start | bytes 1310720 | tf_op jit(solution)/shard_map/all_to_all | solution.py:70
  165.8 16.9 %collective-permute-start.11 = (f32[408,128]{1,0:T(8,128)S(1)}, f32[408,128]{1,0:T(8,128)S(1)}, u32[]{:S(2)}, u32[]{:S(2)}) collective-permute-start(f32[408,128]{1,0:T(8,128)S(1)} %get-tuple-element.52), channel_id=1, source_target_pairs={{0,0},{1,1},{2,2},{3,3},{4,64},{5,65},{6,66},{7,67},{8,128},{9,129... | collective-permute-start | bytes 626696 | tf_op jit(solution)/shard_map/ppermute | solution.py:66
  175.9 1.3 copy-start.1
  178.2 1.0 copy-start.4
  179.2 9.0 %copy-start.2 = (f32[400,768]{1,0:T(8,128)}, f32[400,768]{1,0:T(8,128)S(1)}, u32[]{:S(2)}) copy-start(f32[400,768]{1,0:T(8,128)S(1)} %get-tuple-element.50.rel) | copy-start | bytes 3686404
  182.7 5.6 %copy-start.12 = (f32[408,128]{1,0:T(8,128)}, f32[408,128]{1,0:T(8,128)S(1)}, u32[]{:S(2)}) copy-start(f32[408,128]{1,0:T(8,128)S(1)} %collective-permute-done.11.kept) | copy-start | bytes 626692
  188.3 0.7 copy-start.9
  189.0 21.1 %collective-permute-start.12 = (bf16[16,400,128]{2,1,0:T(8,128)(2,1)}, bf16[16,400,128]{2,1,0:T(8,128)(2,1)}, u32[]{:S(2)}, u32[]{:S(2)}) collective-permute-start(bf16[16,400,128]{2,1,0:T(8,128)(2,1)} %get-tuple-element.55), channel_id=1, source_target_pairs={{0,32},{1,33},{2,34},{3,35},{4,36},{5,37},{6,38},{7,39},{8,40},{9,... | collective-permute-start | bytes 4915208 | tf_op jit(solution)/shard_map/ppermute | solution.py:66
  196.6 23.0 %all-to-all-start.5 = ((bf16[32,80,128]{2,1,0:T(8,128)(2,1)}), bf16[32,80,128]{2,1,0:T(8,128)(2,1)S(1)}, u32[]{:S(2)}, u32[]{:S(2)}) async-start(bf16[32,80,128]{2,1,0:T(8,128)(2,1)} %bitcast.20), calls=%async_computation.5 | async-start | bytes 1310720 | tf_op jit(solution)/shard_map/all_to_all | solution.py:70
  219.7 39.6 %all-to-all-start.6 = ((bf16[16,400,128]{2,1,0:T(8,128)(2,1)}), bf16[16,400,128]{2,1,0:T(8,128)(2,1)S(1)}, u32[]{:S(2)}, u32[]{:S(2)}) async-start(bf16[16,400,128]{2,1,0:T(8,128)(2,1)} %add.64), calls=%async_computation.6 | async-start | bytes 3276800 | tf_op jit(solution)/shard_map/all_to_all | solution.py:70
  226.2 5.0 %collective-permute-start.15 = (f32[80,128]{1,0:T(8,128)S(1)}, f32[80,128]{1,0:T(8,128)S(1)}, u32[]{:S(2)}, u32[]{:S(2)}) collective-permute-start(f32[80,128]{1,0:T(8,128)S(1)} %fold_pieces.5), channel_id=1, source_target_pairs={{0,4},{1,5},{2,6},{3,7},{4,0},{5,1},{6,2},{7,3},{8,12},{9,13},{10,... | collective-permute-start | bytes 122888 | tf_op jit(solution)/shard_map/ppermute | solution.py:66
  231.3 6.1 %collective-permute-start.16 = (f32[80,128]{1,0:T(8,128)S(1)}, f32[80,128]{1,0:T(8,128)S(1)}, u32[]{:S(2)}, u32[]{:S(2)}) collective-permute-start(f32[80,128]{1,0:T(8,128)S(1)} %add.65), channel_id=1, source_target_pairs={{0,8},{1,9},{2,10},{3,11},{4,12},{5,13},{6,14},{7,15},{8,0},{9,1},... | collective-permute-start | bytes 122888 | tf_op jit(solution)/shard_map/ppermute | solution.py:66
  237.4 8.6 %collective-permute-start.17 = (bf16[80,128]{1,0:T(8,128)(2,1)S(1)}, bf16[80,128]{1,0:T(8,128)(2,1)S(1)}, u32[]{:S(2)}, u32[]{:S(2)}) collective-permute-start(bf16[80,128]{1,0:T(8,128)(2,1)S(1)} %add_convert_fusion.2), channel_id=1, source_target_pairs={{0,16},{1,17},{2,18},{3,19},{4,20},{5,21},{6,22},{7,23},{8,24},{9,... | collective-permute-start | bytes 61448 | tf_op jit(solution)/shard_map/ppermute | solution.py:66
  246.0 13.2 %collective-permute-start.18 = (bf16[80,128]{1,0:T(8,128)(2,1)S(1)}, bf16[80,128]{1,0:T(8,128)(2,1)S(1)}, u32[]{:S(2)}, u32[]{:S(2)}) collective-permute-start(bf16[80,128]{1,0:T(8,128)(2,1)S(1)} %add_convert_fusion.1), channel_id=1, source_target_pairs={{0,256},{1,257},{2,258},{3,259},{4,260},{5,261},{6,262},{7,263},{8... | collective-permute-start | bytes 61448 | tf_op jit(solution)/shard_map/ppermute | solution.py:66
  260.2 28.0 %copy-start.3 = (f32[400,768]{1,0:T(8,128)S(1)}, f32[400,768]{1,0:T(8,128)}, u32[]{:S(2)}) copy-start(f32[400,768]{1,0:T(8,128)} %copy-done.2) | copy-start | bytes 3686404
  260.2 28.0 %all-to-all-start.7 = ((bf16[32,80,128]{2,1,0:T(8,128)(2,1)}), bf16[32,80,128]{2,1,0:T(8,128)(2,1)S(1)}, u32[]{:S(2)}, u32[]{:S(2)}) async-start(bf16[32,80,128]{2,1,0:T(8,128)(2,1)} %broadcast_in_dim.36), calls=%async_computation.7 | async-start | bytes 1310720 | tf_op jit(solution)/shard_map/all_to_all | solution.py:70
  275.6 16.3 %collective-permute-start.13 = (bf16[400,128]{1,0:T(8,128)(2,1)}, bf16[400,128]{1,0:T(8,128)(2,1)S(1)}, u32[]{:S(2)}, u32[]{:S(2)}) collective-permute-start(bf16[400,128]{1,0:T(8,128)(2,1)} %fold_pieces.4), channel_id=1, source_target_pairs={{0,0},{1,1},{2,2},{3,3},{4,64},{5,65},{6,66},{7,67},{8,128},{9,129... | collective-permute-start | bytes 307208 | tf_op jit(solution)/shard_map/ppermute | solution.py:66
  286.3 17.0 %collective-permute-start.14 = (bf16[400,128]{1,0:T(8,128)(2,1)}, bf16[400,128]{1,0:T(8,128)(2,1)S(1)}, u32[]{:S(2)}, u32[]{:S(2)}) collective-permute-start(bf16[400,128]{1,0:T(8,128)(2,1)} %convert_element_type.68), channel_id=1, source_target_pairs={{16,0},{17,1},{18,2},{19,3},{80,4},{81,5},{82,6},{83,7},{144,8},{1... | collective-permute-start | bytes 307208 | tf_op jit(solution)/shard_map/ppermute | solution.py:66
  288.2 1.3 copy-start.5
  291.9 11.4 %copy-start.13 = (bf16[400,128]{1,0:T(8,128)(2,1)}, bf16[400,128]{1,0:T(8,128)(2,1)S(1)}, u32[]{:S(2)}) copy-start(bf16[400,128]{1,0:T(8,128)(2,1)S(1)} %collective-permute-done.13.rhs) | copy-start | bytes 307204
  303.3 0.6 copy-start.14

commit v2 on v1

--- a/solution.py
+++ b/solution.py
@@ -1,3 +1,5 @@
+import functools
+
 import jax
 import jax.numpy as jnp
 from jax import lax
@@ -87,7 +89,7 @@
 
 
 def blocks_kernel(
-    scal, here, lists, own, rel, half, other, mine_out, theirs_out, lhs_out, rel_out, table, acc, rel_acc, sems
+    joint, scal, here, lists, own, rel, half, other, mine_out, theirs_out, lhs_out, rel_out, table, acc, rel_acc, sems
 ):
     slots = 10
     width, block = own.shape
@@ -152,12 +154,6 @@
 
     lax.fori_loop(0, scal[7 * slots], step, 0)
 
-    def pack(k, carry):
-        mine_out[k] = acc[k].astype(BF16)
-        theirs_out[k] = acc[16 + k].astype(BF16)
-        return carry
-
-    lax.fori_loop(0, 16, pack, 0)
     tiles = rel_acc.shape[1] // block
     for t in range(tiles - 1):
         rel_out[width * t : width * (t + 1)] = rel_acc[:, block * t : block * (t + 1)].astype(BF16)
@@ -172,29 +168,46 @@
     rel_out[first : first + FOLD] = folded.astype(BF16)
     rel_out[first + FOLD :] = jnp.zeros((rel_out.shape[0] - first - FOLD, block), BF16)
 
-
-def run_blocks(lists, here, own, rel, half, other):
+    def pack(k, carry):
+        for side, out in enumerate((mine_out, theirs_out)):
+            out[k, :width] = acc[16 * side + k].astype(BF16)
+            if joint:
+                piece = ((here[0] ^ side) * 16 + k) * PIECE
+                out[k, width:] = rel_out[pl.ds(pl.multiple_of(piece, 16), PIECE), :]
+        return carry
+
+    lax.fori_loop(0, 16, pack, 0)
+
+
+def run_blocks(lists, here, own, rel, half, other, joint):
     width, block = own.shape
     rel_lanes = rel.shape[1]
+    rows = width + PIECE if joint else width
     vmem = pl.BlockSpec(memory_space=pltpu.VMEM)
     smem = pl.BlockSpec(memory_space=pltpu.SMEM)
     hbm = pl.BlockSpec(memory_space=pl.ANY)
+    out_shape = [
+        jax.ShapeDtypeStruct((16, rows, block), BF16),
+        jax.ShapeDtypeStruct((16, rows, block), BF16),
+        jax.ShapeDtypeStruct((width, block), F32),
+    ]
+    packed = (32 * PIECE, block)
+    scratch = [
+        pltpu.VMEM((32, width, block), BF16),
+        pltpu.VMEM((32, width, block), F32),
+        pltpu.VMEM((width, rel_lanes), F32),
+        pltpu.SemaphoreType.DMA((2,)),
+    ]
+    if joint:
+        scratch = [pltpu.VMEM(packed, BF16)] + scratch
+    else:
+        out_shape = out_shape + [jax.ShapeDtypeStruct(packed, BF16)]
     return pl.pallas_call(
-        blocks_kernel,
-        out_shape=(
-            jax.ShapeDtypeStruct((16, width, block), BF16),
-            jax.ShapeDtypeStruct((16, width, block), BF16),
-            jax.ShapeDtypeStruct((width, block), F32),
-            jax.ShapeDtypeStruct((32 * PIECE, block), BF16),
-        ),
+        functools.partial(blocks_kernel, joint),
+        out_shape=out_shape,
         in_specs=[smem, smem, vmem, vmem, vmem, hbm, hbm],
-        out_specs=(vmem, vmem, vmem, vmem),
-        scratch_shapes=[
-            pltpu.VMEM((32, width, block), BF16),
-            pltpu.VMEM((32, width, block), F32),
-            pltpu.VMEM((width, rel_lanes), F32),
-            pltpu.SemaphoreType.DMA((2,)),
-        ],
+        out_specs=[vmem] * len(out_shape),
+        scratch_shapes=scratch,
         compiler_params=pltpu.CompilerParams(vmem_limit_bytes=40 * MIB),
         cost_estimate=pl.CostEstimate(flops=2 * 10**9, bytes_accessed=10**7, transcendentals=10**6),
         name="edge_blocks",
@@ -215,18 +228,24 @@
     return lax.fori_loop(1, pieces.shape[0], add, pieces[0].astype(F32))
 
 
-def middle_kernel(pieces, lhs, kept, kept_out, table_out):
+def middle_kernel(pieces, lhs, kept, kept_out, table_out, rel_out):
     width = lhs.shape[0]
-    weights, state = adagrad(lhs[...] + add_pieces(pieces), kept[...])
+    total = add_pieces(pieces)
+    weights, state = adagrad(lhs[...] + total[:width], kept[...])
     kept_out[:width] = weights
     kept_out[width:] = jnp.broadcast_to(state, (kept.shape[0] - width, state.shape[1]))
     table_out[...] = weights.astype(BF16)
+    rel_out[...] = total[width:]
 
 
 def middle(pieces, lhs, kept):
     return pl.pallas_call(
         middle_kernel,
-        out_shape=(jax.ShapeDtypeStruct(kept.shape, F32), jax.ShapeDtypeStruct(lhs.shape, BF16)),
+        out_shape=(
+            jax.ShapeDtypeStruct(kept.shape, F32),
+            jax.ShapeDtypeStruct(lhs.shape, BF16),
+            jax.ShapeDtypeStruct((PIECE, lhs.shape[1]), F32),
+        ),
         compiler_params=pltpu.CompilerParams(vmem_limit_bytes=16 * MIB),
         name="middle_update",
     )(pieces, lhs, kept)
@@ -268,14 +287,10 @@
     return mine.astype(F32) + send(mine, z_pairs(step)).astype(F32)
 
 
-def exchange_terms(mine, theirs, rel_part):
-    swapped = send(theirs, OTHER)
-    rel_pieces = exchange(rel_part.reshape(32, PIECE, -1), PLANES)
-    summed, rel_pieces = together(mine + swapped, rel_pieces)
-    rel_mine = fold(rel_pieces, F32)
+def z_steps(total):
     for step, kind in ((1, F32), (2, F32), (4, BF16)):
-        rel_mine = z_step(rel_mine, step, kind)
-    return exchange(summed, SHEETS), rel_mine
+        total = z_step(total, step, kind)
+    return total
 
 
 def spread_relations(mine):
@@ -352,6 +367,9 @@
 
     weights = entities.T
     own = send(weights.astype(BF16), TURN)
+    own, weights, source_rows, target_rows, dst_blocks = together(
+        own, weights, source_rows, target_rows, dst_blocks
+    )
     lists = send(jnp.concatenate([lists_of(0), lists_of(1)]), TURN)
     kept = send(jnp.concatenate([weights, jnp.broadcast_to(entity_state[None], (8, block))]), TURN)
 
@@ -362,22 +380,28 @@
 
     half, lists, kept = together(gather_sheet(own), lists, kept)
     other = send(half, OTHER)
-    mine, theirs, lhs, rel_part = run_blocks(lists[:LISTS].astype(jnp.int32), here, own, rel, half, other)
-    pieces, rel_mine = together(*exchange_terms(mine, theirs, rel_part))
-    kept, own = middle(pieces, lhs, kept)
+    now = lists[:LISTS].astype(jnp.int32)
+    mine, theirs, lhs = run_blocks(now, here, own, rel, half, other, True)
+    pieces = exchange(mine + send(theirs, OTHER), SHEETS)
+    kept, own, rel_mine = middle(pieces, lhs, kept)
     source = send(jnp.concatenate([own, lists[LISTS:]]), NEXT)
     kept = send(kept, TURN)
-    half, source, rel_mine = together(gather_sheet(own), source, z_step(rel_mine, 8, BF16))
+    half, source, rel_mine = together(gather_sheet(own), source, z_steps(rel_mine))
     other = send(half, OTHER)
-    rel, rel_state = relation_update(spread_relations(rel_mine), rel, rel_state, lanes)
+    rel_sum = spread_relations(z_step(rel_mine, 8, BF16))
+    rel, rel_state = relation_update(rel_sum, rel, rel_state, lanes)
     other, kept = together(other, kept)
 
-    lists = source[width:].astype(jnp.int32)
-    mine, theirs, lhs, rel_part = run_blocks(lists, here, source[:width], rel, half, other)
-    pieces, rel_mine = exchange_terms(mine, theirs, rel_part)
+    now = source[width:].astype(jnp.int32)
+    mine, theirs, lhs, rel_part = run_blocks(now, here, source[:width], rel, half, other, False)
+    summed, lhs = together(mine + send(theirs, OTHER), lhs.astype(BF16))
+    lhs = send(lhs, BACK)
+    rel_pieces = exchange(rel_part.reshape(32, PIECE, block), PLANES)
+    summed, rel_pieces, lhs = together(summed, rel_pieces, lhs)
+    rel_mine = z_steps(fold(rel_pieces, F32))
+    rhs = send(fold(exchange(summed, SHEETS), BF16), TURN)
     rel_sum = spread_relations(z_step(rel_mine, 8, BF16))
-    rhs, lhs = together(fold(pieces, BF16), lhs.astype(BF16))
-    weights, state = last(send(rhs, TURN), send(lhs, BACK), kept)
+    weights, state = last(rhs, lhs, kept)
     rel, rel_state = relation_update(rel_sum, rel, rel_state, count)
     return (weights.T, state[0], rel.T, rel_state.T)
 

time: 308 us -> 312 us (1.013)
  the two profiles are of different devices: /device:TPU:27 before, /device:TPU:1 now
where the time goes in v2:
time: 312 us; the launch traced here: 310 us
  starting transfers between devices  165 us (53%)
  waiting for transfers between devices  58.9 us (19%)
  blocking collectives  43.2 us (14%)
  Pallas kernels  16.3 us (5%)
  local copies, waits for them, and re-layouts  15.8 us (5%)
  other arithmetic  9.97 us (3%)
    ppermute x19, starting transfers between devices, send(): return lax.ppermute(value, AXES, pairs)  106 us
    all_to_all x6, starting transfers between devices, exchange(): lax.all_to_all(value, AXES, 0, 0, axis_index_groups=groups, tiled=True)  58.9 us
    ppermute x19, waiting for transfers between devices, send(): return lax.ppermute(value, AXES, pairs)  44.7 us
    all_to_all x1, blocking collectives, exchange(): lax.all_to_all(value, AXES, 0, 0, axis_index_groups=groups, tiled=True)  43.2 us
    all_to_all x6, waiting for transfers between devices, exchange(): lax.all_to_all(value, AXES, 0, 0, axis_index_groups=groups, tiled=True)  14.2 us
    pallas_call x2, Pallas kernels, run_blocks(): pl.pallas_call(functools.partial(blocks_kernel, joint), out_shape=out_sha...  9.1 us
  transfers between devices with their start and end apart: 25, of which 15 were waited for; matrix products, arithmetic and copies ran while one was open for 5% of the time, Pallas kernels for 1%

profile of v2, /device:TPU:1, one launch (start us, length us, event | category | flops | bytes accessed | tf_op | source)
XLA Modules:
  0.0 309.9 jit_solution(17356017597693866192)
XLA Ops:
  0.6 0.9 bitcast_convert_fusion
  1.6 10.2 %collective-permute-start = (bf16[400,128]{1,0:T(8,128)(2,1)S(1)}, bf16[400,128]{1,0:T(8,128)(2,1)S(1)}, u32[]{:S(2)}, u32[]{:S(2)}) collective-permute-start(bf16[400,128]{1,0:T(8,128)(2,1)S(1)} %bitcast_convert_fusion), channel_id=1, source_target_pairs={{0,0},{1,1},{2,2},{3,3},{4,64},{5,65},{6,66},{7,67},{8,128},{9,129... | collective-permute-start | bytes 307208 | tf_op jit(solution)/shard_map/ppermute | solution.py:68
  13.2 0.8 fusion.10
  14.3 0.8 fusion.12
  16.4 1.4 broadcast_in_dim.29
  17.8 10.4 %all-to-all-start = ((bf16[16,400,128]{2,1,0:T(8,128)(2,1)}), bf16[16,400,128]{2,1,0:T(8,128)(2,1)S(1)}, u32[]{:S(2)}, u32[]{:S(2)}) async-start(bf16[16,400,128]{2,1,0:T(8,128)(2,1)} %broadcast_in_dim.29), calls=%async_computation | async-start | bytes 3276800 | tf_op jit(solution)/shard_map/all_to_all | solution.py:72
  28.3 5.9 %collective-permute-start.2 = (f32[408,128]{1,0:T(8,128)S(1)}, f32[408,128]{1,0:T(8,128)S(1)}, u32[]{:S(2)}, u32[]{:S(2)}) collective-permute-start(f32[408,128]{1,0:T(8,128)S(1)} %pad_maximum_fusion), channel_id=1, source_target_pairs={{0,0},{1,1},{2,2},{3,3},{4,64},{5,65},{6,66},{7,67},{8,128},{9,129... | collective-permute-start | bytes 626696 | tf_op jit(solution)/shard_map/ppermute | solution.py:68
  34.2 0.7 concatenate.27
  35.0 0.7 concatenate.25
  35.9 3.5 %collective-permute-start.1 = (bf16[64,128]{1,0:T(8,128)(2,1)S(1)}, bf16[64,128]{1,0:T(8,128)(2,1)S(1)}, u32[]{:S(2)}, u32[]{:S(2)}) collective-permute-start(bf16[64,128]{1,0:T(8,128)(2,1)S(1)} %pad_maximum_fusion.2), channel_id=1, source_target_pairs={{0,0},{1,1},{2,2},{3,3},{4,64},{5,65},{6,66},{7,67},{8,128},{9,129... | collective-permute-start | bytes 49160 | tf_op jit(solution)/shard_map/ppermute | solution.py:68
  39.4 10.1 %collective-permute-done.1 = bf16[64,128]{1,0:T(8,128)(2,1)S(1)} collective-permute-done((bf16[64,128]{1,0:T(8,128)(2,1)S(1)}, bf16[64,128]{1,0:T(8,128)(2,1)S(1)}, u32[]{:S(2)}, u32[]{:S(2)}) %collective-permute-start.1) | collective-permute-done | bytes 16416 | tf_op jit(solution)/shard_map/ppermute | solution.py:68
  49.7 1.9 collective-permute-start.3
  51.6 1.4 pad.26.rel
  53.0 2.2 collective-permute-done.3.other
  55.2 4.0 %edge_blocks.2 = (bf16[16,480,128]{2,1,0:T(8,128)(2,1)S(1)}, bf16[16,480,128]{2,1,0:T(8,128)(2,1)S(1)}, f32[400,128]{1,0:T(8,128)S(1)}) custom-call(s32[128]{0:T(128)S(1)} %slice_bitcast_fusion.5.scal, s32[1]{0:T(128)} %bitcast.14.here, s32[32,128]{1,0:T(8,128)S(1)} %get-tuple-element.77.lists, bf16[400,128]{1,0:T(8,128)(2,1)S(1)} %collective-permute-done.own, ...), custom_call_target="tpu_custom_call" | custom-call | flops 2000000000 | bytes 10000000 | tf_op jit(solution)/shard_map/edge_blocks/pallas_call | solution.py:205
  59.2 2.1 collective-permute-start.4
  61.3 3.8 %collective-permute-done.4 = bf16[16,480,128]{2,1,0:T(8,128)(2,1)S(1)} collective-permute-done((bf16[16,480,128]{2,1,0:T(8,128)(2,1)S(1)}, bf16[16,480,128]{2,1,0:T(8,128)(2,1)S(1)}, u32[]{:S(2)}, u32[]{:S(2)}) %collective-permute-start.4) | collective-permute-done | bytes 1966112 | tf_op jit(solution)/shard_map/ppermute | solution.py:68
  65.7 43.2 %all_to_all.35.pieces = bf16[16,480,128]{2,1,0:T(8,128)(2,1)S(1)} all-to-all(bf16[16,480,128]{2,1,0:T(8,128)(2,1)S(1)} %add.59), channel_id=1, replica_groups={{0,1,2,3,64,65,66,67,128,129,130,131,192,193,194,195},{32,33,34,35,96,9..., dimensions={0} | all-to-all | bytes 3932160 | tf_op jit(solution)/shard_map/all_to_all | solution.py:72
  108.9 0.7 middle_update.1
  109.6 1.4 broadcast_in_dim.34
  111.0 3.7 %all-to-all-start.2 = ((bf16[16,400,128]{2,1,0:T(8,128)(2,1)}), bf16[16,400,128]{2,1,0:T(8,128)(2,1)S(1)}, u32[]{:S(2)}, u32[]{:S(2)}) async-start(bf16[16,400,128]{2,1,0:T(8,128)(2,1)} %broadcast_in_dim.34), calls=%async_computation.2 | async-start | bytes 3276800 | tf_op jit(solution)/shard_map/all_to_all | solution.py:72
  114.8 3.6 %collective-permute-start.6 = (f32[80,128]{1,0:T(8,128)S(1)}, f32[80,128]{1,0:T(8,128)S(1)}, u32[]{:S(2)}, u32[]{:S(2)}) collective-permute-start(f32[80,128]{1,0:T(8,128)S(1)} %get-tuple-element.50), channel_id=1, source_target_pairs={{0,4},{1,5},{2,6},{3,7},{4,0},{5,1},{6,2},{7,3},{8,12},{9,13},{10,... | collective-permute-start | bytes 122888 | tf_op jit(solution)/shard_map/ppermute | solution.py:68
  118.4 1.4 collective-permute-done.6
  119.7 7.3 %collective-permute-start.7 = (f32[80,128]{1,0:T(8,128)S(1)}, f32[80,128]{1,0:T(8,128)S(1)}, u32[]{:S(2)}, u32[]{:S(2)}) collective-permute-start(f32[80,128]{1,0:T(8,128)S(1)} %add.60), channel_id=1, source_target_pairs={{0,8},{1,9},{2,10},{3,11},{4,12},{5,13},{6,14},{7,15},{8,0},{9,1},... | collective-permute-start | bytes 122888 | tf_op jit(solution)/shard_map/ppermute | solution.py:68
  127.0 1.7 collective-permute-done.7
  128.7 4.9 %collective-permute-start.8 = (bf16[80,128]{1,0:T(8,128)(2,1)S(1)}, bf16[80,128]{1,0:T(8,128)(2,1)S(1)}, u32[]{:S(2)}, u32[]{:S(2)}) collective-permute-start(bf16[80,128]{1,0:T(8,128)(2,1)S(1)} %add_convert_fusion.4), channel_id=1, source_target_pairs={{0,16},{1,17},{2,18},{3,19},{4,20},{5,21},{6,22},{7,23},{8,24},{9,... | collective-permute-start | bytes 61448 | tf_op jit(solution)/shard_map/ppermute | solution.py:68
  133.7 4.3 %collective-permute-start.5 = (bf16[432,128]{1,0:T(8,128)(2,1)S(1)}, bf16[432,128]{1,0:T(8,128)(2,1)S(1)}, u32[]{:S(2)}, u32[]{:S(2)}) collective-permute-start(bf16[432,128]{1,0:T(8,128)(2,1)S(1)} %pad_maximum_fusion.1), channel_id=1, source_target_pairs={{0,16},{1,17},{2,18},{3,19},{64,80},{65,81},{66,82},{67,83},{128,1... | collective-permute-start | bytes 331784 | tf_op jit(solution)/shard_map/ppermute | solution.py:68
  138.0 8.3 %collective-permute-done.5 = bf16[432,128]{1,0:T(8,128)(2,1)S(1)} collective-permute-done((bf16[432,128]{1,0:T(8,128)(2,1)S(1)}, bf16[432,128]{1,0:T(8,128)(2,1)S(1)}, u32[]{:S(2)}, u32[]{:S(2)}) %collective-permute-start.5) | collective-permute-done | bytes 110624 | tf_op jit(solution)/shard_map/ppermute | solution.py:68
  146.3 5.9 %collective-permute-start.10 = (bf16[16,400,128]{2,1,0:T(8,128)(2,1)S(1)}, bf16[16,400,128]{2,1,0:T(8,128)(2,1)}, u32[]{:S(2)}, u32[]{:S(2)}) collective-permute-start(bf16[16,400,128]{2,1,0:T(8,128)(2,1)S(1)} %all-to-all-done.2.half), channel_id=1, source_target_pairs={{0,32},{1,33},{2,34},{3,35},{4,36},{5,37},{6,38},{7,39},{8,40},{9,... | collective-permute-start | bytes 4915208 | tf_op jit(solution)/shard_map/ppermute | solution.py:68
  152.2 8.4 %collective-permute-start.9 = (bf16[80,128]{1,0:T(8,128)(2,1)S(1)}, bf16[80,128]{1,0:T(8,128)(2,1)S(1)}, u32[]{:S(2)}, u32[]{:S(2)}) collective-permute-start(bf16[80,128]{1,0:T(8,128)(2,1)S(1)} %convert_add_fusion), channel_id=1, source_target_pairs={{0,256},{1,257},{2,258},{3,259},{4,260},{5,261},{6,262},{7,263},{8... | collective-permute-start | bytes 61448 | tf_op jit(solution)/shard_map/ppermute | solution.py:68
  160.6 4.8 %collective-permute-done.9 = bf16[80,128]{1,0:T(8,128)(2,1)S(1)} collective-permute-done((bf16[80,128]{1,0:T(8,128)(2,1)S(1)}, bf16[80,128]{1,0:T(8,128)(2,1)S(1)}, u32[]{:S(2)}, u32[]{:S(2)}) %collective-permute-start.9) | collective-permute-done | bytes 20512 | tf_op jit(solution)/shard_map/ppermute | solution.py:68
  165.4 0.9 broadcast_in_dim.35
  166.3 8.4 %all-to-all-start.3 = ((bf16[32,80,128]{2,1,0:T(8,128)(2,1)}), bf16[32,80,128]{2,1,0:T(8,128)(2,1)S(1)}, u32[]{:S(2)}, u32[]{:S(2)}) async-start(bf16[32,80,128]{2,1,0:T(8,128)(2,1)} %broadcast_in_dim.35), calls=%async_computation.3 | async-start | bytes 1310720 | tf_op jit(solution)/shard_map/all_to_all | solution.py:72
  174.7 4.4 %collective-permute-start.11 = (f32[408,128]{1,0:T(8,128)}, f32[408,128]{1,0:T(8,128)}, u32[]{:S(2)}, u32[]{:S(2)}) collective-permute-start(f32[408,128]{1,0:T(8,128)} %copy-done.8), channel_id=1, source_target_pairs={{0,0},{1,1},{2,2},{3,3},{4,64},{5,65},{6,66},{7,67},{8,128},{9,129... | collective-permute-start | bytes 626696 | tf_op jit(solution)/shard_map/ppermute | solution.py:68
  179.1 1.5 slice.81.own
  180.7 0.7 slice_convert_fusion.lists
  181.4 5.6 %all-to-all-done.3 = bf16[32,80,128]{2,1,0:T(8,128)(2,1)S(1)} async-done(((bf16[32,80,128]{2,1,0:T(8,128)(2,1)}), bf16[32,80,128]{2,1,0:T(8,128)(2,1)S(1)}, u32[]{:S(2)}, u32[]{:S(2)}) %all-to-all-start.3) | async-done | bytes 655392 | tf_op jit(solution)/shard_map/all_to_all | solution.py:72
  187.0 1.3 copy-done
  188.3 0.9 relation_update.2
  189.3 1.0 copy-done.3
  190.3 5.1 %edge_blocks.3 = (bf16[16,400,128]{2,1,0:T(8,128)(2,1)S(1)}, bf16[16,400,128]{2,1,0:T(8,128)(2,1)}, f32[400,128]{1,0:T(8,128)S(1)}, bf16[2560,128]{1,0:T(8,128)(2,1)S(1)}) custom-call(s32[128]{0:T(128)S(1)} %slice_bitcast_fusion.4.scal, s32[1]{0:T(128)} %bitcast.14.here, s32[32,128]{1,0:T(8,128)S(1)} %slice_convert_fusion.lists, ...), custom_call_target="tpu_custom_call" | custom-call | flops 2000000000 | bytes 10000000 | tf_op jit(solution)/shard_map/edge_blocks/pallas_call | solution.py:205
  196.1 4.5 %collective-permute-start.12 = (bf16[16,400,128]{2,1,0:T(8,128)(2,1)}, bf16[16,400,128]{2,1,0:T(8,128)(2,1)}, u32[]{:S(2)}, u32[]{:S(2)}) collective-permute-start(bf16[16,400,128]{2,1,0:T(8,128)(2,1)} %get-tuple-element.58), channel_id=1, source_target_pairs={{0,32},{1,33},{2,34},{3,35},{4,36},{5,37},{6,38},{7,39},{8,40},{9,... | collective-permute-start | bytes 4915208 | tf_op jit(solution)/shard_map/ppermute | solution.py:68
  200.6 15.5 %all-to-all-start.4 = ((bf16[32,80,128]{2,1,0:T(8,128)(2,1)}), bf16[32,80,128]{2,1,0:T(8,128)(2,1)S(1)}, u32[]{:S(2)}, u32[]{:S(2)}) async-start(bf16[32,80,128]{2,1,0:T(8,128)(2,1)} %bitcast.65), calls=%async_computation.4 | async-start | bytes 1310720 | tf_op jit(solution)/shard_map/all_to_all | solution.py:72
  216.1 0.9 convert_element_type.68
  217.0 3.0 add.64
  220.1 13.5 %collective-permute-start.13 = (bf16[400,128]{1,0:T(8,128)(2,1)S(1)}, bf16[400,128]{1,0:T(8,128)(2,1)S(1)}, u32[]{:S(2)}, u32[]{:S(2)}) collective-permute-start(bf16[400,128]{1,0:T(8,128)(2,1)S(1)} %convert_element_type.68), channel_id=1, source_target_pairs={{16,0},{17,1},{18,2},{19,3},{80,4},{81,5},{82,6},{83,7},{144,8},{1... | collective-permute-start | bytes 307208 | tf_op jit(solution)/shard_map/ppermute | solution.py:68
  233.6 1.6 collective-permute-done.13.lhs
  235.9 8.6 %all-to-all-start.5 = ((bf16[16,400,128]{2,1,0:T(8,128)(2,1)}), bf16[16,400,128]{2,1,0:T(8,128)(2,1)S(1)}, u32[]{:S(2)}, u32[]{:S(2)}) async-start(bf16[16,400,128]{2,1,0:T(8,128)(2,1)} %add.64), calls=%async_computation.5 | async-start | bytes 3276800 | tf_op jit(solution)/shard_map/all_to_all | solution.py:72
  244.7 2.3 collective-permute-start.15
  247.0 2.5 collective-permute-done.15
  249.5 2.1 collective-permute-start.16
  251.6 4.2 %collective-permute-done.16 = f32[80,128]{1,0:T(8,128)S(1)} collective-permute-done((f32[80,128]{1,0:T(8,128)S(1)}, f32[80,128]{1,0:T(8,128)S(1)}, u32[]{:S(2)}, u32[]{:S(2)}) %collective-permute-start.16) | collective-permute-done | bytes 40992 | tf_op jit(solution)/shard_map/ppermute | solution.py:68
  255.9 5.5 %collective-permute-start.17 = (bf16[80,128]{1,0:T(8,128)(2,1)S(1)}, bf16[80,128]{1,0:T(8,128)(2,1)S(1)}, u32[]{:S(2)}, u32[]{:S(2)}) collective-permute-start(bf16[80,128]{1,0:T(8,128)(2,1)S(1)} %add_convert_fusion.2), channel_id=1, source_target_pairs={{0,16},{1,17},{2,18},{3,19},{4,20},{5,21},{6,22},{7,23},{8,24},{9,... | collective-permute-start | bytes 61448 | tf_op jit(solution)/shard_map/ppermute | solution.py:68
  261.4 3.0 collective-permute-done.17
  264.3 12.8 %collective-permute-start.18 = (bf16[80,128]{1,0:T(8,128)(2,1)S(1)}, bf16[80,128]{1,0:T(8,128)(2,1)S(1)}, u32[]{:S(2)}, u32[]{:S(2)}) collective-permute-start(bf16[80,128]{1,0:T(8,128)(2,1)S(1)} %add_convert_fusion.1), channel_id=1, source_target_pairs={{0,256},{1,257},{2,258},{3,259},{4,260},{5,261},{6,262},{7,263},{8... | collective-permute-start | bytes 61448 | tf_op jit(solution)/shard_map/ppermute | solution.py:68
  277.1 1.2 collective-permute-done.18
  278.3 1.0 broadcast_in_dim.36
  279.3 12.2 %all-to-all-start.6 = ((bf16[32,80,128]{2,1,0:T(8,128)(2,1)}), bf16[32,80,128]{2,1,0:T(8,128)(2,1)S(1)}, u32[]{:S(2)}, u32[]{:S(2)}) async-start(bf16[32,80,128]{2,1,0:T(8,128)(2,1)} %broadcast_in_dim.36), calls=%async_computation.6 | async-start | bytes 1310720 | tf_op jit(solution)/shard_map/all_to_all | solution.py:72
  291.5 1.1 fold_pieces.2
  292.6 2.8 collective-permute-start.14
  295.4 8.4 %all-to-all-done.6 = bf16[32,80,128]{2,1,0:T(8,128)(2,1)S(1)} async-done(((bf16[32,80,128]{2,1,0:T(8,128)(2,1)}), bf16[32,80,128]{2,1,0:T(8,128)(2,1)S(1)}, u32[]{:S(2)}, u32[]{:S(2)}) %all-to-all-start.6) | async-done | bytes 655392 | tf_op jit(solution)/shard_map/all_to_all | solution.py:72
  303.8 1.3 copy-done.4
  305.1 2.4 relation_update.3
  308.1 1.8 last_update.1
  (74 shorter events, 6.3 us)
Async XLA Ops:
  1.6 14.1 %collective-permute-start = (bf16[400,128]{1,0:T(8,128)(2,1)S(1)}, bf16[400,128]{1,0:T(8,128)(2,1)S(1)}, u32[]{:S(2)}, u32[]{:S(2)}) collective-permute-start(bf16[400,128]{1,0:T(8,128)(2,1)S(1)} %bitcast_convert_fusion), channel_id=1, source_target_pairs={{0,0},{1,1},{2,2},{3,3},{4,64},{5,65},{6,66},{7,67},{8,128},{9,129... | collective-permute-start | bytes 307208 | tf_op jit(solution)/shard_map/ppermute | solution.py:68
  17.8 10.5 %copy-start.15 = (f32[128]{0:T(128)S(1)}, f32[128]{0:T(128)}, u32[]{:S(2)}) copy-start(f32[128]{0:T(128)} %param.11) | copy-start | bytes 1540
  17.8 10.5 %copy-start.9 = (f32[128,400]{0,1:T(8,128)S(1)}, f32[128,400]{0,1:T(8,128)}, u32[]{:S(2)}) copy-start(f32[128,400]{0,1:T(8,128)} %param.10) | copy-start | bytes 614404
  17.8 18.0 %copy-start.13 = (s32[2,10,128]{2,0,1:T(2,128)S(1)}, s32[2,10,128]{2,0,1:T(2,128)}, u32[]{:S(2)}) copy-start(s32[2,10,128]{2,0,1:T(2,128)} %param.18) | copy-start | bytes 30724
  17.8 18.0 %copy-start.14 = (s32[2,10,128]{2,0,1:T(2,128)S(1)}, s32[2,10,128]{2,0,1:T(2,128)}, u32[]{:S(2)}) copy-start(s32[2,10,128]{2,0,1:T(2,128)} %param.17) | copy-start | bytes 30724
  17.8 31.9 %all-to-all-start = ((bf16[16,400,128]{2,1,0:T(8,128)(2,1)}), bf16[16,400,128]{2,1,0:T(8,128)(2,1)S(1)}, u32[]{:S(2)}, u32[]{:S(2)}) async-start(bf16[16,400,128]{2,1,0:T(8,128)(2,1)} %broadcast_in_dim.29), calls=%async_computation | async-start | bytes 3276800 | tf_op jit(solution)/shard_map/all_to_all | solution.py:72
  28.3 21.2 %collective-permute-start.2 = (f32[408,128]{1,0:T(8,128)S(1)}, f32[408,128]{1,0:T(8,128)S(1)}, u32[]{:S(2)}, u32[]{:S(2)}) collective-permute-start(f32[408,128]{1,0:T(8,128)S(1)} %pad_maximum_fusion), channel_id=1, source_target_pairs={{0,0},{1,1},{2,2},{3,3},{4,64},{5,65},{6,66},{7,67},{8,128},{9,129... | collective-permute-start | bytes 626696 | tf_op jit(solution)/shard_map/ppermute | solution.py:68
  35.9 13.6 %collective-permute-start.1 = (bf16[64,128]{1,0:T(8,128)(2,1)S(1)}, bf16[64,128]{1,0:T(8,128)(2,1)S(1)}, u32[]{:S(2)}, u32[]{:S(2)}) collective-permute-start(bf16[64,128]{1,0:T(8,128)(2,1)S(1)} %pad_maximum_fusion.2), channel_id=1, source_target_pairs={{0,0},{1,1},{2,2},{3,3},{4,64},{5,65},{6,66},{7,67},{8,128},{9,129... | collective-permute-start | bytes 49160 | tf_op jit(solution)/shard_map/ppermute | solution.py:68
  49.7 5.5 %collective-permute-start.3 = (bf16[16,400,128]{2,1,0:T(8,128)(2,1)S(1)}, bf16[16,400,128]{2,1,0:T(8,128)(2,1)}, u32[]{:S(2)}, u32[]{:S(2)}) collective-permute-start(bf16[16,400,128]{2,1,0:T(8,128)(2,1)S(1)} %all-to-all-done.half), channel_id=1, source_target_pairs={{0,32},{1,33},{2,34},{3,35},{4,36},{5,37},{6,38},{7,39},{8,40},{9,... | collective-permute-start | bytes 4915208 | tf_op jit(solution)/shard_map/ppermute | solution.py:68
  59.2 5.9 %collective-permute-start.4 = (bf16[16,480,128]{2,1,0:T(8,128)(2,1)S(1)}, bf16[16,480,128]{2,1,0:T(8,128)(2,1)S(1)}, u32[]{:S(2)}, u32[]{:S(2)}) collective-permute-start(bf16[16,480,128]{2,1,0:T(8,128)(2,1)S(1)} %get-tuple-element.46), channel_id=1, source_target_pairs={{0,32},{1,33},{2,34},{3,35},{4,36},{5,37},{6,38},{7,39},{8,40},{9,... | collective-permute-start | bytes 5898248 | tf_op jit(solution)/shard_map/ppermute | solution.py:68
  109.6 56.7 %copy-start.8 = (f32[408,128]{1,0:T(8,128)}, f32[408,128]{1,0:T(8,128)S(1)}, u32[]{:S(2)}) copy-start(f32[408,128]{1,0:T(8,128)S(1)} %get-tuple-element.55) | copy-start | bytes 626692
  111.0 35.2 %all-to-all-start.2 = ((bf16[16,400,128]{2,1,0:T(8,128)(2,1)}), bf16[16,400,128]{2,1,0:T(8,128)(2,1)S(1)}, u32[]{:S(2)}, u32[]{:S(2)}) async-start(bf16[16,400,128]{2,1,0:T(8,128)(2,1)} %broadcast_in_dim.34), calls=%async_computation.2 | async-start | bytes 3276800 | tf_op jit(solution)/shard_map/all_to_all | solution.py:72
  114.8 5.0 %collective-permute-start.6 = (f32[80,128]{1,0:T(8,128)S(1)}, f32[80,128]{1,0:T(8,128)S(1)}, u32[]{:S(2)}, u32[]{:S(2)}) collective-permute-start(f32[80,128]{1,0:T(8,128)S(1)} %get-tuple-element.50), channel_id=1, source_target_pairs={{0,4},{1,5},{2,6},{3,7},{4,0},{5,1},{6,2},{7,3},{8,12},{9,13},{10,... | collective-permute-start | bytes 122888 | tf_op jit(solution)/shard_map/ppermute | solution.py:68
  119.7 9.0 %collective-permute-start.7 = (f32[80,128]{1,0:T(8,128)S(1)}, f32[80,128]{1,0:T(8,128)S(1)}, u32[]{:S(2)}, u32[]{:S(2)}) collective-permute-start(f32[80,128]{1,0:T(8,128)S(1)} %add.60), channel_id=1, source_target_pairs={{0,8},{1,9},{2,10},{3,11},{4,12},{5,13},{6,14},{7,15},{8,0},{9,1},... | collective-permute-start | bytes 122888 | tf_op jit(solution)/shard_map/ppermute | solution.py:68
  128.7 9.2 %collective-permute-start.8 = (bf16[80,128]{1,0:T(8,128)(2,1)S(1)}, bf16[80,128]{1,0:T(8,128)(2,1)S(1)}, u32[]{:S(2)}, u32[]{:S(2)}) collective-permute-start(bf16[80,128]{1,0:T(8,128)(2,1)S(1)} %add_convert_fusion.4), channel_id=1, source_target_pairs={{0,16},{1,17},{2,18},{3,19},{4,20},{5,21},{6,22},{7,23},{8,24},{9,... | collective-permute-start | bytes 61448 | tf_op jit(solution)/shard_map/ppermute | solution.py:68
  133.7 12.6 %collective-permute-start.5 = (bf16[432,128]{1,0:T(8,128)(2,1)S(1)}, bf16[432,128]{1,0:T(8,128)(2,1)S(1)}, u32[]{:S(2)}, u32[]{:S(2)}) collective-permute-start(bf16[432,128]{1,0:T(8,128)(2,1)S(1)} %pad_maximum_fusion.1), channel_id=1, source_target_pairs={{0,16},{1,17},{2,18},{3,19},{64,80},{65,81},{66,82},{67,83},{128,1... | collective-permute-start | bytes 331784 | tf_op jit(solution)/shard_map/ppermute | solution.py:68
  146.2 20.1 %copy-start.10 = (bf16[432,128]{1,0:T(8,128)(2,1)}, bf16[432,128]{1,0:T(8,128)(2,1)S(1)}, u32[]{:S(2)}) copy-start(bf16[432,128]{1,0:T(8,128)(2,1)S(1)} %collective-permute-done.5) | copy-start | bytes 331780
  146.3 44.0 %collective-permute-start.10 = (bf16[16,400,128]{2,1,0:T(8,128)(2,1)S(1)}, bf16[16,400,128]{2,1,0:T(8,128)(2,1)}, u32[]{:S(2)}, u32[]{:S(2)}) collective-permute-start(bf16[16,400,128]{2,1,0:T(8,128)(2,1)S(1)} %all-to-all-done.2.half), channel_id=1, source_target_pairs={{0,32},{1,33},{2,34},{3,35},{4,36},{5,37},{6,38},{7,39},{8,40},{9,... | collective-permute-start | bytes 4915208 | tf_op jit(solution)/shard_map/ppermute | solution.py:68
  152.2 13.2 %collective-permute-start.9 = (bf16[80,128]{1,0:T(8,128)(2,1)S(1)}, bf16[80,128]{1,0:T(8,128)(2,1)S(1)}, u32[]{:S(2)}, u32[]{:S(2)}) collective-permute-start(bf16[80,128]{1,0:T(8,128)(2,1)S(1)} %convert_add_fusion), channel_id=1, source_target_pairs={{0,256},{1,257},{2,258},{3,259},{4,260},{5,261},{6,262},{7,263},{8... | collective-permute-start | bytes 61448 | tf_op jit(solution)/shard_map/ppermute | solution.py:68
  166.3 20.7 %all-to-all-start.3 = ((bf16[32,80,128]{2,1,0:T(8,128)(2,1)}), bf16[32,80,128]{2,1,0:T(8,128)(2,1)S(1)}, u32[]{:S(2)}, u32[]{:S(2)}) async-start(bf16[32,80,128]{2,1,0:T(8,128)(2,1)} %broadcast_in_dim.35), calls=%async_computation.3 | async-start | bytes 1310720 | tf_op jit(solution)/shard_map/all_to_all | solution.py:72
  174.7 15.6 %collective-permute-start.11 = (f32[408,128]{1,0:T(8,128)}, f32[408,128]{1,0:T(8,128)}, u32[]{:S(2)}, u32[]{:S(2)}) collective-permute-start(f32[408,128]{1,0:T(8,128)} %copy-done.8), channel_id=1, source_target_pairs={{0,0},{1,1},{2,2},{3,3},{4,64},{5,65},{6,66},{7,67},{8,128},{9,129... | collective-permute-start | bytes 626696 | tf_op jit(solution)/shard_map/ppermute | solution.py:68
  187.0 1.3 copy-start
  188.3 2.0 copy-start.7
  189.2 1.0 copy-start.3
  190.3 5.2 %copy-start.1 = (f32[400,768]{1,0:T(8,128)}, f32[400,768]{1,0:T(8,128)S(1)}, u32[]{:S(2)}) copy-start(f32[400,768]{1,0:T(8,128)S(1)} %get-tuple-element.53.rel) | copy-start | bytes 3686404
  195.4 0.7 copy-start.6
  196.1 4.5 %copy-start.5 = (bf16[2560,128]{1,0:T(8,128)(2,1)}, bf16[2560,128]{1,0:T(8,128)(2,1)S(1)}, u32[]{:S(2)}) copy-start(bf16[2560,128]{1,0:T(8,128)(2,1)S(1)} %get-tuple-element.61) | copy-start | bytes 1966084
  196.1 20.9 %collective-permute-start.12 = (bf16[16,400,128]{2,1,0:T(8,128)(2,1)}, bf16[16,400,128]{2,1,0:T(8,128)(2,1)}, u32[]{:S(2)}, u32[]{:S(2)}) collective-permute-start(bf16[16,400,128]{2,1,0:T(8,128)(2,1)} %get-tuple-element.58), channel_id=1, source_target_pairs={{0,32},{1,33},{2,34},{3,35},{4,36},{5,37},{6,38},{7,39},{8,40},{9,... | collective-permute-start | bytes 4915208 | tf_op jit(solution)/shard_map/ppermute | solution.py:68
  200.6 33.0 %all-to-all-start.4 = ((bf16[32,80,128]{2,1,0:T(8,128)(2,1)}), bf16[32,80,128]{2,1,0:T(8,128)(2,1)S(1)}, u32[]{:S(2)}, u32[]{:S(2)}) async-start(bf16[32,80,128]{2,1,0:T(8,128)(2,1)} %bitcast.65), calls=%async_computation.4 | async-start | bytes 1310720 | tf_op jit(solution)/shard_map/all_to_all | solution.py:72
  220.1 15.2 %collective-permute-start.13 = (bf16[400,128]{1,0:T(8,128)(2,1)S(1)}, bf16[400,128]{1,0:T(8,128)(2,1)S(1)}, u32[]{:S(2)}, u32[]{:S(2)}) collective-permute-start(bf16[400,128]{1,0:T(8,128)(2,1)S(1)} %convert_element_type.68), channel_id=1, source_target_pairs={{16,0},{17,1},{18,2},{19,3},{80,4},{81,5},{82,6},{83,7},{144,8},{1... | collective-permute-start | bytes 307208 | tf_op jit(solution)/shard_map/ppermute | solution.py:68
  235.2 0.7 copy-start.11
  235.9 42.4 %all-to-all-start.5 = ((bf16[16,400,128]{2,1,0:T(8,128)(2,1)}), bf16[16,400,128]{2,1,0:T(8,128)(2,1)S(1)}, u32[]{:S(2)}, u32[]{:S(2)}) async-start(bf16[16,400,128]{2,1,0:T(8,128)(2,1)} %add.64), calls=%async_computation.5 | async-start | bytes 3276800 | tf_op jit(solution)/shard_map/all_to_all | solution.py:72
  244.7 4.7 %collective-permute-start.15 = (f32[80,128]{1,0:T(8,128)S(1)}, f32[80,128]{1,0:T(8,128)S(1)}, u32[]{:S(2)}, u32[]{:S(2)}) collective-permute-start(f32[80,128]{1,0:T(8,128)S(1)} %fold_pieces.3), channel_id=1, source_target_pairs={{0,4},{1,5},{2,6},{3,7},{4,0},{5,1},{6,2},{7,3},{8,12},{9,13},{10,... | collective-permute-start | bytes 122888 | tf_op jit(solution)/shard_map/ppermute | solution.py:68
  249.5 6.4 %collective-permute-start.16 = (f32[80,128]{1,0:T(8,128)S(1)}, f32[80,128]{1,0:T(8,128)S(1)}, u32[]{:S(2)}, u32[]{:S(2)}) collective-permute-start(f32[80,128]{1,0:T(8,128)S(1)} %add.65), channel_id=1, source_target_pairs={{0,8},{1,9},{2,10},{3,11},{4,12},{5,13},{6,14},{7,15},{8,0},{9,1},... | collective-permute-start | bytes 122888 | tf_op jit(solution)/shard_map/ppermute | solution.py:68
  255.9 8.4 %collective-permute-start.17 = (bf16[80,128]{1,0:T(8,128)(2,1)S(1)}, bf16[80,128]{1,0:T(8,128)(2,1)S(1)}, u32[]{:S(2)}, u32[]{:S(2)}) collective-permute-start(bf16[80,128]{1,0:T(8,128)(2,1)S(1)} %add_convert_fusion.2), channel_id=1, source_target_pairs={{0,16},{1,17},{2,18},{3,19},{4,20},{5,21},{6,22},{7,23},{8,24},{9,... | collective-permute-start | bytes 61448 | tf_op jit(solution)/shard_map/ppermute | solution.py:68
  264.3 14.0 %collective-permute-start.18 = (bf16[80,128]{1,0:T(8,128)(2,1)S(1)}, bf16[80,128]{1,0:T(8,128)(2,1)S(1)}, u32[]{:S(2)}, u32[]{:S(2)}) collective-permute-start(bf16[80,128]{1,0:T(8,128)(2,1)S(1)} %add_convert_fusion.1), channel_id=1, source_target_pairs={{0,256},{1,257},{2,258},{3,259},{4,260},{5,261},{6,262},{7,263},{8... | collective-permute-start | bytes 61448 | tf_op jit(solution)/shard_map/ppermute | solution.py:68
  279.3 24.5 %copy-start.2 = (f32[400,768]{1,0:T(8,128)S(1)}, f32[400,768]{1,0:T(8,128)}, u32[]{:S(2)}) copy-start(f32[400,768]{1,0:T(8,128)} %copy-done.1) | copy-start | bytes 3686404
  279.3 24.5 %all-to-all-start.6 = ((bf16[32,80,128]{2,1,0:T(8,128)(2,1)}), bf16[32,80,128]{2,1,0:T(8,128)(2,1)S(1)}, u32[]{:S(2)}, u32[]{:S(2)}) async-start(bf16[32,80,128]{2,1,0:T(8,128)(2,1)} %broadcast_in_dim.36), calls=%async_computation.6 | async-start | bytes 1310720 | tf_op jit(solution)/shard_map/all_to_all | solution.py:72
  292.6 14.8 %collective-permute-start.14 = (bf16[400,128]{1,0:T(8,128)(2,1)}, bf16[400,128]{1,0:T(8,128)(2,1)S(1)}, u32[]{:S(2)}, u32[]{:S(2)}) collective-permute-start(bf16[400,128]{1,0:T(8,128)(2,1)} %fold_pieces.2), channel_id=1, source_target_pairs={{0,0},{1,1},{2,2},{3,3},{4,64},{5,65},{6,66},{7,67},{8,128},{9,129... | collective-permute-start | bytes 307208 | tf_op jit(solution)/shard_map/ppermute | solution.py:68
  303.8 1.3 copy-start.4
  307.5 0.6 copy-start.12

commit v3 on v1

--- a/solution.py
+++ b/solution.py
@@ -39,9 +39,8 @@
 
 ALL = range(N_DOM * N_EDGE)
 TURN = [(v, turn(v)) for v in ALL]
-AHEAD = [(v, ahead(v)) for v in ALL]
-BACK = [(ahead(v), v) for v in ALL]
 NEXT = [(turn(v), ahead(v)) for v in ALL]
+PREVIOUS = [(target, source) for source, target in NEXT]
 
 
 OTHER = []
@@ -232,27 +231,27 @@
     )(pieces, lhs, kept)
 
 
-def fold_kernel(pieces, out):
-    out[...] = add_pieces(pieces).astype(out.dtype)
-
-
-def fold(pieces, kind):
+def fold_kernel(pieces, more, out):
+    out[...] = (add_pieces(pieces) + more[...].astype(F32)).astype(out.dtype)
+
+
+def fold(pieces, more):
     return pl.pallas_call(
         fold_kernel,
-        out_shape=jax.ShapeDtypeStruct(pieces.shape[1:], kind),
+        out_shape=jax.ShapeDtypeStruct(more.shape, more.dtype),
         compiler_params=pltpu.CompilerParams(vmem_limit_bytes=16 * MIB),
         name="fold_pieces",
-    )(pieces)
-
-
-def last_kernel(rhs, lhs, kept, weights_out, state_out):
-    weights, state = adagrad(rhs[...].astype(F32) + lhs[...].astype(F32), kept[...])
+    )(pieces, more)
+
+
+def last_kernel(grads, kept, weights_out, state_out):
+    weights, state = adagrad(grads[...].astype(F32), kept[...])
     weights_out[...] = weights
     state_out[...] = state
 
 
-def last(rhs, lhs, kept):
-    width, block = lhs.shape
+def last(grads, kept):
+    width, block = grads.shape
     return pl.pallas_call(
         last_kernel,
         out_shape=(
@@ -260,7 +259,7 @@
             jax.ShapeDtypeStruct((1, block), F32),
         ),
         name="last_update",
-    )(rhs, lhs, kept)
+    )(grads, kept)
 
 
 def z_step(total, step, kind):
@@ -268,14 +267,11 @@
     return mine.astype(F32) + send(mine, z_pairs(step)).astype(F32)
 
 
-def exchange_terms(mine, theirs, rel_part):
-    swapped = send(theirs, OTHER)
-    rel_pieces = exchange(rel_part.reshape(32, PIECE, -1), PLANES)
-    summed, rel_pieces = together(mine + swapped, rel_pieces)
-    rel_mine = fold(rel_pieces, F32)
+def z_steps(total):
+    total = jnp.sum(total, 0, dtype=F32)
     for step, kind in ((1, F32), (2, F32), (4, BF16)):
-        rel_mine = z_step(rel_mine, step, kind)
-    return exchange(summed, SHEETS), rel_mine
+        total = z_step(total, step, kind)
+    return total
 
 
 def spread_relations(mine):
@@ -352,6 +348,9 @@
 
     weights = entities.T
     own = send(weights.astype(BF16), TURN)
+    own, weights, source_rows, target_rows, dst_blocks = together(
+        own, weights, source_rows, target_rows, dst_blocks
+    )
     lists = send(jnp.concatenate([lists_of(0), lists_of(1)]), TURN)
     kept = send(jnp.concatenate([weights, jnp.broadcast_to(entity_state[None], (8, block))]), TURN)
 
@@ -362,8 +361,11 @@
 
     half, lists, kept = together(gather_sheet(own), lists, kept)
     other = send(half, OTHER)
-    mine, theirs, lhs, rel_part = run_blocks(lists[:LISTS].astype(jnp.int32), here, own, rel, half, other)
-    pieces, rel_mine = together(*exchange_terms(mine, theirs, rel_part))
+    now = lists[:LISTS].astype(jnp.int32)
+    mine, theirs, lhs, rel_part = run_blocks(now, here, own, rel, half, other)
+    rel_pieces = exchange(rel_part.reshape(32, PIECE, block), PLANES)
+    summed, rel_pieces = together(mine + send(theirs, OTHER), rel_pieces)
+    pieces, rel_mine = together(exchange(summed, SHEETS), z_steps(rel_pieces))
     kept, own = middle(pieces, lhs, kept)
     source = send(jnp.concatenate([own, lists[LISTS:]]), NEXT)
     kept = send(kept, TURN)
@@ -372,12 +374,16 @@
     rel, rel_state = relation_update(spread_relations(rel_mine), rel, rel_state, lanes)
     other, kept = together(other, kept)
 
-    lists = source[width:].astype(jnp.int32)
-    mine, theirs, lhs, rel_part = run_blocks(lists, here, source[:width], rel, half, other)
-    pieces, rel_mine = exchange_terms(mine, theirs, rel_part)
-    rel_sum = spread_relations(z_step(rel_mine, 8, BF16))
-    rhs, lhs = together(fold(pieces, BF16), lhs.astype(BF16))
-    weights, state = last(send(rhs, TURN), send(lhs, BACK), kept)
+    now = source[width:].astype(jnp.int32)
+    mine, theirs, lhs, rel_part = run_blocks(now, here, source[:width], rel, half, other)
+    rel_pieces = exchange(rel_part.reshape(32, PIECE, block), PLANES)
+    summed, lhs = together(mine + send(theirs, OTHER), lhs.astype(BF16))
+    summed, rel_pieces, lhs = together(summed, rel_pieces, send(lhs, PREVIOUS))
+    rel_mine = z_step(z_steps(rel_pieces), 8, BF16)
+    pieces, rel_mine = together(exchange(summed, SHEETS), rel_mine)
+    grads = send(fold(pieces, lhs), TURN)
+    rel_sum = spread_relations(rel_mine)
+    weights, state = last(grads, kept)
     rel, rel_state = relation_update(rel_sum, rel, rel_state, count)
     return (weights.T, state[0], rel.T, rel_state.T)
 

time: 308 us -> 306 us (level)
  the two profiles are of different devices: /device:TPU:27 before, /device:TPU:1 now
where the time goes in v3:
time: 306 us; the launch traced here: 301 us
  starting transfers between devices  162 us (53%)
  waiting for transfers between devices  78.1 us (26%)
  Pallas kernels  29.8 us (10%)
  local copies, waits for them, and re-layouts  17 us (6%)
  other arithmetic  12.6 us (4%)
    ppermute x19, starting transfers between devices, send(): return lax.ppermute(value, AXES, pairs)  91.5 us
    all_to_all x8, starting transfers between devices, exchange(): lax.all_to_all(value, AXES, 0, 0, axis_index_groups=groups, tiled=True)  70.4 us
    ppermute x19, waiting for transfers between devices, send(): return lax.ppermute(value, AXES, pairs)  58 us
    pallas_call x2, Pallas kernels, run_blocks(): pl.pallas_call(blocks_kernel, out_shape=(jax.ShapeDtypeStruct((16, width,...  23.7 us
    all_to_all x8, waiting for transfers between devices, exchange(): lax.all_to_all(value, AXES, 0, 0, axis_index_groups=groups, tiled=True)  20.1 us
    unnamed x34, local copies, waits for them, and re-layouts  8.47 us
  transfers between devices with their start and end apart: 27, of which 17 were waited for; matrix products, arithmetic and copies ran while one was open for 5% of the time, Pallas kernels for 1%

profile of v3, /device:TPU:1, one launch (start us, length us, event | category | flops | bytes accessed | tf_op | source)
XLA Modules:
  0.0 300.5 jit_solution(3712742278142569075)
XLA Ops:
  0.6 0.9 bitcast_convert_fusion
  1.6 10.2 %collective-permute-start = (bf16[400,128]{1,0:T(8,128)(2,1)S(1)}, bf16[400,128]{1,0:T(8,128)(2,1)S(1)}, u32[]{:S(2)}, u32[]{:S(2)}) collective-permute-start(bf16[400,128]{1,0:T(8,128)(2,1)S(1)} %bitcast_convert_fusion), channel_id=1, source_target_pairs={{0,0},{1,1},{2,2},{3,3},{4,64},{5,65},{6,66},{7,67},{8,128},{9,129... | collective-permute-start | bytes 307208 | tf_op jit(solution)/shard_map/ppermute | solution.py:65
  13.2 0.8 fusion.10
  14.3 0.8 fusion.12
  16.4 1.4 broadcast_in_dim.29
  17.8 10.4 %all-to-all-start = ((bf16[16,400,128]{2,1,0:T(8,128)(2,1)}), bf16[16,400,128]{2,1,0:T(8,128)(2,1)S(1)}, u32[]{:S(2)}, u32[]{:S(2)}) async-start(bf16[16,400,128]{2,1,0:T(8,128)(2,1)} %broadcast_in_dim.29), calls=%async_computation | async-start | bytes 3276800 | tf_op jit(solution)/shard_map/all_to_all | solution.py:69
  28.3 5.9 %collective-permute-start.2 = (f32[408,128]{1,0:T(8,128)S(1)}, f32[408,128]{1,0:T(8,128)S(1)}, u32[]{:S(2)}, u32[]{:S(2)}) collective-permute-start(f32[408,128]{1,0:T(8,128)S(1)} %pad_maximum_fusion), channel_id=1, source_target_pairs={{0,0},{1,1},{2,2},{3,3},{4,64},{5,65},{6,66},{7,67},{8,128},{9,129... | collective-permute-start | bytes 626696 | tf_op jit(solution)/shard_map/ppermute | solution.py:65
  35.9 3.5 %collective-permute-start.1 = (bf16[64,128]{1,0:T(8,128)(2,1)S(1)}, bf16[64,128]{1,0:T(8,128)(2,1)S(1)}, u32[]{:S(2)}, u32[]{:S(2)}) collective-permute-start(bf16[64,128]{1,0:T(8,128)(2,1)S(1)} %pad_maximum_fusion.2), channel_id=1, source_target_pairs={{0,0},{1,1},{2,2},{3,3},{4,64},{5,65},{6,66},{7,67},{8,128},{9,129... | collective-permute-start | bytes 49160 | tf_op jit(solution)/shard_map/ppermute | solution.py:65
  39.4 10.1 %collective-permute-done.1 = bf16[64,128]{1,0:T(8,128)(2,1)S(1)} collective-permute-done((bf16[64,128]{1,0:T(8,128)(2,1)S(1)}, bf16[64,128]{1,0:T(8,128)(2,1)S(1)}, u32[]{:S(2)}, u32[]{:S(2)}) %collective-permute-start.1) | collective-permute-done | bytes 16416 | tf_op jit(solution)/shard_map/ppermute | solution.py:65
  49.7 1.9 collective-permute-start.3
  51.6 1.4 pad.26.rel
  53.0 2.2 collective-permute-done.3.other
  55.2 6.5 %edge_blocks.2 = (bf16[16,400,128]{2,1,0:T(8,128)(2,1)S(1)}, bf16[16,400,128]{2,1,0:T(8,128)(2,1)}, f32[400,128]{1,0:T(8,128)S(1)}, bf16[2560,128]{1,0:T(8,128)(2,1)}) custom-call(s32[128]{0:T(128)S(1)} %slice_bitcast_fusion.5.scal, s32[1]{0:T(128)} %bitcast.14.here, s32[32,128]{1,0:T(8,128)S(1)} %get-tuple-element.89.lists, ...), custom_call_target="tpu_custom_call" | custom-call | flops 2000000000 | bytes 10000000 | tf_op jit(solution)/shard_map/edge_blocks/pallas_call | solution.py:181
  61.7 1.1 copy-done
  62.9 5.9 %collective-permute-start.4 = (bf16[16,400,128]{2,1,0:T(8,128)(2,1)}, bf16[16,400,128]{2,1,0:T(8,128)(2,1)}, u32[]{:S(2)}, u32[]{:S(2)}) collective-permute-start(bf16[16,400,128]{2,1,0:T(8,128)(2,1)} %get-tuple-element.52), channel_id=1, source_target_pairs={{0,32},{1,33},{2,34},{3,35},{4,36},{5,37},{6,38},{7,39},{8,40},{9,... | collective-permute-start | bytes 4915208 | tf_op jit(solution)/shard_map/ppermute | solution.py:65
  68.7 12.9 %all-to-all-start.1 = ((bf16[32,80,128]{2,1,0:T(8,128)(2,1)}), bf16[32,80,128]{2,1,0:T(8,128)(2,1)S(1)}, u32[]{:S(2)}, u32[]{:S(2)}) async-start(bf16[32,80,128]{2,1,0:T(8,128)(2,1)} %bitcast.16), calls=%async_computation.1 | async-start | bytes 1310720 | tf_op jit(solution)/shard_map/all_to_all | solution.py:69
  81.7 3.6 %add.59 = bf16[16,400,128]{2,1,0:T(8,128)(2,1)} add(bf16[16,400,128]{2,1,0:T(8,128)(2,1)} %copy-done, bf16[16,400,128]{2,1,0:T(8,128)(2,1)} %collective-permute-done.4) | non-fusion elementwise | flops 819200 | bytes 4915200 | tf_op jit(solution)/shard_map/add | solution.py:367
  85.3 8.7 %all-to-all-done.1 = bf16[32,80,128]{2,1,0:T(8,128)(2,1)S(1)} async-done(((bf16[32,80,128]{2,1,0:T(8,128)(2,1)}), bf16[32,80,128]{2,1,0:T(8,128)(2,1)S(1)}, u32[]{:S(2)}, u32[]{:S(2)}) %all-to-all-start.1) | async-done | bytes 655392 | tf_op jit(solution)/shard_map/all_to_all | solution.py:69
  94.0 0.8 copy-done.10
  94.8 3.7 %all-to-all-start.2 = ((bf16[16,400,128]{2,1,0:T(8,128)(2,1)}), bf16[16,400,128]{2,1,0:T(8,128)(2,1)S(1)}, u32[]{:S(2)}, u32[]{:S(2)}) async-start(bf16[16,400,128]{2,1,0:T(8,128)(2,1)} %add.59), calls=%async_computation.2 | async-start | bytes 3276800 | tf_op jit(solution)/shard_map/all_to_all | solution.py:69
  98.5 1.2 convert_reduce_fusion.1
  99.7 1.9 collective-permute-start.5
  101.7 3.1 %collective-permute-done.5 = f32[80,128]{1,0:T(8,128)S(1)} collective-permute-done((f32[80,128]{1,0:T(8,128)S(1)}, f32[80,128]{1,0:T(8,128)S(1)}, u32[]{:S(2)}, u32[]{:S(2)}) %collective-permute-start.5) | collective-permute-done | bytes 40992 | tf_op jit(solution)/shard_map/ppermute | solution.py:65
  104.8 6.7 %collective-permute-start.6 = (f32[80,128]{1,0:T(8,128)S(1)}, f32[80,128]{1,0:T(8,128)S(1)}, u32[]{:S(2)}, u32[]{:S(2)}) collective-permute-start(f32[80,128]{1,0:T(8,128)S(1)} %add.60), channel_id=1, source_target_pairs={{0,8},{1,9},{2,10},{3,11},{4,12},{5,13},{6,14},{7,15},{8,0},{9,1},... | collective-permute-start | bytes 122888 | tf_op jit(solution)/shard_map/ppermute | solution.py:65
  111.4 1.7 collective-permute-done.6
  113.1 4.9 %collective-permute-start.7 = (bf16[80,128]{1,0:T(8,128)(2,1)S(1)}, bf16[80,128]{1,0:T(8,128)(2,1)S(1)}, u32[]{:S(2)}, u32[]{:S(2)}) collective-permute-start(bf16[80,128]{1,0:T(8,128)(2,1)S(1)} %add_convert_fusion.2), channel_id=1, source_target_pairs={{0,16},{1,17},{2,18},{3,19},{4,20},{5,21},{6,22},{7,23},{8,24},{9,... | collective-permute-start | bytes 61448 | tf_op jit(solution)/shard_map/ppermute | solution.py:65
  118.0 3.6 %collective-permute-done.7 = bf16[80,128]{1,0:T(8,128)(2,1)S(1)} collective-permute-done((bf16[80,128]{1,0:T(8,128)(2,1)S(1)}, bf16[80,128]{1,0:T(8,128)(2,1)S(1)}, u32[]{:S(2)}, u32[]{:S(2)}) %collective-permute-start.7) | collective-permute-done | bytes 20512 | tf_op jit(solution)/shard_map/ppermute | solution.py:65
  122.8 1.4 broadcast_in_dim.34
  124.2 6.7 %all-to-all-start.3 = ((bf16[16,400,128]{2,1,0:T(8,128)(2,1)}), bf16[16,400,128]{2,1,0:T(8,128)(2,1)}, u32[]{:S(2)}, u32[]{:S(2)}) async-start(bf16[16,400,128]{2,1,0:T(8,128)(2,1)} %broadcast_in_dim.34), calls=%async_computation.3 | async-start | bytes 3276800 | tf_op jit(solution)/shard_map/all_to_all | solution.py:69
  130.9 12.4 %collective-permute-start.9 = (bf16[80,128]{1,0:T(8,128)(2,1)S(1)}, bf16[80,128]{1,0:T(8,128)(2,1)S(1)}, u32[]{:S(2)}, u32[]{:S(2)}) collective-permute-start(bf16[80,128]{1,0:T(8,128)(2,1)S(1)} %convert_add_fusion.2), channel_id=1, source_target_pairs={{0,256},{1,257},{2,258},{3,259},{4,260},{5,261},{6,262},{7,263},{8... | collective-permute-start | bytes 61448 | tf_op jit(solution)/shard_map/ppermute | solution.py:65
  143.3 4.5 %collective-permute-start.8 = (bf16[432,128]{1,0:T(8,128)(2,1)S(1)}, bf16[432,128]{1,0:T(8,128)(2,1)S(1)}, u32[]{:S(2)}, u32[]{:S(2)}) collective-permute-start(bf16[432,128]{1,0:T(8,128)(2,1)S(1)} %pad_maximum_fusion.1), channel_id=1, source_target_pairs={{0,16},{1,17},{2,18},{3,19},{64,80},{65,81},{66,82},{67,83},{128,1... | collective-permute-start | bytes 331784 | tf_op jit(solution)/shard_map/ppermute | solution.py:65
  147.9 2.8 collective-permute-done.8
  150.9 7.9 %collective-permute-start.10 = (bf16[16,400,128]{2,1,0:T(8,128)(2,1)}, bf16[16,400,128]{2,1,0:T(8,128)(2,1)}, u32[]{:S(2)}, u32[]{:S(2)}) collective-permute-start(bf16[16,400,128]{2,1,0:T(8,128)(2,1)} %all-to-all-done.3.half), channel_id=1, source_target_pairs={{0,32},{1,33},{2,34},{3,35},{4,36},{5,37},{6,38},{7,39},{8,40},{9,... | collective-permute-start | bytes 4915208 | tf_op jit(solution)/shard_map/ppermute | solution.py:65
  158.8 0.9 broadcast_in_dim.35
  159.7 6.3 %all-to-all-start.4 = ((bf16[32,80,128]{2,1,0:T(8,128)(2,1)}), bf16[32,80,128]{2,1,0:T(8,128)(2,1)S(1)}, u32[]{:S(2)}, u32[]{:S(2)}) async-start(bf16[32,80,128]{2,1,0:T(8,128)(2,1)} %broadcast_in_dim.35), calls=%async_computation.4 | async-start | bytes 1310720 | tf_op jit(solution)/shard_map/all_to_all | solution.py:69
  166.0 6.8 %collective-permute-start.11 = (f32[408,128]{1,0:T(8,128)S(1)}, f32[408,128]{1,0:T(8,128)S(1)}, u32[]{:S(2)}, u32[]{:S(2)}) collective-permute-start(f32[408,128]{1,0:T(8,128)S(1)} %copy-done.9), channel_id=1, source_target_pairs={{0,0},{1,1},{2,2},{3,3},{4,64},{5,65},{6,66},{7,67},{8,128},{9,129... | collective-permute-start | bytes 626696 | tf_op jit(solution)/shard_map/ppermute | solution.py:65
  172.8 5.5 %all-to-all-done.4 = bf16[32,80,128]{2,1,0:T(8,128)(2,1)S(1)} async-done(((bf16[32,80,128]{2,1,0:T(8,128)(2,1)}), bf16[32,80,128]{2,1,0:T(8,128)(2,1)S(1)}, u32[]{:S(2)}, u32[]{:S(2)}) %all-to-all-start.4) | async-done | bytes 655392 | tf_op jit(solution)/shard_map/all_to_all | solution.py:69
  178.3 1.3 copy-done.1
  179.6 0.9 relation_update.2
  180.5 1.0 copy-done.4
  181.6 17.2 %edge_blocks.3 = (bf16[16,400,128]{2,1,0:T(8,128)(2,1)S(1)}, bf16[16,400,128]{2,1,0:T(8,128)(2,1)}, f32[400,128]{1,0:T(8,128)S(1)}, bf16[2560,128]{1,0:T(8,128)(2,1)}) custom-call(s32[128]{0:T(128)S(1)} %slice_bitcast_fusion.4.scal, s32[1]{0:T(128)} %bitcast.14.here, s32[32,128]{1,0:T(8,128)S(1)} %slice_convert_fusion.lists, ...), custom_call_target="tpu_custom_call" | custom-call | flops 2000000000 | bytes 10000000 | tf_op jit(solution)/shard_map/edge_blocks/pallas_call | solution.py:181
  198.7 1.9 collective-permute-start.12
  200.7 11.0 %all-to-all-start.5 = ((bf16[32,80,128]{2,1,0:T(8,128)(2,1)}), bf16[32,80,128]{2,1,0:T(8,128)(2,1)S(1)}, u32[]{:S(2)}, u32[]{:S(2)}) async-start(bf16[32,80,128]{2,1,0:T(8,128)(2,1)} %bitcast.20), calls=%async_computation.5 | async-start | bytes 1310720 | tf_op jit(solution)/shard_map/all_to_all | solution.py:69
  211.7 3.0 %add.64 = bf16[16,400,128]{2,1,0:T(8,128)(2,1)} add(bf16[16,400,128]{2,1,0:T(8,128)(2,1)S(1)} %get-tuple-element.67, bf16[16,400,128]{2,1,0:T(8,128)(2,1)} %collective-permute-done.12) | non-fusion elementwise | flops 819200 | bytes 4915200 | tf_op jit(solution)/shard_map/add | solution.py:380
  214.8 3.8 %collective-permute-start.13 = (bf16[400,128]{1,0:T(8,128)(2,1)S(1)}, bf16[400,128]{1,0:T(8,128)(2,1)S(1)}, u32[]{:S(2)}, u32[]{:S(2)}) collective-permute-start(bf16[400,128]{1,0:T(8,128)(2,1)S(1)} %convert_element_type.75), channel_id=1, source_target_pairs={{16,0},{17,1},{18,2},{19,3},{80,64},{81,65},{82,66},{83,67},{144,1... | collective-permute-start | bytes 307208 | tf_op jit(solution)/shard_map/ppermute | solution.py:65
  218.5 5.5 %all-to-all-done.5 = bf16[32,80,128]{2,1,0:T(8,128)(2,1)S(1)} async-done(((bf16[32,80,128]{2,1,0:T(8,128)(2,1)}), bf16[32,80,128]{2,1,0:T(8,128)(2,1)S(1)}, u32[]{:S(2)}, u32[]{:S(2)}) %all-to-all-start.5) | async-done | bytes 655392 | tf_op jit(solution)/shard_map/all_to_all | solution.py:69
  224.0 5.2 %collective-permute-done.13.more = bf16[400,128]{1,0:T(8,128)(2,1)S(1)} collective-permute-done((bf16[400,128]{1,0:T(8,128)(2,1)S(1)}, bf16[400,128]{1,0:T(8,128)(2,1)S(1)}, u32[]{:S(2)}, u32[]{:S(2)}) %collective-permute-start.13) | collective-permute-done | bytes 102432 | tf_op jit(solution)/shard_map/ppermute | solution.py:65
  229.8 6.6 %all-to-all-start.6 = ((bf16[16,400,128]{2,1,0:T(8,128)(2,1)}), bf16[16,400,128]{2,1,0:T(8,128)(2,1)S(1)}, u32[]{:S(2)}, u32[]{:S(2)}) async-start(bf16[16,400,128]{2,1,0:T(8,128)(2,1)} %add.64), calls=%async_computation.6 | async-start | bytes 3276800 | tf_op jit(solution)/shard_map/all_to_all | solution.py:69
  236.5 1.9 collective-permute-start.14
  238.4 2.8 collective-permute-done.14
  241.3 1.9 collective-permute-start.15
  243.2 4.5 %collective-permute-done.15 = f32[80,128]{1,0:T(8,128)S(1)} collective-permute-done((f32[80,128]{1,0:T(8,128)S(1)}, f32[80,128]{1,0:T(8,128)S(1)}, u32[]{:S(2)}, u32[]{:S(2)}) %collective-permute-start.15) | collective-permute-done | bytes 40992 | tf_op jit(solution)/shard_map/ppermute | solution.py:65
  247.6 1.9 collective-permute-start.16
  249.6 6.5 %collective-permute-done.16 = bf16[80,128]{1,0:T(8,128)(2,1)S(1)} collective-permute-done((bf16[80,128]{1,0:T(8,128)(2,1)S(1)}, bf16[80,128]{1,0:T(8,128)(2,1)S(1)}, u32[]{:S(2)}, u32[]{:S(2)}) %collective-permute-start.16) | collective-permute-done | bytes 20512 | tf_op jit(solution)/shard_map/ppermute | solution.py:65
  256.1 5.7 %collective-permute-start.17 = (bf16[80,128]{1,0:T(8,128)(2,1)S(1)}, bf16[80,128]{1,0:T(8,128)(2,1)S(1)}, u32[]{:S(2)}, u32[]{:S(2)}) collective-permute-start(bf16[80,128]{1,0:T(8,128)(2,1)S(1)} %add_convert_fusion), channel_id=1, source_target_pairs={{0,256},{1,257},{2,258},{3,259},{4,260},{5,261},{6,262},{7,263},{8... | collective-permute-start | bytes 61448 | tf_op jit(solution)/shard_map/ppermute | solution.py:65
  261.8 7.5 %collective-permute-done.17 = bf16[80,128]{1,0:T(8,128)(2,1)S(1)} collective-permute-done((bf16[80,128]{1,0:T(8,128)(2,1)S(1)}, bf16[80,128]{1,0:T(8,128)(2,1)S(1)}, u32[]{:S(2)}, u32[]{:S(2)}) %collective-permute-start.17) | collective-permute-done | bytes 20512 | tf_op jit(solution)/shard_map/ppermute | solution.py:65
  269.4 0.9 broadcast_in_dim.36
  270.3 12.7 %all-to-all-start.7 = ((bf16[32,80,128]{2,1,0:T(8,128)(2,1)}), bf16[32,80,128]{2,1,0:T(8,128)(2,1)S(1)}, u32[]{:S(2)}, u32[]{:S(2)}) async-start(bf16[32,80,128]{2,1,0:T(8,128)(2,1)} %broadcast_in_dim.36), calls=%async_computation.7 | async-start | bytes 1310720 | tf_op jit(solution)/shard_map/all_to_all | solution.py:69
  283.0 0.9 copy-done.7
  284.4 1.9 collective-permute-start.18
  286.3 8.1 %collective-permute-done.18.grads = bf16[400,128]{1,0:T(8,128)(2,1)S(1)} collective-permute-done((bf16[400,128]{1,0:T(8,128)(2,1)S(1)}, bf16[400,128]{1,0:T(8,128)(2,1)S(1)}, u32[]{:S(2)}, u32[]{:S(2)}) %collective-permute-start.18) | collective-permute-done | bytes 102432 | tf_op jit(solution)/shard_map/ppermute | solution.py:65
  295.1 1.8 last_update.1
  296.9 1.3 copy-done.5
  298.2 2.4 relation_update.3
  (80 shorter events, 8.3 us)
Async XLA Ops:
  1.6 14.1 %collective-permute-start = (bf16[400,128]{1,0:T(8,128)(2,1)S(1)}, bf16[400,128]{1,0:T(8,128)(2,1)S(1)}, u32[]{:S(2)}, u32[]{:S(2)}) collective-permute-start(bf16[400,128]{1,0:T(8,128)(2,1)S(1)} %bitcast_convert_fusion), channel_id=1, source_target_pairs={{0,0},{1,1},{2,2},{3,3},{4,64},{5,65},{6,66},{7,67},{8,128},{9,129... | collective-permute-start | bytes 307208 | tf_op jit(solution)/shard_map/ppermute | solution.py:65
  17.8 10.5 %copy-start.16 = (f32[128]{0:T(128)S(1)}, f32[128]{0:T(128)}, u32[]{:S(2)}) copy-start(f32[128]{0:T(128)} %param.11) | copy-start | bytes 1540
  17.8 10.5 %copy-start.11 = (f32[128,400]{0,1:T(8,128)S(1)}, f32[128,400]{0,1:T(8,128)}, u32[]{:S(2)}) copy-start(f32[128,400]{0,1:T(8,128)} %param.10) | copy-start | bytes 614404
  17.8 18.0 %copy-start.14 = (s32[2,10,128]{2,0,1:T(2,128)S(1)}, s32[2,10,128]{2,0,1:T(2,128)}, u32[]{:S(2)}) copy-start(s32[2,10,128]{2,0,1:T(2,128)} %param.18) | copy-start | bytes 30724
  17.8 18.0 %copy-start.15 = (s32[2,10,128]{2,0,1:T(2,128)S(1)}, s32[2,10,128]{2,0,1:T(2,128)}, u32[]{:S(2)}) copy-start(s32[2,10,128]{2,0,1:T(2,128)} %param.17) | copy-start | bytes 30724
  17.8 31.9 %all-to-all-start = ((bf16[16,400,128]{2,1,0:T(8,128)(2,1)}), bf16[16,400,128]{2,1,0:T(8,128)(2,1)S(1)}, u32[]{:S(2)}, u32[]{:S(2)}) async-start(bf16[16,400,128]{2,1,0:T(8,128)(2,1)} %broadcast_in_dim.29), calls=%async_computation | async-start | bytes 3276800 | tf_op jit(solution)/shard_map/all_to_all | solution.py:69
  28.3 21.2 %collective-permute-start.2 = (f32[408,128]{1,0:T(8,128)S(1)}, f32[408,128]{1,0:T(8,128)S(1)}, u32[]{:S(2)}, u32[]{:S(2)}) collective-permute-start(f32[408,128]{1,0:T(8,128)S(1)} %pad_maximum_fusion), channel_id=1, source_target_pairs={{0,0},{1,1},{2,2},{3,3},{4,64},{5,65},{6,66},{7,67},{8,128},{9,129... | collective-permute-start | bytes 626696 | tf_op jit(solution)/shard_map/ppermute | solution.py:65
  35.9 13.6 %collective-permute-start.1 = (bf16[64,128]{1,0:T(8,128)(2,1)S(1)}, bf16[64,128]{1,0:T(8,128)(2,1)S(1)}, u32[]{:S(2)}, u32[]{:S(2)}) collective-permute-start(bf16[64,128]{1,0:T(8,128)(2,1)S(1)} %pad_maximum_fusion.2), channel_id=1, source_target_pairs={{0,0},{1,1},{2,2},{3,3},{4,64},{5,65},{6,66},{7,67},{8,128},{9,129... | collective-permute-start | bytes 49160 | tf_op jit(solution)/shard_map/ppermute | solution.py:65
  49.7 5.5 %collective-permute-start.3 = (bf16[16,400,128]{2,1,0:T(8,128)(2,1)S(1)}, bf16[16,400,128]{2,1,0:T(8,128)(2,1)}, u32[]{:S(2)}, u32[]{:S(2)}) collective-permute-start(bf16[16,400,128]{2,1,0:T(8,128)(2,1)S(1)} %all-to-all-done.half), channel_id=1, source_target_pairs={{0,32},{1,33},{2,34},{3,35},{4,36},{5,37},{6,38},{7,39},{8,40},{9,... | collective-permute-start | bytes 4915208 | tf_op jit(solution)/shard_map/ppermute | solution.py:65
  61.7 1.2 copy-start
  62.9 18.8 %collective-permute-start.4 = (bf16[16,400,128]{2,1,0:T(8,128)(2,1)}, bf16[16,400,128]{2,1,0:T(8,128)(2,1)}, u32[]{:S(2)}, u32[]{:S(2)}) collective-permute-start(bf16[16,400,128]{2,1,0:T(8,128)(2,1)} %get-tuple-element.52), channel_id=1, source_target_pairs={{0,32},{1,33},{2,34},{3,35},{4,36},{5,37},{6,38},{7,39},{8,40},{9,... | collective-permute-start | bytes 4915208 | tf_op jit(solution)/shard_map/ppermute | solution.py:65
  68.7 25.2 %all-to-all-start.1 = ((bf16[32,80,128]{2,1,0:T(8,128)(2,1)}), bf16[32,80,128]{2,1,0:T(8,128)(2,1)S(1)}, u32[]{:S(2)}, u32[]{:S(2)}) async-start(bf16[32,80,128]{2,1,0:T(8,128)(2,1)} %bitcast.16), calls=%async_computation.1 | async-start | bytes 1310720 | tf_op jit(solution)/shard_map/all_to_all | solution.py:69
  94.0 0.8 copy-start.10
  94.8 26.8 %all-to-all-start.2 = ((bf16[16,400,128]{2,1,0:T(8,128)(2,1)}), bf16[16,400,128]{2,1,0:T(8,128)(2,1)S(1)}, u32[]{:S(2)}, u32[]{:S(2)}) async-start(bf16[16,400,128]{2,1,0:T(8,128)(2,1)} %add.59), calls=%async_computation.2 | async-start | bytes 3276800 | tf_op jit(solution)/shard_map/all_to_all | solution.py:69
  99.7 5.0 %collective-permute-start.5 = (f32[80,128]{1,0:T(8,128)S(1)}, f32[80,128]{1,0:T(8,128)S(1)}, u32[]{:S(2)}, u32[]{:S(2)}) collective-permute-start(f32[80,128]{1,0:T(8,128)S(1)} %convert_reduce_fusion.1), channel_id=1, source_target_pairs={{0,4},{1,5},{2,6},{3,7},{4,0},{5,1},{6,2},{7,3},{8,12},{9,13},{10,... | collective-permute-start | bytes 122888 | tf_op jit(solution)/shard_map/ppermute | solution.py:65
  104.8 8.3 %collective-permute-start.6 = (f32[80,128]{1,0:T(8,128)S(1)}, f32[80,128]{1,0:T(8,128)S(1)}, u32[]{:S(2)}, u32[]{:S(2)}) collective-permute-start(f32[80,128]{1,0:T(8,128)S(1)} %add.60), channel_id=1, source_target_pairs={{0,8},{1,9},{2,10},{3,11},{4,12},{5,13},{6,14},{7,15},{8,0},{9,1},... | collective-permute-start | bytes 122888 | tf_op jit(solution)/shard_map/ppermute | solution.py:65
  113.1 8.4 %collective-permute-start.7 = (bf16[80,128]{1,0:T(8,128)(2,1)S(1)}, bf16[80,128]{1,0:T(8,128)(2,1)S(1)}, u32[]{:S(2)}, u32[]{:S(2)}) collective-permute-start(bf16[80,128]{1,0:T(8,128)(2,1)S(1)} %add_convert_fusion.2), channel_id=1, source_target_pairs={{0,16},{1,17},{2,18},{3,19},{4,20},{5,21},{6,22},{7,23},{8,24},{9,... | collective-permute-start | bytes 61448 | tf_op jit(solution)/shard_map/ppermute | solution.py:65
  122.2 0.7 copy-start.8
  124.2 26.7 %all-to-all-start.3 = ((bf16[16,400,128]{2,1,0:T(8,128)(2,1)}), bf16[16,400,128]{2,1,0:T(8,128)(2,1)}, u32[]{:S(2)}, u32[]{:S(2)}) async-start(bf16[16,400,128]{2,1,0:T(8,128)(2,1)} %broadcast_in_dim.34), calls=%async_computation.3 | async-start | bytes 3276800 | tf_op jit(solution)/shard_map/all_to_all | solution.py:69
  130.9 35.1 %copy-start.9 = (f32[408,128]{1,0:T(8,128)S(1)}, f32[408,128]{1,0:T(8,128)}, u32[]{:S(2)}) copy-start(f32[408,128]{1,0:T(8,128)} %copy-done.8) | copy-start | bytes 626692
  130.9 16.9 %collective-permute-start.9 = (bf16[80,128]{1,0:T(8,128)(2,1)S(1)}, bf16[80,128]{1,0:T(8,128)(2,1)S(1)}, u32[]{:S(2)}, u32[]{:S(2)}) collective-permute-start(bf16[80,128]{1,0:T(8,128)(2,1)S(1)} %convert_add_fusion.2), channel_id=1, source_target_pairs={{0,256},{1,257},{2,258},{3,259},{4,260},{5,261},{6,262},{7,263},{8... | collective-permute-start | bytes 61448 | tf_op jit(solution)/shard_map/ppermute | solution.py:65
  143.3 7.3 %collective-permute-start.8 = (bf16[432,128]{1,0:T(8,128)(2,1)S(1)}, bf16[432,128]{1,0:T(8,128)(2,1)S(1)}, u32[]{:S(2)}, u32[]{:S(2)}) collective-permute-start(bf16[432,128]{1,0:T(8,128)(2,1)S(1)} %pad_maximum_fusion.1), channel_id=1, source_target_pairs={{0,16},{1,17},{2,18},{3,19},{64,80},{65,81},{66,82},{67,83},{128,1... | collective-permute-start | bytes 331784 | tf_op jit(solution)/shard_map/ppermute | solution.py:65
  150.9 30.7 %collective-permute-start.10 = (bf16[16,400,128]{2,1,0:T(8,128)(2,1)}, bf16[16,400,128]{2,1,0:T(8,128)(2,1)}, u32[]{:S(2)}, u32[]{:S(2)}) collective-permute-start(bf16[16,400,128]{2,1,0:T(8,128)(2,1)} %all-to-all-done.3.half), channel_id=1, source_target_pairs={{0,32},{1,33},{2,34},{3,35},{4,36},{5,37},{6,38},{7,39},{8,40},{9,... | collective-permute-start | bytes 4915208 | tf_op jit(solution)/shard_map/ppermute | solution.py:65
  159.7 18.6 %all-to-all-start.4 = ((bf16[32,80,128]{2,1,0:T(8,128)(2,1)}), bf16[32,80,128]{2,1,0:T(8,128)(2,1)S(1)}, u32[]{:S(2)}, u32[]{:S(2)}) async-start(bf16[32,80,128]{2,1,0:T(8,128)(2,1)} %broadcast_in_dim.35), calls=%async_computation.4 | async-start | bytes 1310720 | tf_op jit(solution)/shard_map/all_to_all | solution.py:69
  166.0 15.6 %collective-permute-start.11 = (f32[408,128]{1,0:T(8,128)S(1)}, f32[408,128]{1,0:T(8,128)S(1)}, u32[]{:S(2)}, u32[]{:S(2)}) collective-permute-start(f32[408,128]{1,0:T(8,128)S(1)} %copy-done.9), channel_id=1, source_target_pairs={{0,0},{1,1},{2,2},{3,3},{4,64},{5,65},{6,66},{7,67},{8,128},{9,129... | collective-permute-start | bytes 626696 | tf_op jit(solution)/shard_map/ppermute | solution.py:65
  178.3 1.3 copy-start.1
  180.5 1.0 copy-start.4
  181.5 17.2 %copy-start.2 = (f32[400,768]{1,0:T(8,128)}, f32[400,768]{1,0:T(8,128)S(1)}, u32[]{:S(2)}) copy-start(f32[400,768]{1,0:T(8,128)S(1)} %get-tuple-element.63.rel) | copy-start | bytes 3686404
  181.5 17.2 %copy-start.12 = (f32[408,128]{1,0:T(8,128)}, f32[408,128]{1,0:T(8,128)S(1)}, u32[]{:S(2)}) copy-start(f32[408,128]{1,0:T(8,128)S(1)} %collective-permute-done.11.kept) | copy-start | bytes 626692
  198.7 13.0 %collective-permute-start.12 = (bf16[16,400,128]{2,1,0:T(8,128)(2,1)}, bf16[16,400,128]{2,1,0:T(8,128)(2,1)}, u32[]{:S(2)}, u32[]{:S(2)}) collective-permute-start(bf16[16,400,128]{2,1,0:T(8,128)(2,1)} %get-tuple-element.68), channel_id=1, source_target_pairs={{0,32},{1,33},{2,34},{3,35},{4,36},{5,37},{6,38},{7,39},{8,40},{9,... | collective-permute-start | bytes 4915208 | tf_op jit(solution)/shard_map/ppermute | solution.py:65
  200.7 23.3 %all-to-all-start.5 = ((bf16[32,80,128]{2,1,0:T(8,128)(2,1)}), bf16[32,80,128]{2,1,0:T(8,128)(2,1)S(1)}, u32[]{:S(2)}, u32[]{:S(2)}) async-start(bf16[32,80,128]{2,1,0:T(8,128)(2,1)} %bitcast.20), calls=%async_computation.5 | async-start | bytes 1310720 | tf_op jit(solution)/shard_map/all_to_all | solution.py:69
  214.8 14.4 %collective-permute-start.13 = (bf16[400,128]{1,0:T(8,128)(2,1)S(1)}, bf16[400,128]{1,0:T(8,128)(2,1)S(1)}, u32[]{:S(2)}, u32[]{:S(2)}) collective-permute-start(bf16[400,128]{1,0:T(8,128)(2,1)S(1)} %convert_element_type.75), channel_id=1, source_target_pairs={{16,0},{17,1},{18,2},{19,3},{80,64},{81,65},{82,66},{83,67},{144,1... | collective-permute-start | bytes 307208 | tf_op jit(solution)/shard_map/ppermute | solution.py:65
  229.2 0.6 copy-start.6
  229.8 39.5 %all-to-all-start.6 = ((bf16[16,400,128]{2,1,0:T(8,128)(2,1)}), bf16[16,400,128]{2,1,0:T(8,128)(2,1)S(1)}, u32[]{:S(2)}, u32[]{:S(2)}) async-start(bf16[16,400,128]{2,1,0:T(8,128)(2,1)} %add.64), calls=%async_computation.6 | async-start | bytes 3276800 | tf_op jit(solution)/shard_map/all_to_all | solution.py:69
  236.5 4.7 %collective-permute-start.14 = (f32[80,128]{1,0:T(8,128)S(1)}, f32[80,128]{1,0:T(8,128)S(1)}, u32[]{:S(2)}, u32[]{:S(2)}) collective-permute-start(f32[80,128]{1,0:T(8,128)S(1)} %convert_reduce_fusion), channel_id=1, source_target_pairs={{0,4},{1,5},{2,6},{3,7},{4,0},{5,1},{6,2},{7,3},{8,12},{9,13},{10,... | collective-permute-start | bytes 122888 | tf_op jit(solution)/shard_map/ppermute | solution.py:65
  241.3 6.4 %collective-permute-start.15 = (f32[80,128]{1,0:T(8,128)S(1)}, f32[80,128]{1,0:T(8,128)S(1)}, u32[]{:S(2)}, u32[]{:S(2)}) collective-permute-start(f32[80,128]{1,0:T(8,128)S(1)} %add.65), channel_id=1, source_target_pairs={{0,8},{1,9},{2,10},{3,11},{4,12},{5,13},{6,14},{7,15},{8,0},{9,1},... | collective-permute-start | bytes 122888 | tf_op jit(solution)/shard_map/ppermute | solution.py:65
  247.6 8.4 %collective-permute-start.16 = (bf16[80,128]{1,0:T(8,128)(2,1)S(1)}, bf16[80,128]{1,0:T(8,128)(2,1)S(1)}, u32[]{:S(2)}, u32[]{:S(2)}) collective-permute-start(bf16[80,128]{1,0:T(8,128)(2,1)S(1)} %add_convert_fusion.1), channel_id=1, source_target_pairs={{0,16},{1,17},{2,18},{3,19},{4,20},{5,21},{6,22},{7,23},{8,24},{9,... | collective-permute-start | bytes 61448 | tf_op jit(solution)/shard_map/ppermute | solution.py:65
  256.1 13.2 %collective-permute-start.17 = (bf16[80,128]{1,0:T(8,128)(2,1)S(1)}, bf16[80,128]{1,0:T(8,128)(2,1)S(1)}, u32[]{:S(2)}, u32[]{:S(2)}) collective-permute-start(bf16[80,128]{1,0:T(8,128)(2,1)S(1)} %add_convert_fusion), channel_id=1, source_target_pairs={{0,256},{1,257},{2,258},{3,259},{4,260},{5,261},{6,262},{7,263},{8... | collective-permute-start | bytes 61448 | tf_op jit(solution)/shard_map/ppermute | solution.py:65
  270.3 26.6 %copy-start.3 = (f32[400,768]{1,0:T(8,128)S(1)}, f32[400,768]{1,0:T(8,128)}, u32[]{:S(2)}) copy-start(f32[400,768]{1,0:T(8,128)} %copy-done.2) | copy-start | bytes 3686404
  270.3 26.6 %all-to-all-start.7 = ((bf16[32,80,128]{2,1,0:T(8,128)(2,1)}), bf16[32,80,128]{2,1,0:T(8,128)(2,1)S(1)}, u32[]{:S(2)}, u32[]{:S(2)}) async-start(bf16[32,80,128]{2,1,0:T(8,128)(2,1)} %broadcast_in_dim.36), calls=%async_computation.7 | async-start | bytes 1310720 | tf_op jit(solution)/shard_map/all_to_all | solution.py:69
  283.0 0.9 copy-start.7
  284.4 10.1 %collective-permute-start.18 = (bf16[400,128]{1,0:T(8,128)(2,1)S(1)}, bf16[400,128]{1,0:T(8,128)(2,1)S(1)}, u32[]{:S(2)}, u32[]{:S(2)}) collective-permute-start(bf16[400,128]{1,0:T(8,128)(2,1)S(1)} %fold_pieces.1), channel_id=1, source_target_pairs={{0,0},{1,1},{2,2},{3,3},{4,64},{5,65},{6,66},{7,67},{8,128},{9,129... | collective-permute-start | bytes 307208 | tf_op jit(solution)/shard_map/ppermute | solution.py:65
  294.5 0.6 copy-start.13
  296.9 1.3 copy-start.5

commit v4 on v3

--- a/solution.py
+++ b/solution.py
@@ -111,45 +111,64 @@
     def near(b):
         return ((b >> 4) ^ here[0]) * 16 + (b & 15)
 
-    rows = lax.broadcasted_iota(jnp.int32, (block, block), 0)
-    lanes = lax.broadcasted_iota(jnp.int32, (block, block), 1)
-
-    def step(j, carry):
-        src_hot = jnp.where(rows == lists[pl.ds(j, 1), :], 1.0, 0.0).astype(BF16)
-        tgt_hot = jnp.where(rows == lists[pl.ds(slots + j, 1), :], 1.0, 0.0).astype(BF16)
-        dst, rel_id = near(scal[j]), scal[slots + j] * DIGIT + scal[2 * slots + j]
-        negs = [near(scal[3 * slots + 4 * j + i]) for i in range(4)]
-        rel_tile = pl.ds(pl.multiple_of((rel_id >> 7) * 128, 128), 128)
-        rel_row = jnp.where(rows == (rel_id & 127), 1.0, 0.0).astype(BF16)
-        rel_lane = jnp.where(lanes == (rel_id & 127), 1.0, 0.0).astype(BF16)
+    both = 2 * block
+    rows = lax.broadcasted_iota(jnp.int32, (both, both), 0)
+    lanes = lax.broadcasted_iota(jnp.int32, (both, both), 1)
+    count = scal[7 * slots]
+
+    def hot(match):
+        return jnp.where(match, 1.0, 0.0).astype(BF16)
+
+    def step(i, carry):
+        pair = (2 * i, 2 * i + 1)
+        live = (1.0, jnp.where(pair[1] < count, 1.0, 0.0))
+        sources = jnp.concatenate([lists[pl.ds(j, 1), :] for j in pair], 1)
+        targets = jnp.concatenate([lists[pl.ds(slots + j, 1), :] + block * s for s, j in enumerate(pair)], 1)
+        src_hot = hot(rows[:block] == sources)
+        tgt_hot = hot(rows == targets)
+        dsts = [near(scal[j]) for j in pair]
+        rel_ids = [scal[slots + j] * DIGIT + scal[2 * slots + j] for j in pair]
+        rel_lanes = [rel_id & (block - 1) for rel_id in rel_ids]
+        rel_tiles = [pl.ds(pl.multiple_of((rel_id >> 7) * block, block), block) for rel_id in rel_ids]
+        rel_hot = hot(lanes == jnp.where(rows < block, rel_lanes[0], rel_lanes[1] + block))
         heads = nn(own[...], src_hot)
-        tails = nn(table[dst], tgt_hot)
-        rel_value = rel[:, rel_tile]
-        high = rel_value.astype(BF16)
-        low = (rel_value - high.astype(F32)).astype(BF16)
-        op = nn(high, rel_row) + nn(low, rel_row)
+        tails = nn(jnp.concatenate([table[dst] for dst in dsts], 1), tgt_hot)
+        columns = [
+            pltpu.roll(rel[:, tile], (block - lane) & (block - 1), 1)[:, :1]
+            for tile, lane in zip(rel_tiles, rel_lanes)
+        ]
+        op = jnp.concatenate([jnp.broadcast_to(column, (width, block)) for column in columns], 1)
         h_re, h_im = heads[:mid], heads[mid:]
         r_re, r_im = op[:mid], op[mid:]
         query = jnp.concatenate([h_re * r_re - h_im * r_im, h_re * r_im + h_im * r_re], 0).astype(BF16)
         query_f = query.astype(F32)
+        query_t = query_f.T.astype(BF16)
         positive = jnp.sum(query_f * tails, 0, keepdims=True)
-        neg_rows = jnp.concatenate([table[n] for n in negs], 1)
-        scores = nn(query_f.T.astype(BF16), neg_rows)
-        pos_weight = -jax.nn.sigmoid(-positive)
-        neg_weight = (jax.nn.sigmoid(scores) * (1.0 / scores.shape[1])).astype(BF16)
-        grad_query = pos_weight * tails + nt(neg_rows, neg_weight)
-        neg_add = nn(query, neg_weight)
-        for i, n in enumerate(negs):
-            acc[n] += neg_add[:, block * i : block * (i + 1)]
-        acc[dst] += nt((pos_weight * query_f).astype(BF16), tgt_hot)
+        live_lanes = jnp.where(lanes[:1] < block, live[0], live[1])
+        pos_weight = -jax.nn.sigmoid(-positive) * live_lanes
+        neg_grads = []
+        for s, j in enumerate(pair):
+            negs = [near(scal[3 * slots + 4 * j + n]) for n in range(4)]
+            neg_rows = jnp.concatenate([table[n] for n in negs], 1)
+            scores = nn(query_t[block * s : block * (s + 1)], neg_rows)
+            neg_weight = (jax.nn.sigmoid(scores) * (live[s] / scores.shape[1])).astype(BF16)
+            neg_grads.append(nt(neg_rows, neg_weight))
+            neg_add = nn(query[:, block * s : block * (s + 1)], neg_weight)
+            for t, n in enumerate(negs):
+                acc[n] += neg_add[:, block * t : block * (t + 1)]
+        grad_query = pos_weight * tails + jnp.concatenate(neg_grads, 1)
+        tgt_add = nt((pos_weight * query_f).astype(BF16), tgt_hot)
         g_re, g_im = grad_query[:mid], grad_query[mid:]
         head_grad = jnp.concatenate([g_re * r_re + g_im * r_im, g_im * r_re - g_re * r_im], 0)
         lhs_out[...] += nt(head_grad.astype(BF16), src_hot)
         op_grad = jnp.concatenate([g_re * h_re + g_im * h_im, g_im * h_re - g_re * h_im], 0)
-        rel_acc[:, rel_tile] += nn(op_grad.astype(BF16), rel_lane)
+        rel_add = nn(op_grad.astype(BF16), rel_hot)
+        for s in range(2):
+            acc[dsts[s]] += tgt_add[:, block * s : block * (s + 1)]
+            rel_acc[:, rel_tiles[s]] += rel_add[:, block * s : block * (s + 1)]
         return carry
 
-    lax.fori_loop(0, scal[7 * slots], step, 0)
+    lax.fori_loop(0, (count + 1) >> 1, step, 0)
 
     def pack(k, carry):
         mine_out[k] = acc[k].astype(BF16)
@@ -378,8 +397,10 @@
     mine, theirs, lhs, rel_part = run_blocks(now, here, source[:width], rel, half, other)
     rel_pieces = exchange(rel_part.reshape(32, PIECE, block), PLANES)
     summed, lhs = together(mine + send(theirs, OTHER), lhs.astype(BF16))
-    summed, rel_pieces, lhs = together(summed, rel_pieces, send(lhs, PREVIOUS))
-    rel_mine = z_step(z_steps(rel_pieces), 8, BF16)
+    summed, rel_pieces = together(summed, rel_pieces)
+    rel_mine = jnp.sum(rel_pieces, 0, dtype=F32)
+    rel_mine, lhs = together(z_step(z_step(rel_mine, 1, F32), 2, F32), send(lhs, PREVIOUS))
+    rel_mine = z_step(z_step(rel_mine, 4, BF16), 8, BF16)
     pieces, rel_mine = together(exchange(summed, SHEETS), rel_mine)
     grads = send(fold(pieces, lhs), TURN)
     rel_sum = spread_relations(rel_mine)

time: 306 us -> 299 us (0.977)
  the two profiles are of different devices: /device:TPU:1 before, /device:TPU:17 now
where the time goes in v4:
time: 299 us; the launch traced here: 297 us
  starting transfers between devices  164 us (55%)
  waiting for transfers between devices  79.4 us (27%)
  Pallas kernels  22.5 us (8%)
  local copies, waits for them, and re-layouts  17 us (6%)
  other arithmetic  12.6 us (4%)
    ppermute x19, starting transfers between devices, send(): return lax.ppermute(value, AXES, pairs)  102 us
    all_to_all x8, starting transfers between devices, exchange(): lax.all_to_all(value, AXES, 0, 0, axis_index_groups=groups, tiled=True)  62.8 us
    ppermute x19, waiting for transfers between devices, send(): return lax.ppermute(value, AXES, pairs)  57.8 us
    all_to_all x8, waiting for transfers between devices, exchange(): lax.all_to_all(value, AXES, 0, 0, axis_index_groups=groups, tiled=True)  21.5 us
    pallas_call x2, Pallas kernels, run_blocks(): pl.pallas_call(blocks_kernel, out_shape=(jax.ShapeDtypeStruct((16, width,...  16.4 us
    unnamed x34, local copies, waits for them, and re-layouts  8.46 us
  transfers between devices with their start and end apart: 27, of which 15 were waited for; matrix products, arithmetic and copies ran while one was open for 5% of the time, Pallas kernels for 1%

profile of v4, /device:TPU:17, one launch (start us, length us, event | category | flops | bytes accessed | tf_op | source)
XLA Modules:
  0.0 297.0 jit_solution(13246354894162569847)
XLA Ops:
  0.6 0.9 bitcast_convert_fusion
  1.6 11.9 %collective-permute-start = (bf16[400,128]{1,0:T(8,128)(2,1)S(1)}, bf16[400,128]{1,0:T(8,128)(2,1)S(1)}, u32[]{:S(2)}, u32[]{:S(2)}) collective-permute-start(bf16[400,128]{1,0:T(8,128)(2,1)S(1)} %bitcast_convert_fusion), channel_id=1, source_target_pairs={{0,0},{1,1},{2,2},{3,3},{4,64},{5,65},{6,66},{7,67},{8,128},{9,129... | collective-permute-start | bytes 307208 | tf_op jit(solution)/shard_map/ppermute | solution.py:65
  14.8 0.8 fusion.10
  16.0 0.8 fusion.12
  18.0 1.4 broadcast_in_dim.29
  19.5 7.9 %all-to-all-start = ((bf16[16,400,128]{2,1,0:T(8,128)(2,1)}), bf16[16,400,128]{2,1,0:T(8,128)(2,1)S(1)}, u32[]{:S(2)}, u32[]{:S(2)}) async-start(bf16[16,400,128]{2,1,0:T(8,128)(2,1)} %broadcast_in_dim.29), calls=%async_computation | async-start | bytes 3276800 | tf_op jit(solution)/shard_map/all_to_all | solution.py:69
  27.4 8.4 %collective-permute-start.2 = (f32[408,128]{1,0:T(8,128)S(1)}, f32[408,128]{1,0:T(8,128)S(1)}, u32[]{:S(2)}, u32[]{:S(2)}) collective-permute-start(f32[408,128]{1,0:T(8,128)S(1)} %pad_maximum_fusion), channel_id=1, source_target_pairs={{0,0},{1,1},{2,2},{3,3},{4,64},{5,65},{6,66},{7,67},{8,128},{9,129... | collective-permute-start | bytes 626696 | tf_op jit(solution)/shard_map/ppermute | solution.py:65
  37.4 5.3 %collective-permute-start.1 = (bf16[64,128]{1,0:T(8,128)(2,1)S(1)}, bf16[64,128]{1,0:T(8,128)(2,1)S(1)}, u32[]{:S(2)}, u32[]{:S(2)}) collective-permute-start(bf16[64,128]{1,0:T(8,128)(2,1)S(1)} %pad_maximum_fusion.2), channel_id=1, source_target_pairs={{0,0},{1,1},{2,2},{3,3},{4,64},{5,65},{6,66},{7,67},{8,128},{9,129... | collective-permute-start | bytes 49160 | tf_op jit(solution)/shard_map/ppermute | solution.py:65
  42.7 9.4 %collective-permute-done.1 = bf16[64,128]{1,0:T(8,128)(2,1)S(1)} collective-permute-done((bf16[64,128]{1,0:T(8,128)(2,1)S(1)}, bf16[64,128]{1,0:T(8,128)(2,1)S(1)}, u32[]{:S(2)}, u32[]{:S(2)}) %collective-permute-start.1) | collective-permute-done | bytes 16416 | tf_op jit(solution)/shard_map/ppermute | solution.py:65
  52.1 4.3 %collective-permute-start.3 = (bf16[16,400,128]{2,1,0:T(8,128)(2,1)S(1)}, bf16[16,400,128]{2,1,0:T(8,128)(2,1)}, u32[]{:S(2)}, u32[]{:S(2)}) collective-permute-start(bf16[16,400,128]{2,1,0:T(8,128)(2,1)S(1)} %all-to-all-done.half), channel_id=1, source_target_pairs={{0,32},{1,33},{2,34},{3,35},{4,36},{5,37},{6,38},{7,39},{8,40},{9,... | collective-permute-start | bytes 4915208 | tf_op jit(solution)/shard_map/ppermute | solution.py:65
  56.4 1.4 pad.26.rel
  57.8 1.8 collective-permute-done.3.other
  59.7 7.2 %edge_blocks.2 = (bf16[16,400,128]{2,1,0:T(8,128)(2,1)S(1)}, bf16[16,400,128]{2,1,0:T(8,128)(2,1)}, f32[400,128]{1,0:T(8,128)S(1)}, bf16[2560,128]{1,0:T(8,128)(2,1)}) custom-call(s32[128]{0:T(128)S(1)} %slice_bitcast_fusion.5.scal, s32[1]{0:T(128)} %bitcast.14.here, s32[32,128]{1,0:T(8,128)S(1)} %get-tuple-element.91.lists, ...), custom_call_target="tpu_custom_call" | custom-call | flops 2000000000 | bytes 10000000 | tf_op jit(solution)/shard_map/edge_blocks/pallas_call | solution.py:200
  66.9 1.1 copy-done
  68.1 2.2 collective-permute-start.4
  70.3 9.4 %all-to-all-start.1 = ((bf16[32,80,128]{2,1,0:T(8,128)(2,1)}), bf16[32,80,128]{2,1,0:T(8,128)(2,1)S(1)}, u32[]{:S(2)}, u32[]{:S(2)}) async-start(bf16[32,80,128]{2,1,0:T(8,128)(2,1)} %bitcast.16), calls=%async_computation.1 | async-start | bytes 1310720 | tf_op jit(solution)/shard_map/all_to_all | solution.py:69
  79.8 3.6 %add.59 = bf16[16,400,128]{2,1,0:T(8,128)(2,1)} add(bf16[16,400,128]{2,1,0:T(8,128)(2,1)} %copy-done, bf16[16,400,128]{2,1,0:T(8,128)(2,1)} %collective-permute-done.4) | non-fusion elementwise | flops 819200 | bytes 4915200 | tf_op jit(solution)/shard_map/add | solution.py:386
  83.3 7.0 %all-to-all-done.1 = bf16[32,80,128]{2,1,0:T(8,128)(2,1)S(1)} async-done(((bf16[32,80,128]{2,1,0:T(8,128)(2,1)}), bf16[32,80,128]{2,1,0:T(8,128)(2,1)S(1)}, u32[]{:S(2)}, u32[]{:S(2)}) %all-to-all-start.1) | async-done | bytes 655392 | tf_op jit(solution)/shard_map/all_to_all | solution.py:69
  90.3 0.8 copy-done.10
  91.2 5.4 %all-to-all-start.2 = ((bf16[16,400,128]{2,1,0:T(8,128)(2,1)}), bf16[16,400,128]{2,1,0:T(8,128)(2,1)S(1)}, u32[]{:S(2)}, u32[]{:S(2)}) async-start(bf16[16,400,128]{2,1,0:T(8,128)(2,1)} %add.59), calls=%async_computation.2 | async-start | bytes 3276800 | tf_op jit(solution)/shard_map/all_to_all | solution.py:69
  96.6 1.2 convert_reduce_fusion.1
  97.8 1.9 collective-permute-start.5
  99.7 3.1 %collective-permute-done.5 = f32[80,128]{1,0:T(8,128)S(1)} collective-permute-done((f32[80,128]{1,0:T(8,128)S(1)}, f32[80,128]{1,0:T(8,128)S(1)}, u32[]{:S(2)}, u32[]{:S(2)}) %collective-permute-start.5) | collective-permute-done | bytes 40992 | tf_op jit(solution)/shard_map/ppermute | solution.py:65
  102.8 2.3 collective-permute-start.6
  105.1 3.8 %collective-permute-done.6 = f32[80,128]{1,0:T(8,128)S(1)} collective-permute-done((f32[80,128]{1,0:T(8,128)S(1)}, f32[80,128]{1,0:T(8,128)S(1)}, u32[]{:S(2)}, u32[]{:S(2)}) %collective-permute-start.6) | collective-permute-done | bytes 40992 | tf_op jit(solution)/shard_map/ppermute | solution.py:65
  108.9 5.2 %collective-permute-start.7 = (bf16[80,128]{1,0:T(8,128)(2,1)S(1)}, bf16[80,128]{1,0:T(8,128)(2,1)S(1)}, u32[]{:S(2)}, u32[]{:S(2)}) collective-permute-start(bf16[80,128]{1,0:T(8,128)(2,1)S(1)} %add_convert_fusion.1), channel_id=1, source_target_pairs={{0,16},{1,17},{2,18},{3,19},{4,20},{5,21},{6,22},{7,23},{8,24},{9,... | collective-permute-start | bytes 61448 | tf_op jit(solution)/shard_map/ppermute | solution.py:65
  114.1 3.4 %collective-permute-done.7 = bf16[80,128]{1,0:T(8,128)(2,1)S(1)} collective-permute-done((bf16[80,128]{1,0:T(8,128)(2,1)S(1)}, bf16[80,128]{1,0:T(8,128)(2,1)S(1)}, u32[]{:S(2)}, u32[]{:S(2)}) %collective-permute-start.7) | collective-permute-done | bytes 20512 | tf_op jit(solution)/shard_map/ppermute | solution.py:65
  118.8 1.4 broadcast_in_dim.34
  120.2 7.2 %all-to-all-start.3 = ((bf16[16,400,128]{2,1,0:T(8,128)(2,1)}), bf16[16,400,128]{2,1,0:T(8,128)(2,1)}, u32[]{:S(2)}, u32[]{:S(2)}) async-start(bf16[16,400,128]{2,1,0:T(8,128)(2,1)} %broadcast_in_dim.34), calls=%async_computation.3 | async-start | bytes 3276800 | tf_op jit(solution)/shard_map/all_to_all | solution.py:69
  127.4 14.9 %collective-permute-start.9 = (bf16[80,128]{1,0:T(8,128)(2,1)S(1)}, bf16[80,128]{1,0:T(8,128)(2,1)S(1)}, u32[]{:S(2)}, u32[]{:S(2)}) collective-permute-start(bf16[80,128]{1,0:T(8,128)(2,1)S(1)} %convert_add_fusion.2), channel_id=1, source_target_pairs={{0,256},{1,257},{2,258},{3,259},{4,260},{5,261},{6,262},{7,263},{8... | collective-permute-start | bytes 61448 | tf_op jit(solution)/shard_map/ppermute | solution.py:65
  142.3 1.9 collective-permute-start.8
  144.3 5.5 %collective-permute-done.8 = bf16[432,128]{1,0:T(8,128)(2,1)S(1)} collective-permute-done((bf16[432,128]{1,0:T(8,128)(2,1)S(1)}, bf16[432,128]{1,0:T(8,128)(2,1)S(1)}, u32[]{:S(2)}, u32[]{:S(2)}) %collective-permute-start.8) | collective-permute-done | bytes 110624 | tf_op jit(solution)/shard_map/ppermute | solution.py:65
  149.8 7.2 %collective-permute-start.10 = (bf16[16,400,128]{2,1,0:T(8,128)(2,1)}, bf16[16,400,128]{2,1,0:T(8,128)(2,1)}, u32[]{:S(2)}, u32[]{:S(2)}) collective-permute-start(bf16[16,400,128]{2,1,0:T(8,128)(2,1)} %all-to-all-done.3.half), channel_id=1, source_target_pairs={{0,32},{1,33},{2,34},{3,35},{4,36},{5,37},{6,38},{7,39},{8,40},{9,... | collective-permute-start | bytes 4915208 | tf_op jit(solution)/shard_map/ppermute | solution.py:65
  157.0 0.9 broadcast_in_dim.35
  157.9 7.1 %all-to-all-start.4 = ((bf16[32,80,128]{2,1,0:T(8,128)(2,1)}), bf16[32,80,128]{2,1,0:T(8,128)(2,1)S(1)}, u32[]{:S(2)}, u32[]{:S(2)}) async-start(bf16[32,80,128]{2,1,0:T(8,128)(2,1)} %broadcast_in_dim.35), calls=%async_computation.4 | async-start | bytes 1310720 | tf_op jit(solution)/shard_map/all_to_all | solution.py:69
  165.0 3.9 %collective-permute-start.11 = (f32[408,128]{1,0:T(8,128)S(1)}, f32[408,128]{1,0:T(8,128)S(1)}, u32[]{:S(2)}, u32[]{:S(2)}) collective-permute-start(f32[408,128]{1,0:T(8,128)S(1)} %copy-done.9), channel_id=1, source_target_pairs={{0,0},{1,1},{2,2},{3,3},{4,64},{5,65},{6,66},{7,67},{8,128},{9,129... | collective-permute-start | bytes 626696 | tf_op jit(solution)/shard_map/ppermute | solution.py:65
  169.0 7.0 %all-to-all-done.4 = bf16[32,80,128]{2,1,0:T(8,128)(2,1)S(1)} async-done(((bf16[32,80,128]{2,1,0:T(8,128)(2,1)}), bf16[32,80,128]{2,1,0:T(8,128)(2,1)S(1)}, u32[]{:S(2)}, u32[]{:S(2)}) %all-to-all-start.4) | async-done | bytes 655392 | tf_op jit(solution)/shard_map/all_to_all | solution.py:69
  176.0 1.3 copy-done.1
  177.3 0.9 relation_update.2
  178.2 1.0 copy-done.4
  179.3 6.4 %collective-permute-done.11.kept = f32[408,128]{1,0:T(8,128)S(1)} collective-permute-done((f32[408,128]{1,0:T(8,128)S(1)}, f32[408,128]{1,0:T(8,128)S(1)}, u32[]{:S(2)}, u32[]{:S(2)}) %collective-permute-start.11) | collective-permute-done | bytes 208928 | tf_op jit(solution)/shard_map/ppermute | solution.py:65
  185.7 9.2 %edge_blocks.3 = (bf16[16,400,128]{2,1,0:T(8,128)(2,1)S(1)}, bf16[16,400,128]{2,1,0:T(8,128)(2,1)}, f32[400,128]{1,0:T(8,128)S(1)}, bf16[2560,128]{1,0:T(8,128)(2,1)}) custom-call(s32[128]{0:T(128)S(1)} %slice_bitcast_fusion.4.scal, s32[1]{0:T(128)} %bitcast.14.here, s32[32,128]{1,0:T(8,128)S(1)} %slice_convert_fusion.lists, ...), custom_call_target="tpu_custom_call" | custom-call | flops 2000000000 | bytes 10000000 | tf_op jit(solution)/shard_map/edge_blocks/pallas_call | solution.py:200
  194.9 1.9 collective-permute-start.12
  196.8 9.6 %all-to-all-start.5 = ((bf16[32,80,128]{2,1,0:T(8,128)(2,1)}), bf16[32,80,128]{2,1,0:T(8,128)(2,1)S(1)}, u32[]{:S(2)}, u32[]{:S(2)}) async-start(bf16[32,80,128]{2,1,0:T(8,128)(2,1)} %bitcast.20), calls=%async_computation.5 | async-start | bytes 1310720 | tf_op jit(solution)/shard_map/all_to_all | solution.py:69
  206.4 3.0 %add.64 = bf16[16,400,128]{2,1,0:T(8,128)(2,1)} add(bf16[16,400,128]{2,1,0:T(8,128)(2,1)S(1)} %get-tuple-element.68, bf16[16,400,128]{2,1,0:T(8,128)(2,1)} %collective-permute-done.12) | non-fusion elementwise | flops 819200 | bytes 4915200 | tf_op jit(solution)/shard_map/add | solution.py:399
  209.4 7.5 %all-to-all-done.5 = bf16[32,80,128]{2,1,0:T(8,128)(2,1)S(1)} async-done(((bf16[32,80,128]{2,1,0:T(8,128)(2,1)}), bf16[32,80,128]{2,1,0:T(8,128)(2,1)S(1)}, u32[]{:S(2)}, u32[]{:S(2)}) %all-to-all-start.5) | async-done | bytes 655392 | tf_op jit(solution)/shard_map/all_to_all | solution.py:69
  217.0 5.4 %all-to-all-start.6 = ((bf16[16,400,128]{2,1,0:T(8,128)(2,1)}), bf16[16,400,128]{2,1,0:T(8,128)(2,1)S(1)}, u32[]{:S(2)}, u32[]{:S(2)}) async-start(bf16[16,400,128]{2,1,0:T(8,128)(2,1)} %add.64), calls=%async_computation.6 | async-start | bytes 3276800 | tf_op jit(solution)/shard_map/all_to_all | solution.py:69
  222.4 2.2 collective-permute-start.15
  224.7 3.9 %collective-permute-start.13 = (f32[80,128]{1,0:T(8,128)S(1)}, f32[80,128]{1,0:T(8,128)S(1)}, u32[]{:S(2)}, u32[]{:S(2)}) collective-permute-start(f32[80,128]{1,0:T(8,128)S(1)} %convert_reduce_fusion), channel_id=1, source_target_pairs={{0,4},{1,5},{2,6},{3,7},{4,0},{5,1},{6,2},{7,3},{8,12},{9,13},{10,... | collective-permute-start | bytes 122888 | tf_op jit(solution)/shard_map/ppermute | solution.py:65
  228.6 1.7 collective-permute-done.13
  230.3 4.3 %collective-permute-start.14 = (f32[80,128]{1,0:T(8,128)S(1)}, f32[80,128]{1,0:T(8,128)S(1)}, u32[]{:S(2)}, u32[]{:S(2)}) collective-permute-start(f32[80,128]{1,0:T(8,128)S(1)} %add.65), channel_id=1, source_target_pairs={{0,8},{1,9},{2,10},{3,11},{4,12},{5,13},{6,14},{7,15},{8,0},{9,1},... | collective-permute-start | bytes 122888 | tf_op jit(solution)/shard_map/ppermute | solution.py:65
  234.6 3.9 %collective-permute-done.14 = f32[80,128]{1,0:T(8,128)S(1)} collective-permute-done((f32[80,128]{1,0:T(8,128)S(1)}, f32[80,128]{1,0:T(8,128)S(1)}, u32[]{:S(2)}, u32[]{:S(2)}) %collective-permute-start.14) | collective-permute-done | bytes 40992 | tf_op jit(solution)/shard_map/ppermute | solution.py:65
  239.2 5.7 %collective-permute-start.16 = (bf16[80,128]{1,0:T(8,128)(2,1)S(1)}, bf16[80,128]{1,0:T(8,128)(2,1)S(1)}, u32[]{:S(2)}, u32[]{:S(2)}) collective-permute-start(bf16[80,128]{1,0:T(8,128)(2,1)S(1)} %add.66), channel_id=1, source_target_pairs={{0,16},{1,17},{2,18},{3,19},{4,20},{5,21},{6,22},{7,23},{8,24},{9,... | collective-permute-start | bytes 61448 | tf_op jit(solution)/shard_map/ppermute | solution.py:65
  244.9 2.7 collective-permute-done.16
  247.6 7.5 %collective-permute-start.17 = (bf16[80,128]{1,0:T(8,128)(2,1)S(1)}, bf16[80,128]{1,0:T(8,128)(2,1)S(1)}, u32[]{:S(2)}, u32[]{:S(2)}) collective-permute-start(bf16[80,128]{1,0:T(8,128)(2,1)S(1)} %add_convert_fusion), channel_id=1, source_target_pairs={{0,256},{1,257},{2,258},{3,259},{4,260},{5,261},{6,262},{7,263},{8... | collective-permute-start | bytes 61448 | tf_op jit(solution)/shard_map/ppermute | solution.py:65
  255.1 5.8 %collective-permute-done.17 = bf16[80,128]{1,0:T(8,128)(2,1)S(1)} collective-permute-done((bf16[80,128]{1,0:T(8,128)(2,1)S(1)}, bf16[80,128]{1,0:T(8,128)(2,1)S(1)}, u32[]{:S(2)}, u32[]{:S(2)}) %collective-permute-start.17) | collective-permute-done | bytes 20512 | tf_op jit(solution)/shard_map/ppermute | solution.py:65
  260.9 0.9 broadcast_in_dim.36
  261.8 10.7 %all-to-all-start.7 = ((bf16[32,80,128]{2,1,0:T(8,128)(2,1)}), bf16[32,80,128]{2,1,0:T(8,128)(2,1)S(1)}, u32[]{:S(2)}, u32[]{:S(2)}) async-start(bf16[32,80,128]{2,1,0:T(8,128)(2,1)} %broadcast_in_dim.36), calls=%async_computation.7 | async-start | bytes 1310720 | tf_op jit(solution)/shard_map/all_to_all | solution.py:69
  272.5 0.9 copy-done.7
  273.9 6.7 %collective-permute-start.18 = (bf16[400,128]{1,0:T(8,128)(2,1)S(1)}, bf16[400,128]{1,0:T(8,128)(2,1)S(1)}, u32[]{:S(2)}, u32[]{:S(2)}) collective-permute-start(bf16[400,128]{1,0:T(8,128)(2,1)S(1)} %fold_pieces.1), channel_id=1, source_target_pairs={{0,0},{1,1},{2,2},{3,3},{4,64},{5,65},{6,66},{7,67},{8,128},{9,129... | collective-permute-start | bytes 307208 | tf_op jit(solution)/shard_map/ppermute | solution.py:65
  280.6 10.3 %collective-permute-done.18.grads = bf16[400,128]{1,0:T(8,128)(2,1)S(1)} collective-permute-done((bf16[400,128]{1,0:T(8,128)(2,1)S(1)}, bf16[400,128]{1,0:T(8,128)(2,1)S(1)}, u32[]{:S(2)}, u32[]{:S(2)}) %collective-permute-start.18) | collective-permute-done | bytes 102432 | tf_op jit(solution)/shard_map/ppermute | solution.py:65
  291.6 1.8 last_update.1
  293.4 1.3 copy-done.5
  294.6 2.4 relation_update.3
  (80 shorter events, 7.9 us)
Async XLA Ops:
  1.6 15.8 %collective-permute-start = (bf16[400,128]{1,0:T(8,128)(2,1)S(1)}, bf16[400,128]{1,0:T(8,128)(2,1)S(1)}, u32[]{:S(2)}, u32[]{:S(2)}) collective-permute-start(bf16[400,128]{1,0:T(8,128)(2,1)S(1)} %bitcast_convert_fusion), channel_id=1, source_target_pairs={{0,0},{1,1},{2,2},{3,3},{4,64},{5,65},{6,66},{7,67},{8,128},{9,129... | collective-permute-start | bytes 307208 | tf_op jit(solution)/shard_map/ppermute | solution.py:65
  19.4 7.9 %copy-start.16 = (f32[128]{0:T(128)S(1)}, f32[128]{0:T(128)}, u32[]{:S(2)}) copy-start(f32[128]{0:T(128)} %param.11) | copy-start | bytes 1540
  19.4 8.0 %copy-start.11 = (f32[128,400]{0,1:T(8,128)S(1)}, f32[128,400]{0,1:T(8,128)}, u32[]{:S(2)}) copy-start(f32[128,400]{0,1:T(8,128)} %param.10) | copy-start | bytes 614404
  19.4 17.9 %copy-start.14 = (s32[2,10,128]{2,0,1:T(2,128)S(1)}, s32[2,10,128]{2,0,1:T(2,128)}, u32[]{:S(2)}) copy-start(s32[2,10,128]{2,0,1:T(2,128)} %param.18) | copy-start | bytes 30724
  19.4 17.9 %copy-start.15 = (s32[2,10,128]{2,0,1:T(2,128)S(1)}, s32[2,10,128]{2,0,1:T(2,128)}, u32[]{:S(2)}) copy-start(s32[2,10,128]{2,0,1:T(2,128)} %param.17) | copy-start | bytes 30724
  19.5 32.7 %all-to-all-start = ((bf16[16,400,128]{2,1,0:T(8,128)(2,1)}), bf16[16,400,128]{2,1,0:T(8,128)(2,1)S(1)}, u32[]{:S(2)}, u32[]{:S(2)}) async-start(bf16[16,400,128]{2,1,0:T(8,128)(2,1)} %broadcast_in_dim.29), calls=%async_computation | async-start | bytes 3276800 | tf_op jit(solution)/shard_map/all_to_all | solution.py:69
  27.4 24.7 %collective-permute-start.2 = (f32[408,128]{1,0:T(8,128)S(1)}, f32[408,128]{1,0:T(8,128)S(1)}, u32[]{:S(2)}, u32[]{:S(2)}) collective-permute-start(f32[408,128]{1,0:T(8,128)S(1)} %pad_maximum_fusion), channel_id=1, source_target_pairs={{0,0},{1,1},{2,2},{3,3},{4,64},{5,65},{6,66},{7,67},{8,128},{9,129... | collective-permute-start | bytes 626696 | tf_op jit(solution)/shard_map/ppermute | solution.py:65
  37.4 14.7 %collective-permute-start.1 = (bf16[64,128]{1,0:T(8,128)(2,1)S(1)}, bf16[64,128]{1,0:T(8,128)(2,1)S(1)}, u32[]{:S(2)}, u32[]{:S(2)}) collective-permute-start(bf16[64,128]{1,0:T(8,128)(2,1)S(1)} %pad_maximum_fusion.2), channel_id=1, source_target_pairs={{0,0},{1,1},{2,2},{3,3},{4,64},{5,65},{6,66},{7,67},{8,128},{9,129... | collective-permute-start | bytes 49160 | tf_op jit(solution)/shard_map/ppermute | solution.py:65
  52.1 7.5 %collective-permute-start.3 = (bf16[16,400,128]{2,1,0:T(8,128)(2,1)S(1)}, bf16[16,400,128]{2,1,0:T(8,128)(2,1)}, u32[]{:S(2)}, u32[]{:S(2)}) collective-permute-start(bf16[16,400,128]{2,1,0:T(8,128)(2,1)S(1)} %all-to-all-done.half), channel_id=1, source_target_pairs={{0,32},{1,33},{2,34},{3,35},{4,36},{5,37},{6,38},{7,39},{8,40},{9,... | collective-permute-start | bytes 4915208 | tf_op jit(solution)/shard_map/ppermute | solution.py:65
  66.9 1.2 copy-start
  68.1 11.7 %collective-permute-start.4 = (bf16[16,400,128]{2,1,0:T(8,128)(2,1)}, bf16[16,400,128]{2,1,0:T(8,128)(2,1)}, u32[]{:S(2)}, u32[]{:S(2)}) collective-permute-start(bf16[16,400,128]{2,1,0:T(8,128)(2,1)} %get-tuple-element.53), channel_id=1, source_target_pairs={{0,32},{1,33},{2,34},{3,35},{4,36},{5,37},{6,38},{7,39},{8,40},{9,... | collective-permute-start | bytes 4915208 | tf_op jit(solution)/shard_map/ppermute | solution.py:65
  70.3 20.0 %all-to-all-start.1 = ((bf16[32,80,128]{2,1,0:T(8,128)(2,1)}), bf16[32,80,128]{2,1,0:T(8,128)(2,1)S(1)}, u32[]{:S(2)}, u32[]{:S(2)}) async-start(bf16[32,80,128]{2,1,0:T(8,128)(2,1)} %bitcast.16), calls=%async_computation.1 | async-start | bytes 1310720 | tf_op jit(solution)/shard_map/all_to_all | solution.py:69
  90.3 0.8 copy-start.10
  91.2 26.4 %all-to-all-start.2 = ((bf16[16,400,128]{2,1,0:T(8,128)(2,1)}), bf16[16,400,128]{2,1,0:T(8,128)(2,1)S(1)}, u32[]{:S(2)}, u32[]{:S(2)}) async-start(bf16[16,400,128]{2,1,0:T(8,128)(2,1)} %add.59), calls=%async_computation.2 | async-start | bytes 3276800 | tf_op jit(solution)/shard_map/all_to_all | solution.py:69
  97.8 5.0 %collective-permute-start.5 = (f32[80,128]{1,0:T(8,128)S(1)}, f32[80,128]{1,0:T(8,128)S(1)}, u32[]{:S(2)}, u32[]{:S(2)}) collective-permute-start(f32[80,128]{1,0:T(8,128)S(1)} %convert_reduce_fusion.1), channel_id=1, source_target_pairs={{0,4},{1,5},{2,6},{3,7},{4,0},{5,1},{6,2},{7,3},{8,12},{9,13},{10,... | collective-permute-start | bytes 122888 | tf_op jit(solution)/shard_map/ppermute | solution.py:65
  102.8 6.1 %collective-permute-start.6 = (f32[80,128]{1,0:T(8,128)S(1)}, f32[80,128]{1,0:T(8,128)S(1)}, u32[]{:S(2)}, u32[]{:S(2)}) collective-permute-start(f32[80,128]{1,0:T(8,128)S(1)} %add.60), channel_id=1, source_target_pairs={{0,8},{1,9},{2,10},{3,11},{4,12},{5,13},{6,14},{7,15},{8,0},{9,1},... | collective-permute-start | bytes 122888 | tf_op jit(solution)/shard_map/ppermute | solution.py:65
  108.9 8.6 %collective-permute-start.7 = (bf16[80,128]{1,0:T(8,128)(2,1)S(1)}, bf16[80,128]{1,0:T(8,128)(2,1)S(1)}, u32[]{:S(2)}, u32[]{:S(2)}) collective-permute-start(bf16[80,128]{1,0:T(8,128)(2,1)S(1)} %add_convert_fusion.1), channel_id=1, source_target_pairs={{0,16},{1,17},{2,18},{3,19},{4,20},{5,21},{6,22},{7,23},{8,24},{9,... | collective-permute-start | bytes 61448 | tf_op jit(solution)/shard_map/ppermute | solution.py:65
  118.1 0.7 copy-start.8
  120.2 29.7 %all-to-all-start.3 = ((bf16[16,400,128]{2,1,0:T(8,128)(2,1)}), bf16[16,400,128]{2,1,0:T(8,128)(2,1)}, u32[]{:S(2)}, u32[]{:S(2)}) async-start(bf16[16,400,128]{2,1,0:T(8,128)(2,1)} %broadcast_in_dim.34), calls=%async_computation.3 | async-start | bytes 3276800 | tf_op jit(solution)/shard_map/all_to_all | solution.py:69
  127.4 37.7 %copy-start.9 = (f32[408,128]{1,0:T(8,128)S(1)}, f32[408,128]{1,0:T(8,128)}, u32[]{:S(2)}) copy-start(f32[408,128]{1,0:T(8,128)} %copy-done.8) | copy-start | bytes 626692
  127.4 16.9 %collective-permute-start.9 = (bf16[80,128]{1,0:T(8,128)(2,1)S(1)}, bf16[80,128]{1,0:T(8,128)(2,1)S(1)}, u32[]{:S(2)}, u32[]{:S(2)}) collective-permute-start(bf16[80,128]{1,0:T(8,128)(2,1)S(1)} %convert_add_fusion.2), channel_id=1, source_target_pairs={{0,256},{1,257},{2,258},{3,259},{4,260},{5,261},{6,262},{7,263},{8... | collective-permute-start | bytes 61448 | tf_op jit(solution)/shard_map/ppermute | solution.py:65
  142.3 7.5 %collective-permute-start.8 = (bf16[432,128]{1,0:T(8,128)(2,1)S(1)}, bf16[432,128]{1,0:T(8,128)(2,1)S(1)}, u32[]{:S(2)}, u32[]{:S(2)}) collective-permute-start(bf16[432,128]{1,0:T(8,128)(2,1)S(1)} %pad_maximum_fusion.1), channel_id=1, source_target_pairs={{0,16},{1,17},{2,18},{3,19},{64,80},{65,81},{66,82},{67,83},{128,1... | collective-permute-start | bytes 331784 | tf_op jit(solution)/shard_map/ppermute | solution.py:65
  149.8 35.9 %collective-permute-start.10 = (bf16[16,400,128]{2,1,0:T(8,128)(2,1)}, bf16[16,400,128]{2,1,0:T(8,128)(2,1)}, u32[]{:S(2)}, u32[]{:S(2)}) collective-permute-start(bf16[16,400,128]{2,1,0:T(8,128)(2,1)} %all-to-all-done.3.half), channel_id=1, source_target_pairs={{0,32},{1,33},{2,34},{3,35},{4,36},{5,37},{6,38},{7,39},{8,40},{9,... | collective-permute-start | bytes 4915208 | tf_op jit(solution)/shard_map/ppermute | solution.py:65
  157.9 18.1 %all-to-all-start.4 = ((bf16[32,80,128]{2,1,0:T(8,128)(2,1)}), bf16[32,80,128]{2,1,0:T(8,128)(2,1)S(1)}, u32[]{:S(2)}, u32[]{:S(2)}) async-start(bf16[32,80,128]{2,1,0:T(8,128)(2,1)} %broadcast_in_dim.35), calls=%async_computation.4 | async-start | bytes 1310720 | tf_op jit(solution)/shard_map/all_to_all | solution.py:69
  165.0 20.6 %collective-permute-start.11 = (f32[408,128]{1,0:T(8,128)S(1)}, f32[408,128]{1,0:T(8,128)S(1)}, u32[]{:S(2)}, u32[]{:S(2)}) collective-permute-start(f32[408,128]{1,0:T(8,128)S(1)} %copy-done.9), channel_id=1, source_target_pairs={{0,0},{1,1},{2,2},{3,3},{4,64},{5,65},{6,66},{7,67},{8,128},{9,129... | collective-permute-start | bytes 626696 | tf_op jit(solution)/shard_map/ppermute | solution.py:65
  176.0 1.3 copy-start.1
  178.2 1.0 copy-start.4
  179.3 15.6 %copy-start.2 = (f32[400,768]{1,0:T(8,128)}, f32[400,768]{1,0:T(8,128)S(1)}, u32[]{:S(2)}) copy-start(f32[400,768]{1,0:T(8,128)S(1)} %get-tuple-element.64.rel) | copy-start | bytes 3686404
  185.7 9.2 %copy-start.12 = (f32[408,128]{1,0:T(8,128)}, f32[408,128]{1,0:T(8,128)S(1)}, u32[]{:S(2)}) copy-start(f32[408,128]{1,0:T(8,128)S(1)} %collective-permute-done.11.kept) | copy-start | bytes 626692
  194.9 11.6 %collective-permute-start.12 = (bf16[16,400,128]{2,1,0:T(8,128)(2,1)}, bf16[16,400,128]{2,1,0:T(8,128)(2,1)}, u32[]{:S(2)}, u32[]{:S(2)}) collective-permute-start(bf16[16,400,128]{2,1,0:T(8,128)(2,1)} %get-tuple-element.69), channel_id=1, source_target_pairs={{0,32},{1,33},{2,34},{3,35},{4,36},{5,37},{6,38},{7,39},{8,40},{9,... | collective-permute-start | bytes 4915208 | tf_op jit(solution)/shard_map/ppermute | solution.py:65
  196.8 20.2 %all-to-all-start.5 = ((bf16[32,80,128]{2,1,0:T(8,128)(2,1)}), bf16[32,80,128]{2,1,0:T(8,128)(2,1)S(1)}, u32[]{:S(2)}, u32[]{:S(2)}) async-start(bf16[32,80,128]{2,1,0:T(8,128)(2,1)} %bitcast.20), calls=%async_computation.5 | async-start | bytes 1310720 | tf_op jit(solution)/shard_map/all_to_all | solution.py:69
  217.0 43.9 %all-to-all-start.6 = ((bf16[16,400,128]{2,1,0:T(8,128)(2,1)}), bf16[16,400,128]{2,1,0:T(8,128)(2,1)S(1)}, u32[]{:S(2)}, u32[]{:S(2)}) async-start(bf16[16,400,128]{2,1,0:T(8,128)(2,1)} %add.64), calls=%async_computation.6 | async-start | bytes 3276800 | tf_op jit(solution)/shard_map/all_to_all | solution.py:69
  222.4 16.1 %collective-permute-start.15 = (bf16[400,128]{1,0:T(8,128)(2,1)S(1)}, bf16[400,128]{1,0:T(8,128)(2,1)S(1)}, u32[]{:S(2)}, u32[]{:S(2)}) collective-permute-start(bf16[400,128]{1,0:T(8,128)(2,1)S(1)} %convert_element_type.75), channel_id=1, source_target_pairs={{16,0},{17,1},{18,2},{19,3},{80,64},{81,65},{82,66},{83,67},{144,1... | collective-permute-start | bytes 307208 | tf_op jit(solution)/shard_map/ppermute | solution.py:65
  224.7 5.6 %collective-permute-start.13 = (f32[80,128]{1,0:T(8,128)S(1)}, f32[80,128]{1,0:T(8,128)S(1)}, u32[]{:S(2)}, u32[]{:S(2)}) collective-permute-start(f32[80,128]{1,0:T(8,128)S(1)} %convert_reduce_fusion), channel_id=1, source_target_pairs={{0,4},{1,5},{2,6},{3,7},{4,0},{5,1},{6,2},{7,3},{8,12},{9,13},{10,... | collective-permute-start | bytes 122888 | tf_op jit(solution)/shard_map/ppermute | solution.py:65
  230.3 8.2 %collective-permute-start.14 = (f32[80,128]{1,0:T(8,128)S(1)}, f32[80,128]{1,0:T(8,128)S(1)}, u32[]{:S(2)}, u32[]{:S(2)}) collective-permute-start(f32[80,128]{1,0:T(8,128)S(1)} %add.65), channel_id=1, source_target_pairs={{0,8},{1,9},{2,10},{3,11},{4,12},{5,13},{6,14},{7,15},{8,0},{9,1},... | collective-permute-start | bytes 122888 | tf_op jit(solution)/shard_map/ppermute | solution.py:65
  238.5 0.6 copy-start.6
  239.2 8.4 %collective-permute-start.16 = (bf16[80,128]{1,0:T(8,128)(2,1)S(1)}, bf16[80,128]{1,0:T(8,128)(2,1)S(1)}, u32[]{:S(2)}, u32[]{:S(2)}) collective-permute-start(bf16[80,128]{1,0:T(8,128)(2,1)S(1)} %add.66), channel_id=1, source_target_pairs={{0,16},{1,17},{2,18},{3,19},{4,20},{5,21},{6,22},{7,23},{8,24},{9,... | collective-permute-start | bytes 61448 | tf_op jit(solution)/shard_map/ppermute | solution.py:65
  247.6 13.2 %collective-permute-start.17 = (bf16[80,128]{1,0:T(8,128)(2,1)S(1)}, bf16[80,128]{1,0:T(8,128)(2,1)S(1)}, u32[]{:S(2)}, u32[]{:S(2)}) collective-permute-start(bf16[80,128]{1,0:T(8,128)(2,1)S(1)} %add_convert_fusion), channel_id=1, source_target_pairs={{0,256},{1,257},{2,258},{3,259},{4,260},{5,261},{6,262},{7,263},{8... | collective-permute-start | bytes 61448 | tf_op jit(solution)/shard_map/ppermute | solution.py:65
  261.8 31.5 %copy-start.3 = (f32[400,768]{1,0:T(8,128)S(1)}, f32[400,768]{1,0:T(8,128)}, u32[]{:S(2)}) copy-start(f32[400,768]{1,0:T(8,128)} %copy-done.2) | copy-start | bytes 3686404
  261.8 31.5 %all-to-all-start.7 = ((bf16[32,80,128]{2,1,0:T(8,128)(2,1)}), bf16[32,80,128]{2,1,0:T(8,128)(2,1)S(1)}, u32[]{:S(2)}, u32[]{:S(2)}) async-start(bf16[32,80,128]{2,1,0:T(8,128)(2,1)} %broadcast_in_dim.36), calls=%async_computation.7 | async-start | bytes 1310720 | tf_op jit(solution)/shard_map/all_to_all | solution.py:69
  272.5 0.9 copy-start.7
  273.9 17.0 %collective-permute-start.18 = (bf16[400,128]{1,0:T(8,128)(2,1)S(1)}, bf16[400,128]{1,0:T(8,128)(2,1)S(1)}, u32[]{:S(2)}, u32[]{:S(2)}) collective-permute-start(bf16[400,128]{1,0:T(8,128)(2,1)S(1)} %fold_pieces.1), channel_id=1, source_target_pairs={{0,0},{1,1},{2,2},{3,3},{4,64},{5,65},{6,66},{7,67},{8,128},{9,129... | collective-permute-start | bytes 307208 | tf_op jit(solution)/shard_map/ppermute | solution.py:65
  290.9 0.6 copy-start.13
  293.3 1.3 copy-start.5

commit v5 on v4

--- a/solution.py
+++ b/solution.py
@@ -403,9 +403,9 @@
     rel_mine = z_step(z_step(rel_mine, 4, BF16), 8, BF16)
     pieces, rel_mine = together(exchange(summed, SHEETS), rel_mine)
     grads = send(fold(pieces, lhs), TURN)
-    rel_sum = spread_relations(rel_mine)
+    rel, rel_state = relation_update(spread_relations(rel_mine), rel, rel_state, count)
+    kept, rel, rel_state = together(kept, rel, rel_state)
     weights, state = last(grads, kept)
-    rel, rel_state = relation_update(rel_sum, rel, rel_state, count)
     return (weights.T, state[0], rel.T, rel_state.T)
 
 

time: 299 us -> 297 us (level)
  the two profiles are of different devices: /device:TPU:17 before, /device:TPU:1 now
where the time goes in v5:
time: 297 us; the launch traced here: 294 us
  starting transfers between devices  172 us (58%)
  waiting for transfers between devices  70.9 us (24%)
  Pallas kernels  19.9 us (7%)
  local copies, waits for them, and re-layouts  17 us (6%)
  other arithmetic  12.6 us (4%)
    ppermute x19, starting transfers between devices, send(): return lax.ppermute(value, AXES, pairs)  103 us
    all_to_all x8, starting transfers between devices, exchange(): lax.all_to_all(value, AXES, 0, 0, axis_index_groups=groups, tiled=True)  70 us
    ppermute x19, waiting for transfers between devices, send(): return lax.ppermute(value, AXES, pairs)  41.2 us
    all_to_all x8, waiting for transfers between devices, exchange(): lax.all_to_all(value, AXES, 0, 0, axis_index_groups=groups, tiled=True)  29.7 us
    pallas_call x2, Pallas kernels, run_blocks(): pl.pallas_call(blocks_kernel, out_shape=(jax.ShapeDtypeStruct((16, width,...  13.1 us
    unnamed x34, local copies, waits for them, and re-layouts  8.46 us
  transfers between devices with their start and end apart: 27, of which 16 were waited for; matrix products, arithmetic and copies ran while one was open for 5% of the time, Pallas kernels for 2%

profile of v5, /device:TPU:1, one launch (start us, length us, event | category | flops | bytes accessed | tf_op | source)
XLA Modules:
  0.0 294.1 jit_solution(5988159438878680789)
XLA Ops:
  0.6 0.9 bitcast_convert_fusion
  1.6 10.2 %collective-permute-start = (bf16[400,128]{1,0:T(8,128)(2,1)S(1)}, bf16[400,128]{1,0:T(8,128)(2,1)S(1)}, u32[]{:S(2)}, u32[]{:S(2)}) collective-permute-start(bf16[400,128]{1,0:T(8,128)(2,1)S(1)} %bitcast_convert_fusion), channel_id=1, source_target_pairs={{0,0},{1,1},{2,2},{3,3},{4,64},{5,65},{6,66},{7,67},{8,128},{9,129... | collective-permute-start | bytes 307208 | tf_op jit(solution)/shard_map/ppermute | solution.py:65
  13.2 0.8 fusion.10
  14.3 0.8 fusion.12
  16.4 1.4 broadcast_in_dim.29
  17.8 10.4 %all-to-all-start = ((bf16[16,400,128]{2,1,0:T(8,128)(2,1)}), bf16[16,400,128]{2,1,0:T(8,128)(2,1)S(1)}, u32[]{:S(2)}, u32[]{:S(2)}) async-start(bf16[16,400,128]{2,1,0:T(8,128)(2,1)} %broadcast_in_dim.29), calls=%async_computation | async-start | bytes 3276800 | tf_op jit(solution)/shard_map/all_to_all | solution.py:69
  28.3 5.9 %collective-permute-start.2 = (f32[408,128]{1,0:T(8,128)S(1)}, f32[408,128]{1,0:T(8,128)S(1)}, u32[]{:S(2)}, u32[]{:S(2)}) collective-permute-start(f32[408,128]{1,0:T(8,128)S(1)} %pad_maximum_fusion), channel_id=1, source_target_pairs={{0,0},{1,1},{2,2},{3,3},{4,64},{5,65},{6,66},{7,67},{8,128},{9,129... | collective-permute-start | bytes 626696 | tf_op jit(solution)/shard_map/ppermute | solution.py:65
  35.9 3.5 %collective-permute-start.1 = (bf16[64,128]{1,0:T(8,128)(2,1)S(1)}, bf16[64,128]{1,0:T(8,128)(2,1)S(1)}, u32[]{:S(2)}, u32[]{:S(2)}) collective-permute-start(bf16[64,128]{1,0:T(8,128)(2,1)S(1)} %pad_maximum_fusion.2), channel_id=1, source_target_pairs={{0,0},{1,1},{2,2},{3,3},{4,64},{5,65},{6,66},{7,67},{8,128},{9,129... | collective-permute-start | bytes 49160 | tf_op jit(solution)/shard_map/ppermute | solution.py:65
  39.4 10.1 %collective-permute-done.1 = bf16[64,128]{1,0:T(8,128)(2,1)S(1)} collective-permute-done((bf16[64,128]{1,0:T(8,128)(2,1)S(1)}, bf16[64,128]{1,0:T(8,128)(2,1)S(1)}, u32[]{:S(2)}, u32[]{:S(2)}) %collective-permute-start.1) | collective-permute-done | bytes 16416 | tf_op jit(solution)/shard_map/ppermute | solution.py:65
  49.7 1.9 collective-permute-start.3
  51.6 1.4 pad.26.rel
  53.0 2.2 collective-permute-done.3.other
  55.2 7.2 %edge_blocks.2 = (bf16[16,400,128]{2,1,0:T(8,128)(2,1)S(1)}, bf16[16,400,128]{2,1,0:T(8,128)(2,1)}, f32[400,128]{1,0:T(8,128)S(1)}, bf16[2560,128]{1,0:T(8,128)(2,1)}) custom-call(s32[128]{0:T(128)S(1)} %slice_bitcast_fusion.5.scal, s32[1]{0:T(128)} %bitcast.14.here, s32[32,128]{1,0:T(8,128)S(1)} %get-tuple-element.97.lists, ...), custom_call_target="tpu_custom_call" | custom-call | flops 2000000000 | bytes 10000000 | tf_op jit(solution)/shard_map/edge_blocks/pallas_call | solution.py:200
  62.4 1.1 copy-done
  63.6 2.0 collective-permute-start.4
  65.6 12.0 %all-to-all-start.1 = ((bf16[32,80,128]{2,1,0:T(8,128)(2,1)}), bf16[32,80,128]{2,1,0:T(8,128)(2,1)S(1)}, u32[]{:S(2)}, u32[]{:S(2)}) async-start(bf16[32,80,128]{2,1,0:T(8,128)(2,1)} %bitcast.16), calls=%async_computation.1 | async-start | bytes 1310720 | tf_op jit(solution)/shard_map/all_to_all | solution.py:69
  77.6 3.6 %add.59 = bf16[16,400,128]{2,1,0:T(8,128)(2,1)} add(bf16[16,400,128]{2,1,0:T(8,128)(2,1)} %copy-done, bf16[16,400,128]{2,1,0:T(8,128)(2,1)} %collective-permute-done.4) | non-fusion elementwise | flops 819200 | bytes 4915200 | tf_op jit(solution)/shard_map/add | solution.py:386
  81.1 8.7 %all-to-all-done.1 = bf16[32,80,128]{2,1,0:T(8,128)(2,1)S(1)} async-done(((bf16[32,80,128]{2,1,0:T(8,128)(2,1)}), bf16[32,80,128]{2,1,0:T(8,128)(2,1)S(1)}, u32[]{:S(2)}, u32[]{:S(2)}) %all-to-all-start.1) | async-done | bytes 655392 | tf_op jit(solution)/shard_map/all_to_all | solution.py:69
  89.8 0.8 copy-done.10
  90.7 3.7 %all-to-all-start.2 = ((bf16[16,400,128]{2,1,0:T(8,128)(2,1)}), bf16[16,400,128]{2,1,0:T(8,128)(2,1)S(1)}, u32[]{:S(2)}, u32[]{:S(2)}) async-start(bf16[16,400,128]{2,1,0:T(8,128)(2,1)} %add.59), calls=%async_computation.2 | async-start | bytes 3276800 | tf_op jit(solution)/shard_map/all_to_all | solution.py:69
  94.4 1.2 convert_reduce_fusion.1
  95.6 5.3 %collective-permute-start.5 = (f32[80,128]{1,0:T(8,128)S(1)}, f32[80,128]{1,0:T(8,128)S(1)}, u32[]{:S(2)}, u32[]{:S(2)}) collective-permute-start(f32[80,128]{1,0:T(8,128)S(1)} %convert_reduce_fusion.1), channel_id=1, source_target_pairs={{0,4},{1,5},{2,6},{3,7},{4,0},{5,1},{6,2},{7,3},{8,12},{9,13},{10,... | collective-permute-start | bytes 122888 | tf_op jit(solution)/shard_map/ppermute | solution.py:65
  100.9 1.7 collective-permute-done.5
  102.6 2.5 collective-permute-start.6
  105.1 3.4 %collective-permute-done.6 = f32[80,128]{1,0:T(8,128)S(1)} collective-permute-done((f32[80,128]{1,0:T(8,128)S(1)}, f32[80,128]{1,0:T(8,128)S(1)}, u32[]{:S(2)}, u32[]{:S(2)}) %collective-permute-start.6) | collective-permute-done | bytes 40992 | tf_op jit(solution)/shard_map/ppermute | solution.py:65
  108.5 5.9 %collective-permute-start.7 = (bf16[80,128]{1,0:T(8,128)(2,1)S(1)}, bf16[80,128]{1,0:T(8,128)(2,1)S(1)}, u32[]{:S(2)}, u32[]{:S(2)}) collective-permute-start(bf16[80,128]{1,0:T(8,128)(2,1)S(1)} %add_convert_fusion.1), channel_id=1, source_target_pairs={{0,16},{1,17},{2,18},{3,19},{4,20},{5,21},{6,22},{7,23},{8,24},{9,... | collective-permute-start | bytes 61448 | tf_op jit(solution)/shard_map/ppermute | solution.py:65
  114.4 2.5 collective-permute-done.7
  118.6 1.4 broadcast_in_dim.34
  120.0 6.3 %all-to-all-start.3 = ((bf16[16,400,128]{2,1,0:T(8,128)(2,1)}), bf16[16,400,128]{2,1,0:T(8,128)(2,1)}, u32[]{:S(2)}, u32[]{:S(2)}) async-start(bf16[16,400,128]{2,1,0:T(8,128)(2,1)} %broadcast_in_dim.34), calls=%async_computation.3 | async-start | bytes 3276800 | tf_op jit(solution)/shard_map/all_to_all | solution.py:69
  126.3 19.3 %collective-permute-start.9 = (bf16[80,128]{1,0:T(8,128)(2,1)S(1)}, bf16[80,128]{1,0:T(8,128)(2,1)S(1)}, u32[]{:S(2)}, u32[]{:S(2)}) collective-permute-start(bf16[80,128]{1,0:T(8,128)(2,1)S(1)} %convert_add_fusion.2), channel_id=1, source_target_pairs={{0,256},{1,257},{2,258},{3,259},{4,260},{5,261},{6,262},{7,263},{8... | collective-permute-start | bytes 61448 | tf_op jit(solution)/shard_map/ppermute | solution.py:65
  145.7 1.9 collective-permute-start.8
  147.6 4.7 %collective-permute-done.8 = bf16[432,128]{1,0:T(8,128)(2,1)S(1)} collective-permute-done((bf16[432,128]{1,0:T(8,128)(2,1)S(1)}, bf16[432,128]{1,0:T(8,128)(2,1)S(1)}, u32[]{:S(2)}, u32[]{:S(2)}) %collective-permute-start.8) | collective-permute-done | bytes 110624 | tf_op jit(solution)/shard_map/ppermute | solution.py:65
  152.4 7.1 %collective-permute-start.10 = (bf16[16,400,128]{2,1,0:T(8,128)(2,1)}, bf16[16,400,128]{2,1,0:T(8,128)(2,1)}, u32[]{:S(2)}, u32[]{:S(2)}) collective-permute-start(bf16[16,400,128]{2,1,0:T(8,128)(2,1)} %all-to-all-done.3.half), channel_id=1, source_target_pairs={{0,32},{1,33},{2,34},{3,35},{4,36},{5,37},{6,38},{7,39},{8,40},{9,... | collective-permute-start | bytes 4915208 | tf_op jit(solution)/shard_map/ppermute | solution.py:65
  159.5 0.9 broadcast_in_dim.35
  160.4 7.3 %all-to-all-start.4 = ((bf16[32,80,128]{2,1,0:T(8,128)(2,1)}), bf16[32,80,128]{2,1,0:T(8,128)(2,1)S(1)}, u32[]{:S(2)}, u32[]{:S(2)}) async-start(bf16[32,80,128]{2,1,0:T(8,128)(2,1)} %broadcast_in_dim.35), calls=%async_computation.4 | async-start | bytes 1310720 | tf_op jit(solution)/shard_map/all_to_all | solution.py:69
  167.8 5.2 %collective-permute-start.11 = (f32[408,128]{1,0:T(8,128)S(1)}, f32[408,128]{1,0:T(8,128)S(1)}, u32[]{:S(2)}, u32[]{:S(2)}) collective-permute-start(f32[408,128]{1,0:T(8,128)S(1)} %copy-done.9), channel_id=1, source_target_pairs={{0,0},{1,1},{2,2},{3,3},{4,64},{5,65},{6,66},{7,67},{8,128},{9,129... | collective-permute-start | bytes 626696 | tf_op jit(solution)/shard_map/ppermute | solution.py:65
  173.0 7.0 %all-to-all-done.4 = bf16[32,80,128]{2,1,0:T(8,128)(2,1)S(1)} async-done(((bf16[32,80,128]{2,1,0:T(8,128)(2,1)}), bf16[32,80,128]{2,1,0:T(8,128)(2,1)S(1)}, u32[]{:S(2)}, u32[]{:S(2)}) %all-to-all-start.4) | async-done | bytes 655392 | tf_op jit(solution)/shard_map/all_to_all | solution.py:69
  180.0 1.3 copy-done.1
  181.3 0.9 relation_update.2
  182.3 1.0 copy-done.4
  183.3 5.9 %edge_blocks.3 = (bf16[16,400,128]{2,1,0:T(8,128)(2,1)S(1)}, bf16[16,400,128]{2,1,0:T(8,128)(2,1)}, f32[400,128]{1,0:T(8,128)S(1)}, bf16[2560,128]{1,0:T(8,128)(2,1)}) custom-call(s32[128]{0:T(128)S(1)} %slice_bitcast_fusion.4.scal, s32[1]{0:T(128)} %bitcast.14.here, s32[32,128]{1,0:T(8,128)S(1)} %slice_convert_fusion.lists, ...), custom_call_target="tpu_custom_call" | custom-call | flops 2000000000 | bytes 10000000 | tf_op jit(solution)/shard_map/edge_blocks/pallas_call | solution.py:200
  189.2 3.2 %collective-permute-start.12 = (bf16[16,400,128]{2,1,0:T(8,128)(2,1)}, bf16[16,400,128]{2,1,0:T(8,128)(2,1)}, u32[]{:S(2)}, u32[]{:S(2)}) collective-permute-start(bf16[16,400,128]{2,1,0:T(8,128)(2,1)} %get-tuple-element.72), channel_id=1, source_target_pairs={{0,32},{1,33},{2,34},{3,35},{4,36},{5,37},{6,38},{7,39},{8,40},{9,... | collective-permute-start | bytes 4915208 | tf_op jit(solution)/shard_map/ppermute | solution.py:65
  192.4 16.4 %all-to-all-start.5 = ((bf16[32,80,128]{2,1,0:T(8,128)(2,1)}), bf16[32,80,128]{2,1,0:T(8,128)(2,1)S(1)}, u32[]{:S(2)}, u32[]{:S(2)}) async-start(bf16[32,80,128]{2,1,0:T(8,128)(2,1)} %bitcast.20), calls=%async_computation.5 | async-start | bytes 1310720 | tf_op jit(solution)/shard_map/all_to_all | solution.py:69
  208.9 3.0 %add.64 = bf16[16,400,128]{2,1,0:T(8,128)(2,1)} add(bf16[16,400,128]{2,1,0:T(8,128)(2,1)S(1)} %get-tuple-element.71, bf16[16,400,128]{2,1,0:T(8,128)(2,1)} %collective-permute-done.12) | non-fusion elementwise | flops 819200 | bytes 4915200 | tf_op jit(solution)/shard_map/add | solution.py:399
  211.9 9.2 %all-to-all-done.5 = bf16[32,80,128]{2,1,0:T(8,128)(2,1)S(1)} async-done(((bf16[32,80,128]{2,1,0:T(8,128)(2,1)}), bf16[32,80,128]{2,1,0:T(8,128)(2,1)S(1)}, u32[]{:S(2)}, u32[]{:S(2)}) %all-to-all-start.5) | async-done | bytes 655392 | tf_op jit(solution)/shard_map/all_to_all | solution.py:69
  221.2 3.7 %all-to-all-start.6 = ((bf16[16,400,128]{2,1,0:T(8,128)(2,1)}), bf16[16,400,128]{2,1,0:T(8,128)(2,1)S(1)}, u32[]{:S(2)}, u32[]{:S(2)}) async-start(bf16[16,400,128]{2,1,0:T(8,128)(2,1)} %add.64), calls=%async_computation.6 | async-start | bytes 3276800 | tf_op jit(solution)/shard_map/all_to_all | solution.py:69
  224.9 2.3 collective-permute-start.15
  227.3 1.9 collective-permute-start.13
  229.2 3.1 %collective-permute-done.13 = f32[80,128]{1,0:T(8,128)S(1)} collective-permute-done((f32[80,128]{1,0:T(8,128)S(1)}, f32[80,128]{1,0:T(8,128)S(1)}, u32[]{:S(2)}, u32[]{:S(2)}) %collective-permute-start.13) | collective-permute-done | bytes 40992 | tf_op jit(solution)/shard_map/ppermute | solution.py:65
  232.3 5.3 %collective-permute-start.14 = (f32[80,128]{1,0:T(8,128)S(1)}, f32[80,128]{1,0:T(8,128)S(1)}, u32[]{:S(2)}, u32[]{:S(2)}) collective-permute-start(f32[80,128]{1,0:T(8,128)S(1)} %add.65), channel_id=1, source_target_pairs={{0,8},{1,9},{2,10},{3,11},{4,12},{5,13},{6,14},{7,15},{8,0},{9,1},... | collective-permute-start | bytes 122888 | tf_op jit(solution)/shard_map/ppermute | solution.py:65
  237.6 4.7 %collective-permute-done.14 = f32[80,128]{1,0:T(8,128)S(1)} collective-permute-done((f32[80,128]{1,0:T(8,128)S(1)}, f32[80,128]{1,0:T(8,128)S(1)}, u32[]{:S(2)}, u32[]{:S(2)}) %collective-permute-start.14) | collective-permute-done | bytes 40992 | tf_op jit(solution)/shard_map/ppermute | solution.py:65
  243.0 4.5 %collective-permute-start.16 = (bf16[80,128]{1,0:T(8,128)(2,1)S(1)}, bf16[80,128]{1,0:T(8,128)(2,1)S(1)}, u32[]{:S(2)}, u32[]{:S(2)}) collective-permute-start(bf16[80,128]{1,0:T(8,128)(2,1)S(1)} %add.66), channel_id=1, source_target_pairs={{0,16},{1,17},{2,18},{3,19},{4,20},{5,21},{6,22},{7,23},{8,24},{9,... | collective-permute-start | bytes 61448 | tf_op jit(solution)/shard_map/ppermute | solution.py:65
  247.5 3.9 %collective-permute-done.16 = bf16[80,128]{1,0:T(8,128)(2,1)S(1)} collective-permute-done((bf16[80,128]{1,0:T(8,128)(2,1)S(1)}, bf16[80,128]{1,0:T(8,128)(2,1)S(1)}, u32[]{:S(2)}, u32[]{:S(2)}) %collective-permute-start.16) | collective-permute-done | bytes 20512 | tf_op jit(solution)/shard_map/ppermute | solution.py:65
  251.5 8.3 %collective-permute-start.17 = (bf16[80,128]{1,0:T(8,128)(2,1)S(1)}, bf16[80,128]{1,0:T(8,128)(2,1)S(1)}, u32[]{:S(2)}, u32[]{:S(2)}) collective-permute-start(bf16[80,128]{1,0:T(8,128)(2,1)S(1)} %add_convert_fusion), channel_id=1, source_target_pairs={{0,256},{1,257},{2,258},{3,259},{4,260},{5,261},{6,262},{7,263},{8... | collective-permute-start | bytes 61448 | tf_op jit(solution)/shard_map/ppermute | solution.py:65
  259.8 4.9 %collective-permute-done.17 = bf16[80,128]{1,0:T(8,128)(2,1)S(1)} collective-permute-done((bf16[80,128]{1,0:T(8,128)(2,1)S(1)}, bf16[80,128]{1,0:T(8,128)(2,1)S(1)}, u32[]{:S(2)}, u32[]{:S(2)}) %collective-permute-start.17) | collective-permute-done | bytes 20512 | tf_op jit(solution)/shard_map/ppermute | solution.py:65
  264.7 0.9 broadcast_in_dim.36
  265.7 10.1 %all-to-all-start.7 = ((bf16[32,80,128]{2,1,0:T(8,128)(2,1)}), bf16[32,80,128]{2,1,0:T(8,128)(2,1)S(1)}, u32[]{:S(2)}, u32[]{:S(2)}) async-start(bf16[32,80,128]{2,1,0:T(8,128)(2,1)} %broadcast_in_dim.36), calls=%async_computation.7 | async-start | bytes 1310720 | tf_op jit(solution)/shard_map/all_to_all | solution.py:69
  275.7 0.9 copy-done.7
  276.6 1.1 fold_pieces.1
  277.7 6.1 %collective-permute-start.18 = (bf16[400,128]{1,0:T(8,128)(2,1)}, bf16[400,128]{1,0:T(8,128)(2,1)S(1)}, u32[]{:S(2)}, u32[]{:S(2)}) collective-permute-start(bf16[400,128]{1,0:T(8,128)(2,1)} %fold_pieces.1), channel_id=1, source_target_pairs={{0,0},{1,1},{2,2},{3,3},{4,64},{5,65},{6,66},{7,67},{8,128},{9,129... | collective-permute-start | bytes 307208 | tf_op jit(solution)/shard_map/ppermute | solution.py:65
  283.9 4.1 %all-to-all-done.7 = bf16[32,80,128]{2,1,0:T(8,128)(2,1)S(1)} async-done(((bf16[32,80,128]{2,1,0:T(8,128)(2,1)}), bf16[32,80,128]{2,1,0:T(8,128)(2,1)S(1)}, u32[]{:S(2)}, u32[]{:S(2)}) %all-to-all-start.7) | async-done | bytes 655392 | tf_op jit(solution)/shard_map/all_to_all | solution.py:69
  288.0 1.3 copy-done.5
  289.3 2.4 relation_update.3
  292.3 1.8 last_update.1
  (80 shorter events, 8.0 us)
Async XLA Ops:
  1.6 14.1 %collective-permute-start = (bf16[400,128]{1,0:T(8,128)(2,1)S(1)}, bf16[400,128]{1,0:T(8,128)(2,1)S(1)}, u32[]{:S(2)}, u32[]{:S(2)}) collective-permute-start(bf16[400,128]{1,0:T(8,128)(2,1)S(1)} %bitcast_convert_fusion), channel_id=1, source_target_pairs={{0,0},{1,1},{2,2},{3,3},{4,64},{5,65},{6,66},{7,67},{8,128},{9,129... | collective-permute-start | bytes 307208 | tf_op jit(solution)/shard_map/ppermute | solution.py:65
  17.8 10.5 %copy-start.16 = (f32[128]{0:T(128)S(1)}, f32[128]{0:T(128)}, u32[]{:S(2)}) copy-start(f32[128]{0:T(128)} %param.11) | copy-start | bytes 1540
  17.8 10.5 %copy-start.11 = (f32[128,400]{0,1:T(8,128)S(1)}, f32[128,400]{0,1:T(8,128)}, u32[]{:S(2)}) copy-start(f32[128,400]{0,1:T(8,128)} %param.10) | copy-start | bytes 614404
  17.8 18.0 %copy-start.14 = (s32[2,10,128]{2,0,1:T(2,128)S(1)}, s32[2,10,128]{2,0,1:T(2,128)}, u32[]{:S(2)}) copy-start(s32[2,10,128]{2,0,1:T(2,128)} %param.18) | copy-start | bytes 30724
  17.8 18.0 %copy-start.15 = (s32[2,10,128]{2,0,1:T(2,128)S(1)}, s32[2,10,128]{2,0,1:T(2,128)}, u32[]{:S(2)}) copy-start(s32[2,10,128]{2,0,1:T(2,128)} %param.17) | copy-start | bytes 30724
  17.8 31.9 %all-to-all-start = ((bf16[16,400,128]{2,1,0:T(8,128)(2,1)}), bf16[16,400,128]{2,1,0:T(8,128)(2,1)S(1)}, u32[]{:S(2)}, u32[]{:S(2)}) async-start(bf16[16,400,128]{2,1,0:T(8,128)(2,1)} %broadcast_in_dim.29), calls=%async_computation | async-start | bytes 3276800 | tf_op jit(solution)/shard_map/all_to_all | solution.py:69
  28.3 21.2 %collective-permute-start.2 = (f32[408,128]{1,0:T(8,128)S(1)}, f32[408,128]{1,0:T(8,128)S(1)}, u32[]{:S(2)}, u32[]{:S(2)}) collective-permute-start(f32[408,128]{1,0:T(8,128)S(1)} %pad_maximum_fusion), channel_id=1, source_target_pairs={{0,0},{1,1},{2,2},{3,3},{4,64},{5,65},{6,66},{7,67},{8,128},{9,129... | collective-permute-start | bytes 626696 | tf_op jit(solution)/shard_map/ppermute | solution.py:65
  35.9 13.6 %collective-permute-start.1 = (bf16[64,128]{1,0:T(8,128)(2,1)S(1)}, bf16[64,128]{1,0:T(8,128)(2,1)S(1)}, u32[]{:S(2)}, u32[]{:S(2)}) collective-permute-start(bf16[64,128]{1,0:T(8,128)(2,1)S(1)} %pad_maximum_fusion.2), channel_id=1, source_target_pairs={{0,0},{1,1},{2,2},{3,3},{4,64},{5,65},{6,66},{7,67},{8,128},{9,129... | collective-permute-start | bytes 49160 | tf_op jit(solution)/shard_map/ppermute | solution.py:65
  49.7 5.5 %collective-permute-start.3 = (bf16[16,400,128]{2,1,0:T(8,128)(2,1)S(1)}, bf16[16,400,128]{2,1,0:T(8,128)(2,1)}, u32[]{:S(2)}, u32[]{:S(2)}) collective-permute-start(bf16[16,400,128]{2,1,0:T(8,128)(2,1)S(1)} %all-to-all-done.half), channel_id=1, source_target_pairs={{0,32},{1,33},{2,34},{3,35},{4,36},{5,37},{6,38},{7,39},{8,40},{9,... | collective-permute-start | bytes 4915208 | tf_op jit(solution)/shard_map/ppermute | solution.py:65
  62.4 1.2 copy-start
  63.6 14.0 %collective-permute-start.4 = (bf16[16,400,128]{2,1,0:T(8,128)(2,1)}, bf16[16,400,128]{2,1,0:T(8,128)(2,1)}, u32[]{:S(2)}, u32[]{:S(2)}) collective-permute-start(bf16[16,400,128]{2,1,0:T(8,128)(2,1)} %get-tuple-element.56), channel_id=1, source_target_pairs={{0,32},{1,33},{2,34},{3,35},{4,36},{5,37},{6,38},{7,39},{8,40},{9,... | collective-permute-start | bytes 4915208 | tf_op jit(solution)/shard_map/ppermute | solution.py:65
  65.6 24.2 %all-to-all-start.1 = ((bf16[32,80,128]{2,1,0:T(8,128)(2,1)}), bf16[32,80,128]{2,1,0:T(8,128)(2,1)S(1)}, u32[]{:S(2)}, u32[]{:S(2)}) async-start(bf16[32,80,128]{2,1,0:T(8,128)(2,1)} %bitcast.16), calls=%async_computation.1 | async-start | bytes 1310720 | tf_op jit(solution)/shard_map/all_to_all | solution.py:69
  89.8 0.8 copy-start.10
  90.7 26.7 %all-to-all-start.2 = ((bf16[16,400,128]{2,1,0:T(8,128)(2,1)}), bf16[16,400,128]{2,1,0:T(8,128)(2,1)S(1)}, u32[]{:S(2)}, u32[]{:S(2)}) async-start(bf16[16,400,128]{2,1,0:T(8,128)(2,1)} %add.59), calls=%async_computation.2 | async-start | bytes 3276800 | tf_op jit(solution)/shard_map/all_to_all | solution.py:69
  95.6 7.0 %collective-permute-start.5 = (f32[80,128]{1,0:T(8,128)S(1)}, f32[80,128]{1,0:T(8,128)S(1)}, u32[]{:S(2)}, u32[]{:S(2)}) collective-permute-start(f32[80,128]{1,0:T(8,128)S(1)} %convert_reduce_fusion.1), channel_id=1, source_target_pairs={{0,4},{1,5},{2,6},{3,7},{4,0},{5,1},{6,2},{7,3},{8,12},{9,13},{10,... | collective-permute-start | bytes 122888 | tf_op jit(solution)/shard_map/ppermute | solution.py:65
  102.6 5.9 %collective-permute-start.6 = (f32[80,128]{1,0:T(8,128)S(1)}, f32[80,128]{1,0:T(8,128)S(1)}, u32[]{:S(2)}, u32[]{:S(2)}) collective-permute-start(f32[80,128]{1,0:T(8,128)S(1)} %add.60), channel_id=1, source_target_pairs={{0,8},{1,9},{2,10},{3,11},{4,12},{5,13},{6,14},{7,15},{8,0},{9,1},... | collective-permute-start | bytes 122888 | tf_op jit(solution)/shard_map/ppermute | solution.py:65
  108.5 8.4 %collective-permute-start.7 = (bf16[80,128]{1,0:T(8,128)(2,1)S(1)}, bf16[80,128]{1,0:T(8,128)(2,1)S(1)}, u32[]{:S(2)}, u32[]{:S(2)}) collective-permute-start(bf16[80,128]{1,0:T(8,128)(2,1)S(1)} %add_convert_fusion.1), channel_id=1, source_target_pairs={{0,16},{1,17},{2,18},{3,19},{4,20},{5,21},{6,22},{7,23},{8,24},{9,... | collective-permute-start | bytes 61448 | tf_op jit(solution)/shard_map/ppermute | solution.py:65
  117.9 0.7 copy-start.8
  120.0 32.4 %all-to-all-start.3 = ((bf16[16,400,128]{2,1,0:T(8,128)(2,1)}), bf16[16,400,128]{2,1,0:T(8,128)(2,1)}, u32[]{:S(2)}, u32[]{:S(2)}) async-start(bf16[16,400,128]{2,1,0:T(8,128)(2,1)} %broadcast_in_dim.34), calls=%async_computation.3 | async-start | bytes 3276800 | tf_op jit(solution)/shard_map/all_to_all | solution.py:69
  126.3 41.4 %copy-start.9 = (f32[408,128]{1,0:T(8,128)S(1)}, f32[408,128]{1,0:T(8,128)}, u32[]{:S(2)}) copy-start(f32[408,128]{1,0:T(8,128)} %copy-done.8) | copy-start | bytes 626692
  126.3 21.3 %collective-permute-start.9 = (bf16[80,128]{1,0:T(8,128)(2,1)S(1)}, bf16[80,128]{1,0:T(8,128)(2,1)S(1)}, u32[]{:S(2)}, u32[]{:S(2)}) collective-permute-start(bf16[80,128]{1,0:T(8,128)(2,1)S(1)} %convert_add_fusion.2), channel_id=1, source_target_pairs={{0,256},{1,257},{2,258},{3,259},{4,260},{5,261},{6,262},{7,263},{8... | collective-permute-start | bytes 61448 | tf_op jit(solution)/shard_map/ppermute | solution.py:65
  145.7 6.7 %collective-permute-start.8 = (bf16[432,128]{1,0:T(8,128)(2,1)S(1)}, bf16[432,128]{1,0:T(8,128)(2,1)S(1)}, u32[]{:S(2)}, u32[]{:S(2)}) collective-permute-start(bf16[432,128]{1,0:T(8,128)(2,1)S(1)} %pad_maximum_fusion.1), channel_id=1, source_target_pairs={{0,16},{1,17},{2,18},{3,19},{64,80},{65,81},{66,82},{67,83},{128,1... | collective-permute-start | bytes 331784 | tf_op jit(solution)/shard_map/ppermute | solution.py:65
  152.4 30.9 %collective-permute-start.10 = (bf16[16,400,128]{2,1,0:T(8,128)(2,1)}, bf16[16,400,128]{2,1,0:T(8,128)(2,1)}, u32[]{:S(2)}, u32[]{:S(2)}) collective-permute-start(bf16[16,400,128]{2,1,0:T(8,128)(2,1)} %all-to-all-done.3.half), channel_id=1, source_target_pairs={{0,32},{1,33},{2,34},{3,35},{4,36},{5,37},{6,38},{7,39},{8,40},{9,... | collective-permute-start | bytes 4915208 | tf_op jit(solution)/shard_map/ppermute | solution.py:65
  160.4 19.6 %all-to-all-start.4 = ((bf16[32,80,128]{2,1,0:T(8,128)(2,1)}), bf16[32,80,128]{2,1,0:T(8,128)(2,1)S(1)}, u32[]{:S(2)}, u32[]{:S(2)}) async-start(bf16[32,80,128]{2,1,0:T(8,128)(2,1)} %broadcast_in_dim.35), calls=%async_computation.4 | async-start | bytes 1310720 | tf_op jit(solution)/shard_map/all_to_all | solution.py:69
  167.8 15.6 %collective-permute-start.11 = (f32[408,128]{1,0:T(8,128)S(1)}, f32[408,128]{1,0:T(8,128)S(1)}, u32[]{:S(2)}, u32[]{:S(2)}) collective-permute-start(f32[408,128]{1,0:T(8,128)S(1)} %copy-done.9), channel_id=1, source_target_pairs={{0,0},{1,1},{2,2},{3,3},{4,64},{5,65},{6,66},{7,67},{8,128},{9,129... | collective-permute-start | bytes 626696 | tf_op jit(solution)/shard_map/ppermute | solution.py:65
  180.0 1.3 copy-start.1
  182.3 1.0 copy-start.4
  183.3 5.9 %copy-start.2 = (f32[400,768]{1,0:T(8,128)}, f32[400,768]{1,0:T(8,128)S(1)}, u32[]{:S(2)}) copy-start(f32[400,768]{1,0:T(8,128)S(1)} %get-tuple-element.67.rel) | copy-start | bytes 3686404
  183.3 5.9 %copy-start.12 = (f32[408,128]{1,0:T(8,128)}, f32[408,128]{1,0:T(8,128)S(1)}, u32[]{:S(2)}) copy-start(f32[408,128]{1,0:T(8,128)S(1)} %collective-permute-done.11.kept) | copy-start | bytes 626692
  189.2 19.7 %collective-permute-start.12 = (bf16[16,400,128]{2,1,0:T(8,128)(2,1)}, bf16[16,400,128]{2,1,0:T(8,128)(2,1)}, u32[]{:S(2)}, u32[]{:S(2)}) collective-permute-start(bf16[16,400,128]{2,1,0:T(8,128)(2,1)} %get-tuple-element.72), channel_id=1, source_target_pairs={{0,32},{1,33},{2,34},{3,35},{4,36},{5,37},{6,38},{7,39},{8,40},{9,... | collective-permute-start | bytes 4915208 | tf_op jit(solution)/shard_map/ppermute | solution.py:65
  192.4 28.7 %all-to-all-start.5 = ((bf16[32,80,128]{2,1,0:T(8,128)(2,1)}), bf16[32,80,128]{2,1,0:T(8,128)(2,1)S(1)}, u32[]{:S(2)}, u32[]{:S(2)}) async-start(bf16[32,80,128]{2,1,0:T(8,128)(2,1)} %bitcast.20), calls=%async_computation.5 | async-start | bytes 1310720 | tf_op jit(solution)/shard_map/all_to_all | solution.py:69
  221.2 43.5 %all-to-all-start.6 = ((bf16[16,400,128]{2,1,0:T(8,128)(2,1)}), bf16[16,400,128]{2,1,0:T(8,128)(2,1)S(1)}, u32[]{:S(2)}, u32[]{:S(2)}) async-start(bf16[16,400,128]{2,1,0:T(8,128)(2,1)} %add.64), calls=%async_computation.6 | async-start | bytes 3276800 | tf_op jit(solution)/shard_map/all_to_all | solution.py:69
  224.9 17.4 %collective-permute-start.15 = (bf16[400,128]{1,0:T(8,128)(2,1)S(1)}, bf16[400,128]{1,0:T(8,128)(2,1)S(1)}, u32[]{:S(2)}, u32[]{:S(2)}) collective-permute-start(bf16[400,128]{1,0:T(8,128)(2,1)S(1)} %convert_element_type.75), channel_id=1, source_target_pairs={{16,0},{17,1},{18,2},{19,3},{80,64},{81,65},{82,66},{83,67},{144,1... | collective-permute-start | bytes 307208 | tf_op jit(solution)/shard_map/ppermute | solution.py:65
  227.3 5.0 %collective-permute-start.13 = (f32[80,128]{1,0:T(8,128)S(1)}, f32[80,128]{1,0:T(8,128)S(1)}, u32[]{:S(2)}, u32[]{:S(2)}) collective-permute-start(f32[80,128]{1,0:T(8,128)S(1)} %convert_reduce_fusion), channel_id=1, source_target_pairs={{0,4},{1,5},{2,6},{3,7},{4,0},{5,1},{6,2},{7,3},{8,12},{9,13},{10,... | collective-permute-start | bytes 122888 | tf_op jit(solution)/shard_map/ppermute | solution.py:65
  232.3 10.0 %collective-permute-start.14 = (f32[80,128]{1,0:T(8,128)S(1)}, f32[80,128]{1,0:T(8,128)S(1)}, u32[]{:S(2)}, u32[]{:S(2)}) collective-permute-start(f32[80,128]{1,0:T(8,128)S(1)} %add.65), channel_id=1, source_target_pairs={{0,8},{1,9},{2,10},{3,11},{4,12},{5,13},{6,14},{7,15},{8,0},{9,1},... | collective-permute-start | bytes 122888 | tf_op jit(solution)/shard_map/ppermute | solution.py:65
  242.4 0.6 copy-start.6
  243.0 8.4 %collective-permute-start.16 = (bf16[80,128]{1,0:T(8,128)(2,1)S(1)}, bf16[80,128]{1,0:T(8,128)(2,1)S(1)}, u32[]{:S(2)}, u32[]{:S(2)}) collective-permute-start(bf16[80,128]{1,0:T(8,128)(2,1)S(1)} %add.66), channel_id=1, source_target_pairs={{0,16},{1,17},{2,18},{3,19},{4,20},{5,21},{6,22},{7,23},{8,24},{9,... | collective-permute-start | bytes 61448 | tf_op jit(solution)/shard_map/ppermute | solution.py:65
  251.5 13.2 %collective-permute-start.17 = (bf16[80,128]{1,0:T(8,128)(2,1)S(1)}, bf16[80,128]{1,0:T(8,128)(2,1)S(1)}, u32[]{:S(2)}, u32[]{:S(2)}) collective-permute-start(bf16[80,128]{1,0:T(8,128)(2,1)S(1)} %add_convert_fusion), channel_id=1, source_target_pairs={{0,256},{1,257},{2,258},{3,259},{4,260},{5,261},{6,262},{7,263},{8... | collective-permute-start | bytes 61448 | tf_op jit(solution)/shard_map/ppermute | solution.py:65
  265.7 22.4 %copy-start.3 = (f32[400,768]{1,0:T(8,128)S(1)}, f32[400,768]{1,0:T(8,128)}, u32[]{:S(2)}) copy-start(f32[400,768]{1,0:T(8,128)} %copy-done.2) | copy-start | bytes 3686404
  265.7 22.4 %all-to-all-start.7 = ((bf16[32,80,128]{2,1,0:T(8,128)(2,1)}), bf16[32,80,128]{2,1,0:T(8,128)(2,1)S(1)}, u32[]{:S(2)}, u32[]{:S(2)}) async-start(bf16[32,80,128]{2,1,0:T(8,128)(2,1)} %broadcast_in_dim.36), calls=%async_computation.7 | async-start | bytes 1310720 | tf_op jit(solution)/shard_map/all_to_all | solution.py:69
  275.7 0.9 copy-start.7
  277.7 13.9 %collective-permute-start.18 = (bf16[400,128]{1,0:T(8,128)(2,1)}, bf16[400,128]{1,0:T(8,128)(2,1)S(1)}, u32[]{:S(2)}, u32[]{:S(2)}) collective-permute-start(bf16[400,128]{1,0:T(8,128)(2,1)} %fold_pieces.1), channel_id=1, source_target_pairs={{0,0},{1,1},{2,2},{3,3},{4,64},{5,65},{6,66},{7,67},{8,128},{9,129... | collective-permute-start | bytes 307208 | tf_op jit(solution)/shard_map/ppermute | solution.py:65
  288.0 1.3 copy-start.5
  291.7 0.6 copy-start.13

commit v6 on v5

--- a/solution.py
+++ b/solution.py
@@ -86,7 +86,7 @@
 
 
 def blocks_kernel(
-    scal, here, lists, own, rel, half, other, mine_out, theirs_out, lhs_out, rel_out, table, acc, rel_acc, sems
+    scal, here, lists, own, rel, half, other, mine_out, theirs_out, lhs_out, rel_out, table, acc, rel_acc, sems, update=None
 ):
     slots = 10
     width, block = own.shape
@@ -97,6 +97,8 @@
     ]
     for copy in copies:
         copy.start()
+    if update is not None:
+        relation_kernel(*update)
 
     def clear(k, carry):
         acc[k] = jnp.zeros((width, block), F32)
@@ -191,32 +193,49 @@
     rel_out[first + FOLD :] = jnp.zeros((rel_out.shape[0] - first - FOLD, block), BF16)
 
 
-def run_blocks(lists, here, own, rel, half, other):
+def updating_kernel(
+    scal, here, lists, own, rel, half, other, packed, rel_state,
+    mine_out, theirs_out, lhs_out, rel_out, new_rel, new_state,
+    table, acc, rel_acc, sems,
+):
+    blocks_kernel(
+        scal, here, lists, own, new_rel, half, other, mine_out, theirs_out, lhs_out, rel_out, table, acc, rel_acc, sems,
+        update=(packed, rel, rel_state, new_rel, new_state),
+    )
+
+
+def run_blocks(lists, here, own, rel, half, other, rel_sum=None, rel_state=None):
     width, block = own.shape
-    rel_lanes = rel.shape[1]
     vmem = pl.BlockSpec(memory_space=pltpu.VMEM)
     smem = pl.BlockSpec(memory_space=pltpu.SMEM)
     hbm = pl.BlockSpec(memory_space=pl.ANY)
+    kernel, more, out_shape = blocks_kernel, [], [
+        jax.ShapeDtypeStruct((16, width, block), BF16),
+        jax.ShapeDtypeStruct((16, width, block), BF16),
+        jax.ShapeDtypeStruct((width, block), F32),
+        jax.ShapeDtypeStruct((32 * PIECE, block), BF16),
+    ]
+    if rel_sum is not None:
+        kernel, more = updating_kernel, [rel_sum.reshape(-1, block), rel_state]
+        out_shape = out_shape + [
+            jax.ShapeDtypeStruct(rel.shape, F32),
+            jax.ShapeDtypeStruct(rel_state.shape, F32),
+        ]
     return pl.pallas_call(
-        blocks_kernel,
-        out_shape=(
-            jax.ShapeDtypeStruct((16, width, block), BF16),
-            jax.ShapeDtypeStruct((16, width, block), BF16),
-            jax.ShapeDtypeStruct((width, block), F32),
-            jax.ShapeDtypeStruct((32 * PIECE, block), BF16),
-        ),
-        in_specs=[smem, smem, vmem, vmem, vmem, hbm, hbm],
-        out_specs=(vmem, vmem, vmem, vmem),
+        kernel,
+        out_shape=out_shape,
+        in_specs=[smem, smem, vmem, vmem, vmem, hbm, hbm] + [vmem] * len(more),
+        out_specs=[vmem] * len(out_shape),
         scratch_shapes=[
             pltpu.VMEM((32, width, block), BF16),
             pltpu.VMEM((32, width, block), F32),
-            pltpu.VMEM((width, rel_lanes), F32),
+            pltpu.VMEM((width, rel.shape[1]), F32),
             pltpu.SemaphoreType.DMA((2,)),
         ],
-        compiler_params=pltpu.CompilerParams(vmem_limit_bytes=40 * MIB),
+        compiler_params=pltpu.CompilerParams(vmem_limit_bytes=44 * MIB),
         cost_estimate=pl.CostEstimate(flops=2 * 10**9, bytes_accessed=10**7, transcendentals=10**6),
         name="edge_blocks",
-    )(lists[20], here, lists, own, rel, half, other)
+    )(lists[20], here, lists, own, rel, half, other, *more)
 
 
 def adagrad(grads, kept):
@@ -233,18 +252,25 @@
     return lax.fori_loop(1, pieces.shape[0], add, pieces[0].astype(F32))
 
 
-def middle_kernel(pieces, lhs, kept, kept_out, table_out):
+def middle_kernel(pieces, lhs, kept, kept_out, table_out, copies_out):
     width = lhs.shape[0]
     weights, state = adagrad(lhs[...] + add_pieces(pieces), kept[...])
     kept_out[:width] = weights
     kept_out[width:] = jnp.broadcast_to(state, (kept.shape[0] - width, state.shape[1]))
-    table_out[...] = weights.astype(BF16)
+    table = weights.astype(BF16)
+    table_out[...] = table
+    for k in range(copies_out.shape[0]):
+        copies_out[k] = table
 
 
 def middle(pieces, lhs, kept):
     return pl.pallas_call(
         middle_kernel,
-        out_shape=(jax.ShapeDtypeStruct(kept.shape, F32), jax.ShapeDtypeStruct(lhs.shape, BF16)),
+        out_shape=(
+            jax.ShapeDtypeStruct(kept.shape, F32),
+            jax.ShapeDtypeStruct(lhs.shape, BF16),
+            jax.ShapeDtypeStruct((16,) + lhs.shape, BF16),
+        ),
         compiler_params=pltpu.CompilerParams(vmem_limit_bytes=16 * MIB),
         name="middle_update",
     )(pieces, lhs, kept)
@@ -385,16 +411,18 @@
     rel_pieces = exchange(rel_part.reshape(32, PIECE, block), PLANES)
     summed, rel_pieces = together(mine + send(theirs, OTHER), rel_pieces)
     pieces, rel_mine = together(exchange(summed, SHEETS), z_steps(rel_pieces))
-    kept, own = middle(pieces, lhs, kept)
+    kept, own, copies = middle(pieces, lhs, kept)
     source = send(jnp.concatenate([own, lists[LISTS:]]), NEXT)
     kept = send(kept, TURN)
-    half, source, rel_mine = together(gather_sheet(own), source, z_step(rel_mine, 8, BF16))
+    half, source, rel_mine = together(exchange(copies, SHEETS), source, z_step(rel_mine, 8, BF16))
     other = send(half, OTHER)
-    rel, rel_state = relation_update(spread_relations(rel_mine), rel, rel_state, lanes)
+    rel_sum = spread_relations(rel_mine)
     other, kept = together(other, kept)
 
     now = source[width:].astype(jnp.int32)
-    mine, theirs, lhs, rel_part = run_blocks(now, here, source[:width], rel, half, other)
+    mine, theirs, lhs, rel_part, rel, rel_state = run_blocks(
+        now, here, source[:width], rel, half, other, rel_sum, rel_state
+    )
     rel_pieces = exchange(rel_part.reshape(32, PIECE, block), PLANES)
     summed, lhs = together(mine + send(theirs, OTHER), lhs.astype(BF16))
     summed, rel_pieces = together(summed, rel_pieces)

time: 297 us -> 303 us (1.020)
  local copies, waits for them, and re-layouts: 17 us -> 21.3 us
    ppermute x19, waiting for transfers between devices: 41.2 us -> 47.5 us  [send(): return lax.ppermute(value, AXES, pairs)]
    unnamed x34 -> x52, local copies, waits for them, and re-layouts: 8.46 us -> 13.4 us
    all_to_all x8, waiting for transfers between devices: 29.7 us -> 25.7 us  [exchange(): lax.all_to_all(value, AXES, 0, 0, axis_index_groups=groups, tiled=True)]
    ppermute x19, starting transfers between devices: 103 us -> 99 us  [send(): return lax.ppermute(value, AXES, pairs)]
  transfers between devices with their start and end apart: 27 -> 27, of which waited for: 16 -> 17; matrix products, arithmetic and copies ran while one was open for 5% -> 6% of each run, Pallas kernels for 2% -> 1%
where the time goes in v6:
time: 303 us; the launch traced here: 300 us
  starting transfers between devices  169 us (56%)
  waiting for transfers between devices  73.2 us (24%)
  Pallas kernels  22.5 us (7%)
  local copies, waits for them, and re-layouts  21.3 us (7%)
  other arithmetic  12.6 us (4%)
    ppermute x19, starting transfers between devices, send(): return lax.ppermute(value, AXES, pairs)  99 us
    all_to_all x8, starting transfers between devices, exchange(): lax.all_to_all(value, AXES, 0, 0, axis_index_groups=groups, tiled=True)  69.8 us
    ppermute x19, waiting for transfers between devices, send(): return lax.ppermute(value, AXES, pairs)  47.5 us
    all_to_all x8, waiting for transfers between devices, exchange(): lax.all_to_all(value, AXES, 0, 0, axis_index_groups=groups, tiled=True)  25.7 us
    pallas_call x2, Pallas kernels, run_blocks(): pl.pallas_call(kernel, out_shape=out_shape, in_specs=[smem, smem, vmem, v...  15.3 us
    unnamed x52, local copies, waits for them, and re-layouts  13.4 us
  transfers between devices with their start and end apart: 27, of which 17 were waited for; matrix products, arithmetic and copies ran while one was open for 6% of the time, Pallas kernels for 1%

profile of v6, /device:TPU:1, one launch (start us, length us, event | category | flops | bytes accessed | tf_op | source)
XLA Modules:
  0.0 299.6 jit_solution(2477991338880416530)
XLA Ops:
  0.6 0.9 bitcast_convert_fusion
  1.6 10.2 %collective-permute-start = (bf16[400,128]{1,0:T(8,128)(2,1)S(1)}, bf16[400,128]{1,0:T(8,128)(2,1)S(1)}, u32[]{:S(2)}, u32[]{:S(2)}) collective-permute-start(bf16[400,128]{1,0:T(8,128)(2,1)S(1)} %bitcast_convert_fusion), channel_id=1, source_target_pairs={{0,0},{1,1},{2,2},{3,3},{4,64},{5,65},{6,66},{7,67},{8,128},{9,129... | collective-permute-start | bytes 307208 | tf_op jit(solution)/shard_map/ppermute | solution.py:65
  16.4 1.4 broadcast_in_dim.26
  17.8 10.4 %all-to-all-start = ((bf16[16,400,128]{2,1,0:T(8,128)(2,1)}), bf16[16,400,128]{2,1,0:T(8,128)(2,1)S(1)}, u32[]{:S(2)}, u32[]{:S(2)}) async-start(bf16[16,400,128]{2,1,0:T(8,128)(2,1)} %broadcast_in_dim.26), calls=%async_computation | async-start | bytes 3276800 | tf_op jit(solution)/shard_map/all_to_all | solution.py:69
  28.3 5.9 %collective-permute-start.2 = (f32[408,128]{1,0:T(8,128)S(1)}, f32[408,128]{1,0:T(8,128)S(1)}, u32[]{:S(2)}, u32[]{:S(2)}) collective-permute-start(f32[408,128]{1,0:T(8,128)S(1)} %pad_maximum_fusion), channel_id=1, source_target_pairs={{0,0},{1,1},{2,2},{3,3},{4,64},{5,65},{6,66},{7,67},{8,128},{9,129... | collective-permute-start | bytes 626696 | tf_op jit(solution)/shard_map/ppermute | solution.py:65
  35.9 3.5 %collective-permute-start.1 = (bf16[64,128]{1,0:T(8,128)(2,1)S(1)}, bf16[64,128]{1,0:T(8,128)(2,1)S(1)}, u32[]{:S(2)}, u32[]{:S(2)}) collective-permute-start(bf16[64,128]{1,0:T(8,128)(2,1)S(1)} %pad_maximum_fusion.2), channel_id=1, source_target_pairs={{0,0},{1,1},{2,2},{3,3},{4,64},{5,65},{6,66},{7,67},{8,128},{9,129... | collective-permute-start | bytes 49160 | tf_op jit(solution)/shard_map/ppermute | solution.py:65
  39.4 10.1 %collective-permute-done.1 = bf16[64,128]{1,0:T(8,128)(2,1)S(1)} collective-permute-done((bf16[64,128]{1,0:T(8,128)(2,1)S(1)}, bf16[64,128]{1,0:T(8,128)(2,1)S(1)}, u32[]{:S(2)}, u32[]{:S(2)}) %collective-permute-start.1) | collective-permute-done | bytes 16416 | tf_op jit(solution)/shard_map/ppermute | solution.py:65
  49.7 1.9 collective-permute-start.3
  51.6 1.4 pad.26.rel
  53.1 2.0 collective-permute-done.3.other
  55.1 1.2 copy-done.16
  56.3 1.4 copy-done.17
  57.7 9.6 %edge_blocks.2 = (bf16[16,400,128]{2,1,0:T(8,128)(2,1)S(1)}, bf16[16,400,128]{2,1,0:T(8,128)(2,1)}, f32[400,128]{1,0:T(8,128)S(1)}, bf16[2560,128]{1,0:T(8,128)(2,1)S(1)}) custom-call(s32[128]{0:T(128)S(1)} %slice_bitcast_fusion.5.scal, s32[1]{0:T(128)} %bitcast.14.here, s32[32,128]{1,0:T(8,128)S(1)} %get-tuple-element.99.lists, ...), custom_call_target="tpu_custom_call" | custom-call | flops 2000000000 | bytes 10000000 | tf_op jit(solution)/shard_map/edge_blocks/pallas_call | solution.py:224
  68.9 1.9 collective-permute-start.4
  70.8 11.8 %all-to-all-start.1 = ((bf16[32,80,128]{2,1,0:T(8,128)(2,1)}), bf16[32,80,128]{2,1,0:T(8,128)(2,1)S(1)}, u32[]{:S(2)}, u32[]{:S(2)}) async-start(bf16[32,80,128]{2,1,0:T(8,128)(2,1)} %bitcast.66), calls=%async_computation.1 | async-start | bytes 1310720 | tf_op jit(solution)/shard_map/all_to_all | solution.py:69
  82.6 3.1 %add.59 = bf16[16,400,128]{2,1,0:T(8,128)(2,1)} add(bf16[16,400,128]{2,1,0:T(8,128)(2,1)S(1)} %get-tuple-element.56, bf16[16,400,128]{2,1,0:T(8,128)(2,1)} %collective-permute-done.4) | non-fusion elementwise | flops 819200 | bytes 4915200 | tf_op jit(solution)/shard_map/add | solution.py:412
  85.7 9.1 %all-to-all-done.1 = bf16[32,80,128]{2,1,0:T(8,128)(2,1)S(1)} async-done(((bf16[32,80,128]{2,1,0:T(8,128)(2,1)}), bf16[32,80,128]{2,1,0:T(8,128)(2,1)S(1)}, u32[]{:S(2)}, u32[]{:S(2)}) %all-to-all-start.1) | async-done | bytes 655392 | tf_op jit(solution)/shard_map/all_to_all | solution.py:69
  94.9 3.7 %all-to-all-start.2 = ((bf16[16,400,128]{2,1,0:T(8,128)(2,1)}), bf16[16,400,128]{2,1,0:T(8,128)(2,1)S(1)}, u32[]{:S(2)}, u32[]{:S(2)}) async-start(bf16[16,400,128]{2,1,0:T(8,128)(2,1)} %add.59), calls=%async_computation.2 | async-start | bytes 3276800 | tf_op jit(solution)/shard_map/all_to_all | solution.py:69
  98.7 1.9 collective-permute-start.5
  100.6 2.8 collective-permute-done.5
  103.5 2.9 collective-permute-start.6
  106.3 3.5 %collective-permute-done.6 = f32[80,128]{1,0:T(8,128)S(1)} collective-permute-done((f32[80,128]{1,0:T(8,128)S(1)}, f32[80,128]{1,0:T(8,128)S(1)}, u32[]{:S(2)}, u32[]{:S(2)}) %collective-permute-start.6) | collective-permute-done | bytes 40992 | tf_op jit(solution)/shard_map/ppermute | solution.py:65
  109.8 3.6 %collective-permute-start.7 = (bf16[80,128]{1,0:T(8,128)(2,1)S(1)}, bf16[80,128]{1,0:T(8,128)(2,1)S(1)}, u32[]{:S(2)}, u32[]{:S(2)}) collective-permute-start(bf16[80,128]{1,0:T(8,128)(2,1)S(1)} %add_convert_fusion.1), channel_id=1, source_target_pairs={{0,16},{1,17},{2,18},{3,19},{4,20},{5,21},{6,22},{7,23},{8,24},{9,... | collective-permute-start | bytes 61448 | tf_op jit(solution)/shard_map/ppermute | solution.py:65
  113.4 4.8 %collective-permute-done.7 = bf16[80,128]{1,0:T(8,128)(2,1)S(1)} collective-permute-done((bf16[80,128]{1,0:T(8,128)(2,1)S(1)}, bf16[80,128]{1,0:T(8,128)(2,1)S(1)}, u32[]{:S(2)}, u32[]{:S(2)}) %collective-permute-start.7) | collective-permute-done | bytes 20512 | tf_op jit(solution)/shard_map/ppermute | solution.py:65
  118.3 3.4 %all-to-all-done.2.pieces = bf16[16,400,128]{2,1,0:T(8,128)(2,1)S(1)} async-done(((bf16[16,400,128]{2,1,0:T(8,128)(2,1)}), bf16[16,400,128]{2,1,0:T(8,128)(2,1)S(1)}, u32[]{:S(2)}, u32[]{:S(2)}) %all-to-all-start.2) | async-done | bytes 1638432 | tf_op jit(solution)/shard_map/all_to_all | solution.py:69
  121.7 1.9 middle_update.1
  123.6 5.1 %all-to-all-start.3 = ((bf16[16,400,128]{2,1,0:T(8,128)(2,1)}), bf16[16,400,128]{2,1,0:T(8,128)(2,1)}, u32[]{:S(2)}, u32[]{:S(2)}) async-start(bf16[16,400,128]{2,1,0:T(8,128)(2,1)} %get-tuple-element.64), calls=%async_computation.3 | async-start | bytes 3276800 | tf_op jit(solution)/shard_map/all_to_all | solution.py:69
  128.7 14.6 %collective-permute-start.9 = (bf16[80,128]{1,0:T(8,128)(2,1)S(1)}, bf16[80,128]{1,0:T(8,128)(2,1)S(1)}, u32[]{:S(2)}, u32[]{:S(2)}) collective-permute-start(bf16[80,128]{1,0:T(8,128)(2,1)S(1)} %convert_add_fusion.2), channel_id=1, source_target_pairs={{0,256},{1,257},{2,258},{3,259},{4,260},{5,261},{6,262},{7,263},{8... | collective-permute-start | bytes 61448 | tf_op jit(solution)/shard_map/ppermute | solution.py:65
  143.3 1.9 collective-permute-start.8
  145.3 5.0 %collective-permute-done.8 = bf16[432,128]{1,0:T(8,128)(2,1)S(1)} collective-permute-done((bf16[432,128]{1,0:T(8,128)(2,1)S(1)}, bf16[432,128]{1,0:T(8,128)(2,1)S(1)}, u32[]{:S(2)}, u32[]{:S(2)}) %collective-permute-start.8) | collective-permute-done | bytes 110624 | tf_op jit(solution)/shard_map/ppermute | solution.py:65
  150.2 7.4 %collective-permute-start.10 = (bf16[16,400,128]{2,1,0:T(8,128)(2,1)}, bf16[16,400,128]{2,1,0:T(8,128)(2,1)}, u32[]{:S(2)}, u32[]{:S(2)}) collective-permute-start(bf16[16,400,128]{2,1,0:T(8,128)(2,1)} %all-to-all-done.3.half), channel_id=1, source_target_pairs={{0,32},{1,33},{2,34},{3,35},{4,36},{5,37},{6,38},{7,39},{8,40},{9,... | collective-permute-start | bytes 4915208 | tf_op jit(solution)/shard_map/ppermute | solution.py:65
  157.7 0.9 broadcast_in_dim.31
  158.6 7.3 %all-to-all-start.4 = ((bf16[32,80,128]{2,1,0:T(8,128)(2,1)}), bf16[32,80,128]{2,1,0:T(8,128)(2,1)S(1)}, u32[]{:S(2)}, u32[]{:S(2)}) async-start(bf16[32,80,128]{2,1,0:T(8,128)(2,1)} %broadcast_in_dim.31), calls=%async_computation.4 | async-start | bytes 1310720 | tf_op jit(solution)/shard_map/all_to_all | solution.py:69
  166.0 5.2 %collective-permute-start.11 = (f32[408,128]{1,0:T(8,128)S(1)}, f32[408,128]{1,0:T(8,128)S(1)}, u32[]{:S(2)}, u32[]{:S(2)}) collective-permute-start(f32[408,128]{1,0:T(8,128)S(1)} %get-tuple-element.69), channel_id=1, source_target_pairs={{0,0},{1,1},{2,2},{3,3},{4,64},{5,65},{6,66},{7,67},{8,128},{9,129... | collective-permute-start | bytes 626696 | tf_op jit(solution)/shard_map/ppermute | solution.py:65
  171.8 5.7 %collective-permute-done.11.kept = f32[408,128]{1,0:T(8,128)S(1)} collective-permute-done((f32[408,128]{1,0:T(8,128)S(1)}, f32[408,128]{1,0:T(8,128)S(1)}, u32[]{:S(2)}, u32[]{:S(2)}) %collective-permute-start.11) | collective-permute-done | bytes 208928 | tf_op jit(solution)/shard_map/ppermute | solution.py:65
  178.3 0.9 copy-done.13
  179.1 1.3 copy-done.18
  180.4 5.7 %edge_blocks.3 = (bf16[16,400,128]{2,1,0:T(8,128)(2,1)S(1)}, bf16[16,400,128]{2,1,0:T(8,128)(2,1)}, f32[400,128]{1,0:T(8,128)S(1)}, bf16[2560,128]{1,0:T(8,128)(...) custom-call(s32[128]{0:T(128)S(1)} %slice_bitcast_fusion.4.scal, s32[1]{0:T(128)} %bitcast.14.here, ...), custom_call_target="tpu_custom_call" | custom-call | flops 2000000000 | bytes 10000000 | tf_op jit(solution)/shard_map/edge_blocks/pallas_call | solution.py:224
  186.2 1.0 copy-done.2
  187.2 1.0 copy-done.4
  189.7 6.4 %collective-permute-start.12 = (bf16[16,400,128]{2,1,0:T(8,128)(2,1)}, bf16[16,400,128]{2,1,0:T(8,128)(2,1)}, u32[]{:S(2)}, u32[]{:S(2)}) collective-permute-start(bf16[16,400,128]{2,1,0:T(8,128)(2,1)} %get-tuple-element.73), channel_id=1, source_target_pairs={{0,32},{1,33},{2,34},{3,35},{4,36},{5,37},{6,38},{7,39},{8,40},{9,... | collective-permute-start | bytes 4915208 | tf_op jit(solution)/shard_map/ppermute | solution.py:65
  196.2 14.9 %all-to-all-start.5 = ((bf16[32,80,128]{2,1,0:T(8,128)(2,1)}), bf16[32,80,128]{2,1,0:T(8,128)(2,1)S(1)}, u32[]{:S(2)}, u32[]{:S(2)}) async-start(bf16[32,80,128]{2,1,0:T(8,128)(2,1)} %bitcast.65), calls=%async_computation.5 | async-start | bytes 1310720 | tf_op jit(solution)/shard_map/all_to_all | solution.py:69
  211.1 1.6 convert_element_type.75
  212.7 3.1 %add.64 = bf16[16,400,128]{2,1,0:T(8,128)(2,1)} add(bf16[16,400,128]{2,1,0:T(8,128)(2,1)S(1)} %get-tuple-element.72, bf16[16,400,128]{2,1,0:T(8,128)(2,1)} %collective-permute-done.12) | non-fusion elementwise | flops 819200 | bytes 4915200 | tf_op jit(solution)/shard_map/add | solution.py:427
  215.7 7.7 %all-to-all-done.5 = bf16[32,80,128]{2,1,0:T(8,128)(2,1)S(1)} async-done(((bf16[32,80,128]{2,1,0:T(8,128)(2,1)}), bf16[32,80,128]{2,1,0:T(8,128)(2,1)S(1)}, u32[]{:S(2)}, u32[]{:S(2)}) %all-to-all-start.5) | async-done | bytes 655392 | tf_op jit(solution)/shard_map/all_to_all | solution.py:69
  223.4 3.7 %all-to-all-start.6 = ((bf16[16,400,128]{2,1,0:T(8,128)(2,1)}), bf16[16,400,128]{2,1,0:T(8,128)(2,1)S(1)}, u32[]{:S(2)}, u32[]{:S(2)}) async-start(bf16[16,400,128]{2,1,0:T(8,128)(2,1)} %add.64), calls=%async_computation.6 | async-start | bytes 3276800 | tf_op jit(solution)/shard_map/all_to_all | solution.py:69
  227.1 6.6 %collective-permute-start.15 = (bf16[400,128]{1,0:T(8,128)(2,1)S(1)}, bf16[400,128]{1,0:T(8,128)(2,1)S(1)}, u32[]{:S(2)}, u32[]{:S(2)}) collective-permute-start(bf16[400,128]{1,0:T(8,128)(2,1)S(1)} %copy-done.21), channel_id=1, source_target_pairs={{16,0},{17,1},{18,2},{19,3},{80,64},{81,65},{82,66},{83,67},{144,1... | collective-permute-start | bytes 307208 | tf_op jit(solution)/shard_map/ppermute | solution.py:65
  233.8 2.0 collective-permute-start.13
  235.8 3.0 %collective-permute-done.13 = f32[80,128]{1,0:T(8,128)S(1)} collective-permute-done((f32[80,128]{1,0:T(8,128)S(1)}, f32[80,128]{1,0:T(8,128)S(1)}, u32[]{:S(2)}, u32[]{:S(2)}) %collective-permute-start.13) | collective-permute-done | bytes 40992 | tf_op jit(solution)/shard_map/ppermute | solution.py:65
  238.9 2.0 collective-permute-start.14
  240.9 4.2 %collective-permute-done.14 = f32[80,128]{1,0:T(8,128)S(1)} collective-permute-done((f32[80,128]{1,0:T(8,128)S(1)}, f32[80,128]{1,0:T(8,128)S(1)}, u32[]{:S(2)}, u32[]{:S(2)}) %collective-permute-start.14) | collective-permute-done | bytes 40992 | tf_op jit(solution)/shard_map/ppermute | solution.py:65
  245.7 5.8 %collective-permute-start.16 = (bf16[80,128]{1,0:T(8,128)(2,1)S(1)}, bf16[80,128]{1,0:T(8,128)(2,1)S(1)}, u32[]{:S(2)}, u32[]{:S(2)}) collective-permute-start(bf16[80,128]{1,0:T(8,128)(2,1)S(1)} %add.66), channel_id=1, source_target_pairs={{0,16},{1,17},{2,18},{3,19},{4,20},{5,21},{6,22},{7,23},{8,24},{9,... | collective-permute-start | bytes 61448 | tf_op jit(solution)/shard_map/ppermute | solution.py:65
  251.5 2.6 collective-permute-done.16
  254.2 9.4 %collective-permute-start.17 = (bf16[80,128]{1,0:T(8,128)(2,1)S(1)}, bf16[80,128]{1,0:T(8,128)(2,1)S(1)}, u32[]{:S(2)}, u32[]{:S(2)}) collective-permute-start(bf16[80,128]{1,0:T(8,128)(2,1)S(1)} %add_convert_fusion), channel_id=1, source_target_pairs={{0,256},{1,257},{2,258},{3,259},{4,260},{5,261},{6,262},{7,263},{8... | collective-permute-start | bytes 61448 | tf_op jit(solution)/shard_map/ppermute | solution.py:65
  263.6 3.8 %collective-permute-done.17 = bf16[80,128]{1,0:T(8,128)(2,1)S(1)} collective-permute-done((bf16[80,128]{1,0:T(8,128)(2,1)S(1)}, bf16[80,128]{1,0:T(8,128)(2,1)S(1)}, u32[]{:S(2)}, u32[]{:S(2)}) %collective-permute-start.17) | collective-permute-done | bytes 20512 | tf_op jit(solution)/shard_map/ppermute | solution.py:65
  267.4 1.0 broadcast_in_dim.32
  268.4 12.8 %all-to-all-start.7 = ((bf16[32,80,128]{2,1,0:T(8,128)(2,1)}), bf16[32,80,128]{2,1,0:T(8,128)(2,1)S(1)}, u32[]{:S(2)}, u32[]{:S(2)}) async-start(bf16[32,80,128]{2,1,0:T(8,128)(2,1)} %broadcast_in_dim.32), calls=%async_computation.7 | async-start | bytes 1310720 | tf_op jit(solution)/shard_map/all_to_all | solution.py:69
  281.2 0.9 copy-done.12
  282.1 1.1 fold_pieces.1
  283.2 5.7 %collective-permute-start.18 = (bf16[400,128]{1,0:T(8,128)(2,1)}, bf16[400,128]{1,0:T(8,128)(2,1)S(1)}, u32[]{:S(2)}, u32[]{:S(2)}) collective-permute-start(bf16[400,128]{1,0:T(8,128)(2,1)} %fold_pieces.1), channel_id=1, source_target_pairs={{0,0},{1,1},{2,2},{3,3},{4,64},{5,65},{6,66},{7,67},{8,128},{9,129... | collective-permute-start | bytes 307208 | tf_op jit(solution)/shard_map/ppermute | solution.py:65
  288.9 4.6 %all-to-all-done.7 = bf16[32,80,128]{2,1,0:T(8,128)(2,1)S(1)} async-done(((bf16[32,80,128]{2,1,0:T(8,128)(2,1)}), bf16[32,80,128]{2,1,0:T(8,128)(2,1)S(1)}, u32[]{:S(2)}, u32[]{:S(2)}) %all-to-all-start.7) | async-done | bytes 655392 | tf_op jit(solution)/shard_map/all_to_all | solution.py:69
  293.5 1.3 copy-done.5
  294.8 2.4 relation_update.1
  297.8 1.8 last_update.1
  (96 shorter events, 12.4 us)
Async XLA Ops:
  1.6 14.1 %collective-permute-start = (bf16[400,128]{1,0:T(8,128)(2,1)S(1)}, bf16[400,128]{1,0:T(8,128)(2,1)S(1)}, u32[]{:S(2)}, u32[]{:S(2)}) collective-permute-start(bf16[400,128]{1,0:T(8,128)(2,1)S(1)} %bitcast_convert_fusion), channel_id=1, source_target_pairs={{0,0},{1,1},{2,2},{3,3},{4,64},{5,65},{6,66},{7,67},{8,128},{9,129... | collective-permute-start | bytes 307208 | tf_op jit(solution)/shard_map/ppermute | solution.py:65
  15.7 2.1 copy-start.14
  17.8 10.5 %copy-start.25 = (f32[128]{0:T(128)S(1)}, f32[128]{0:T(128)}, u32[]{:S(2)}) copy-start(f32[128]{0:T(128)} %param.11) | copy-start | bytes 1540
  17.8 10.5 %copy-start.19 = (f32[128,400]{0,1:T(8,128)S(1)}, f32[128,400]{0,1:T(8,128)}, u32[]{:S(2)}) copy-start(f32[128,400]{0,1:T(8,128)} %param.10) | copy-start | bytes 614404
  17.8 18.0 %copy-start.23 = (s32[2,10,128]{2,0,1:T(2,128)S(1)}, s32[2,10,128]{2,0,1:T(2,128)}, u32[]{:S(2)}) copy-start(s32[2,10,128]{2,0,1:T(2,128)} %param.18) | copy-start | bytes 30724
  17.8 18.0 %copy-start.24 = (s32[2,10,128]{2,0,1:T(2,128)S(1)}, s32[2,10,128]{2,0,1:T(2,128)}, u32[]{:S(2)}) copy-start(s32[2,10,128]{2,0,1:T(2,128)} %param.17) | copy-start | bytes 30724
  17.8 31.9 %all-to-all-start = ((bf16[16,400,128]{2,1,0:T(8,128)(2,1)}), bf16[16,400,128]{2,1,0:T(8,128)(2,1)S(1)}, u32[]{:S(2)}, u32[]{:S(2)}) async-start(bf16[16,400,128]{2,1,0:T(8,128)(2,1)} %broadcast_in_dim.26), calls=%async_computation | async-start | bytes 3276800 | tf_op jit(solution)/shard_map/all_to_all | solution.py:69
  28.3 21.2 %collective-permute-start.2 = (f32[408,128]{1,0:T(8,128)S(1)}, f32[408,128]{1,0:T(8,128)S(1)}, u32[]{:S(2)}, u32[]{:S(2)}) collective-permute-start(f32[408,128]{1,0:T(8,128)S(1)} %pad_maximum_fusion), channel_id=1, source_target_pairs={{0,0},{1,1},{2,2},{3,3},{4,64},{5,65},{6,66},{7,67},{8,128},{9,129... | collective-permute-start | bytes 626696 | tf_op jit(solution)/shard_map/ppermute | solution.py:65
  35.9 13.6 %collective-permute-start.1 = (bf16[64,128]{1,0:T(8,128)(2,1)S(1)}, bf16[64,128]{1,0:T(8,128)(2,1)S(1)}, u32[]{:S(2)}, u32[]{:S(2)}) collective-permute-start(bf16[64,128]{1,0:T(8,128)(2,1)S(1)} %pad_maximum_fusion.2), channel_id=1, source_target_pairs={{0,0},{1,1},{2,2},{3,3},{4,64},{5,65},{6,66},{7,67},{8,128},{9,129... | collective-permute-start | bytes 49160 | tf_op jit(solution)/shard_map/ppermute | solution.py:65
  49.7 5.4 %collective-permute-start.3 = (bf16[16,400,128]{2,1,0:T(8,128)(2,1)S(1)}, bf16[16,400,128]{2,1,0:T(8,128)(2,1)S(1)}, u32[]{:S(2)}, u32[]{:S(2)}) collective-permute-start(bf16[16,400,128]{2,1,0:T(8,128)(2,1)S(1)} %all-to-all-done.half), channel_id=1, source_target_pairs={{0,32},{1,33},{2,34},{3,35},{4,36},{5,37},{6,38},{7,39},{8,40},{9,... | collective-permute-start | bytes 4915208 | tf_op jit(solution)/shard_map/ppermute | solution.py:65
  51.6 4.7 %copy-start.15 = (bf16[400,128]{1,0:T(8,128)(2,1)S(1)}, bf16[400,128]{1,0:T(8,128)(2,1)}, u32[]{:S(2)}) copy-start(bf16[400,128]{1,0:T(8,128)(2,1)} %copy-done.14) | copy-start | bytes 307204
  53.0 14.3 %copy-start = (f32[400,768]{1,0:T(8,128)}, f32[400,768]{1,0:T(8,128)S(1)}, u32[]{:S(2)}) copy-start(f32[400,768]{1,0:T(8,128)S(1)} %pad.26.rel) | copy-start | bytes 3686404
  55.1 1.2 copy-start.16
  56.3 1.4 copy-start.17
  67.4 0.8 copy-start.7
  68.2 0.7 copy-start.9
  68.9 13.7 %collective-permute-start.4 = (bf16[16,400,128]{2,1,0:T(8,128)(2,1)}, bf16[16,400,128]{2,1,0:T(8,128)(2,1)}, u32[]{:S(2)}, u32[]{:S(2)}) collective-permute-start(bf16[16,400,128]{2,1,0:T(8,128)(2,1)} %get-tuple-element.57), channel_id=1, source_target_pairs={{0,32},{1,33},{2,34},{3,35},{4,36},{5,37},{6,38},{7,39},{8,40},{9,... | collective-permute-start | bytes 4915208 | tf_op jit(solution)/shard_map/ppermute | solution.py:65
  70.8 24.1 %all-to-all-start.1 = ((bf16[32,80,128]{2,1,0:T(8,128)(2,1)}), bf16[32,80,128]{2,1,0:T(8,128)(2,1)S(1)}, u32[]{:S(2)}, u32[]{:S(2)}) async-start(bf16[32,80,128]{2,1,0:T(8,128)(2,1)} %bitcast.66), calls=%async_computation.1 | async-start | bytes 1310720 | tf_op jit(solution)/shard_map/all_to_all | solution.py:69
  85.7 36.0 %copy-start.10 = (f32[400,128]{1,0:T(8,128)S(1)}, f32[400,128]{1,0:T(8,128)}, u32[]{:S(2)}) copy-start(f32[400,128]{1,0:T(8,128)} %copy-done.9) | copy-start | bytes 614404
  94.9 26.8 %all-to-all-start.2 = ((bf16[16,400,128]{2,1,0:T(8,128)(2,1)}), bf16[16,400,128]{2,1,0:T(8,128)(2,1)S(1)}, u32[]{:S(2)}, u32[]{:S(2)}) async-start(bf16[16,400,128]{2,1,0:T(8,128)(2,1)} %add.59), calls=%async_computation.2 | async-start | bytes 3276800 | tf_op jit(solution)/shard_map/all_to_all | solution.py:69
  98.7 4.7 %collective-permute-start.5 = (f32[80,128]{1,0:T(8,128)S(1)}, f32[80,128]{1,0:T(8,128)S(1)}, u32[]{:S(2)}, u32[]{:S(2)}) collective-permute-start(f32[80,128]{1,0:T(8,128)S(1)} %convert_reduce_fusion.1), channel_id=1, source_target_pairs={{0,4},{1,5},{2,6},{3,7},{4,0},{5,1},{6,2},{7,3},{8,12},{9,13},{10,... | collective-permute-start | bytes 122888 | tf_op jit(solution)/shard_map/ppermute | solution.py:65
  103.5 6.4 %collective-permute-start.6 = (f32[80,128]{1,0:T(8,128)S(1)}, f32[80,128]{1,0:T(8,128)S(1)}, u32[]{:S(2)}, u32[]{:S(2)}) collective-permute-start(f32[80,128]{1,0:T(8,128)S(1)} %add.60), channel_id=1, source_target_pairs={{0,8},{1,9},{2,10},{3,11},{4,12},{5,13},{6,14},{7,15},{8,0},{9,1},... | collective-permute-start | bytes 122888 | tf_op jit(solution)/shard_map/ppermute | solution.py:65
  109.8 8.4 %collective-permute-start.7 = (bf16[80,128]{1,0:T(8,128)(2,1)S(1)}, bf16[80,128]{1,0:T(8,128)(2,1)S(1)}, u32[]{:S(2)}, u32[]{:S(2)}) collective-permute-start(bf16[80,128]{1,0:T(8,128)(2,1)S(1)} %add_convert_fusion.1), channel_id=1, source_target_pairs={{0,16},{1,17},{2,18},{3,19},{4,20},{5,21},{6,22},{7,23},{8,24},{9,... | collective-permute-start | bytes 61448 | tf_op jit(solution)/shard_map/ppermute | solution.py:65
  123.6 26.7 %all-to-all-start.3 = ((bf16[16,400,128]{2,1,0:T(8,128)(2,1)}), bf16[16,400,128]{2,1,0:T(8,128)(2,1)}, u32[]{:S(2)}, u32[]{:S(2)}) async-start(bf16[16,400,128]{2,1,0:T(8,128)(2,1)} %get-tuple-element.64), calls=%async_computation.3 | async-start | bytes 3276800 | tf_op jit(solution)/shard_map/all_to_all | solution.py:69
  128.7 49.6 %copy-start.1 = (f32[400,768]{1,0:T(8,128)S(1)}, f32[400,768]{1,0:T(8,128)}, u32[]{:S(2)}) copy-start(f32[400,768]{1,0:T(8,128)} %copy-done) | copy-start | bytes 3686404
  128.7 16.6 %collective-permute-start.9 = (bf16[80,128]{1,0:T(8,128)(2,1)S(1)}, bf16[80,128]{1,0:T(8,128)(2,1)S(1)}, u32[]{:S(2)}, u32[]{:S(2)}) collective-permute-start(bf16[80,128]{1,0:T(8,128)(2,1)S(1)} %convert_add_fusion.2), channel_id=1, source_target_pairs={{0,256},{1,257},{2,258},{3,259},{4,260},{5,261},{6,262},{7,263},{8... | collective-permute-start | bytes 61448 | tf_op jit(solution)/shard_map/ppermute | solution.py:65
  143.3 6.9 %collective-permute-start.8 = (bf16[432,128]{1,0:T(8,128)(2,1)S(1)}, bf16[432,128]{1,0:T(8,128)(2,1)S(1)}, u32[]{:S(2)}, u32[]{:S(2)}) collective-permute-start(bf16[432,128]{1,0:T(8,128)(2,1)S(1)} %pad_maximum_fusion.1), channel_id=1, source_target_pairs={{0,16},{1,17},{2,18},{3,19},{64,80},{65,81},{66,82},{67,83},{128,1... | collective-permute-start | bytes 331784 | tf_op jit(solution)/shard_map/ppermute | solution.py:65
  150.2 27.3 %collective-permute-start.10 = (bf16[16,400,128]{2,1,0:T(8,128)(2,1)}, bf16[16,400,128]{2,1,0:T(8,128)(2,1)}, u32[]{:S(2)}, u32[]{:S(2)}) collective-permute-start(bf16[16,400,128]{2,1,0:T(8,128)(2,1)} %all-to-all-done.3.half), channel_id=1, source_target_pairs={{0,32},{1,33},{2,34},{3,35},{4,36},{5,37},{6,38},{7,39},{8,40},{9,... | collective-permute-start | bytes 4915208 | tf_op jit(solution)/shard_map/ppermute | solution.py:65
  158.6 19.6 %all-to-all-start.4 = ((bf16[32,80,128]{2,1,0:T(8,128)(2,1)}), bf16[32,80,128]{2,1,0:T(8,128)(2,1)S(1)}, u32[]{:S(2)}, u32[]{:S(2)}) async-start(bf16[32,80,128]{2,1,0:T(8,128)(2,1)} %broadcast_in_dim.31), calls=%async_computation.4 | async-start | bytes 1310720 | tf_op jit(solution)/shard_map/all_to_all | solution.py:69
  166.0 11.6 %collective-permute-start.11 = (f32[408,128]{1,0:T(8,128)S(1)}, f32[408,128]{1,0:T(8,128)S(1)}, u32[]{:S(2)}, u32[]{:S(2)}) collective-permute-start(f32[408,128]{1,0:T(8,128)S(1)} %get-tuple-element.69), channel_id=1, source_target_pairs={{0,0},{1,1},{2,2},{3,3},{4,64},{5,65},{6,66},{7,67},{8,128},{9,129... | collective-permute-start | bytes 626696 | tf_op jit(solution)/shard_map/ppermute | solution.py:65
  177.5 0.7 copy-start.20
  178.3 0.9 copy-start.13
  179.1 1.3 copy-start.18
  186.2 1.0 copy-start.2
  187.2 1.0 copy-start.4
  188.2 0.8 copy-start.6
  189.1 0.7 copy-start.8
  189.7 22.9 %collective-permute-start.12 = (bf16[16,400,128]{2,1,0:T(8,128)(2,1)}, bf16[16,400,128]{2,1,0:T(8,128)(2,1)}, u32[]{:S(2)}, u32[]{:S(2)}) collective-permute-start(bf16[16,400,128]{2,1,0:T(8,128)(2,1)} %get-tuple-element.73), channel_id=1, source_target_pairs={{0,32},{1,33},{2,34},{3,35},{4,36},{5,37},{6,38},{7,39},{8,40},{9,... | collective-permute-start | bytes 4915208 | tf_op jit(solution)/shard_map/ppermute | solution.py:65
  196.2 27.2 %all-to-all-start.5 = ((bf16[32,80,128]{2,1,0:T(8,128)(2,1)}), bf16[32,80,128]{2,1,0:T(8,128)(2,1)S(1)}, u32[]{:S(2)}, u32[]{:S(2)}) async-start(bf16[32,80,128]{2,1,0:T(8,128)(2,1)} %bitcast.65), calls=%async_computation.5 | async-start | bytes 1310720 | tf_op jit(solution)/shard_map/all_to_all | solution.py:69
  215.7 11.4 %copy-start.21 = (bf16[400,128]{1,0:T(8,128)(2,1)S(1)}, bf16[400,128]{1,0:T(8,128)(2,1)}, u32[]{:S(2)}) copy-start(bf16[400,128]{1,0:T(8,128)(2,1)} %convert_element_type.75) | copy-start | bytes 307204
  223.4 44.0 %all-to-all-start.6 = ((bf16[16,400,128]{2,1,0:T(8,128)(2,1)}), bf16[16,400,128]{2,1,0:T(8,128)(2,1)S(1)}, u32[]{:S(2)}, u32[]{:S(2)}) async-start(bf16[16,400,128]{2,1,0:T(8,128)(2,1)} %add.64), calls=%async_computation.6 | async-start | bytes 3276800 | tf_op jit(solution)/shard_map/all_to_all | solution.py:69
  227.1 17.9 %collective-permute-start.15 = (bf16[400,128]{1,0:T(8,128)(2,1)S(1)}, bf16[400,128]{1,0:T(8,128)(2,1)S(1)}, u32[]{:S(2)}, u32[]{:S(2)}) collective-permute-start(bf16[400,128]{1,0:T(8,128)(2,1)S(1)} %copy-done.21), channel_id=1, source_target_pairs={{16,0},{17,1},{18,2},{19,3},{80,64},{81,65},{82,66},{83,67},{144,1... | collective-permute-start | bytes 307208 | tf_op jit(solution)/shard_map/ppermute | solution.py:65
  233.8 5.0 %collective-permute-start.13 = (f32[80,128]{1,0:T(8,128)S(1)}, f32[80,128]{1,0:T(8,128)S(1)}, u32[]{:S(2)}, u32[]{:S(2)}) collective-permute-start(f32[80,128]{1,0:T(8,128)S(1)} %convert_reduce_fusion), channel_id=1, source_target_pairs={{0,4},{1,5},{2,6},{3,7},{4,0},{5,1},{6,2},{7,3},{8,12},{9,13},{10,... | collective-permute-start | bytes 122888 | tf_op jit(solution)/shard_map/ppermute | solution.py:65
  238.9 6.2 %collective-permute-start.14 = (f32[80,128]{1,0:T(8,128)S(1)}, f32[80,128]{1,0:T(8,128)S(1)}, u32[]{:S(2)}, u32[]{:S(2)}) collective-permute-start(f32[80,128]{1,0:T(8,128)S(1)} %add.65), channel_id=1, source_target_pairs={{0,8},{1,9},{2,10},{3,11},{4,12},{5,13},{6,14},{7,15},{8,0},{9,1},... | collective-permute-start | bytes 122888 | tf_op jit(solution)/shard_map/ppermute | solution.py:65
  245.1 0.6 copy-start.11
  245.7 8.4 %collective-permute-start.16 = (bf16[80,128]{1,0:T(8,128)(2,1)S(1)}, bf16[80,128]{1,0:T(8,128)(2,1)S(1)}, u32[]{:S(2)}, u32[]{:S(2)}) collective-permute-start(bf16[80,128]{1,0:T(8,128)(2,1)S(1)} %add.66), channel_id=1, source_target_pairs={{0,16},{1,17},{2,18},{3,19},{4,20},{5,21},{6,22},{7,23},{8,24},{9,... | collective-permute-start | bytes 61448 | tf_op jit(solution)/shard_map/ppermute | solution.py:65
  254.2 13.2 %collective-permute-start.17 = (bf16[80,128]{1,0:T(8,128)(2,1)S(1)}, bf16[80,128]{1,0:T(8,128)(2,1)S(1)}, u32[]{:S(2)}, u32[]{:S(2)}) collective-permute-start(bf16[80,128]{1,0:T(8,128)(2,1)S(1)} %add_convert_fusion), channel_id=1, source_target_pairs={{0,256},{1,257},{2,258},{3,259},{4,260},{5,261},{6,262},{7,263},{8... | collective-permute-start | bytes 61448 | tf_op jit(solution)/shard_map/ppermute | solution.py:65
  268.4 25.1 %copy-start.3 = (f32[400,768]{1,0:T(8,128)S(1)}, f32[400,768]{1,0:T(8,128)}, u32[]{:S(2)}) copy-start(f32[400,768]{1,0:T(8,128)} %copy-done.2) | copy-start | bytes 3686404
  268.4 25.1 %all-to-all-start.7 = ((bf16[32,80,128]{2,1,0:T(8,128)(2,1)}), bf16[32,80,128]{2,1,0:T(8,128)(2,1)S(1)}, u32[]{:S(2)}, u32[]{:S(2)}) async-start(bf16[32,80,128]{2,1,0:T(8,128)(2,1)} %broadcast_in_dim.32), calls=%async_computation.7 | async-start | bytes 1310720 | tf_op jit(solution)/shard_map/all_to_all | solution.py:69
  281.2 0.9 copy-start.12
  283.2 13.9 %collective-permute-start.18 = (bf16[400,128]{1,0:T(8,128)(2,1)}, bf16[400,128]{1,0:T(8,128)(2,1)S(1)}, u32[]{:S(2)}, u32[]{:S(2)}) collective-permute-start(bf16[400,128]{1,0:T(8,128)(2,1)} %fold_pieces.1), channel_id=1, source_target_pairs={{0,0},{1,1},{2,2},{3,3},{4,64},{5,65},{6,66},{7,67},{8,128},{9,129... | collective-permute-start | bytes 307208 | tf_op jit(solution)/shard_map/ppermute | solution.py:65
  293.5 1.3 copy-start.5
  297.2 0.6 copy-start.22

commit v7 on v5

--- a/solution.py
+++ b/solution.py
@@ -399,8 +399,10 @@
     summed, lhs = together(mine + send(theirs, OTHER), lhs.astype(BF16))
     summed, rel_pieces = together(summed, rel_pieces)
     rel_mine = jnp.sum(rel_pieces, 0, dtype=F32)
-    rel_mine, lhs = together(z_step(z_step(rel_mine, 1, F32), 2, F32), send(lhs, PREVIOUS))
-    rel_mine = z_step(z_step(rel_mine, 4, BF16), 8, BF16)
+    rel_mine, lhs = together(z_step(rel_mine, 1, F32), lhs)
+    rel_mine = z_step(z_step(rel_mine, 2, F32), 4, BF16)
+    rel_mine, lhs = together(rel_mine, send(lhs, PREVIOUS))
+    rel_mine = z_step(rel_mine, 8, BF16)
     pieces, rel_mine = together(exchange(summed, SHEETS), rel_mine)
     grads = send(fold(pieces, lhs), TURN)
     rel, rel_state = relation_update(spread_relations(rel_mine), rel, rel_state, count)

time: 297 us -> 299 us (level)
  waiting for transfers between devices: 70.9 us -> 80.2 us
  starting transfers between devices: 172 us -> 167 us
    ppermute x19, waiting for transfers between devices: 41.2 us -> 46.1 us  [send(): return lax.ppermute(value, AXES, pairs)]
    all_to_all x8, waiting for transfers between devices: 29.7 us -> 34.1 us  [exchange(): lax.all_to_all(value, AXES, 0, 0, axis_index_groups=groups, tiled=True)]
    ppermute x19, starting transfers between devices: 103 us -> 98.6 us  [send(): return lax.ppermute(value, AXES, pairs)]
  transfers between devices with their start and end apart: 27 -> 27, of which waited for: 16 -> 17; matrix products, arithmetic and copies ran while one was open for 5% -> 5% of each run, Pallas kernels for 2% -> 1%
where the time goes in v7:
time: 299 us; the launch traced here: 296 us
  starting transfers between devices  167 us (56%)
  waiting for transfers between devices  80.2 us (27%)
  Pallas kernels  18.2 us (6%)
  local copies, waits for them, and re-layouts  17 us (6%)
  other arithmetic  12.6 us (4%)
    ppermute x19, starting transfers between devices, send(): return lax.ppermute(value, AXES, pairs)  98.6 us
    all_to_all x8, starting transfers between devices, exchange(): lax.all_to_all(value, AXES, 0, 0, axis_index_groups=groups, tiled=True)  68.7 us
    ppermute x19, waiting for transfers between devices, send(): return lax.ppermute(value, AXES, pairs)  46.1 us
    all_to_all x8, waiting for transfers between devices, exchange(): lax.all_to_all(value, AXES, 0, 0, axis_index_groups=groups, tiled=True)  34.1 us
    pallas_call x2, Pallas kernels, run_blocks(): pl.pallas_call(blocks_kernel, out_shape=(jax.ShapeDtypeStruct((16, width,...  11.5 us
    unnamed x34, local copies, waits for them, and re-layouts  8.46 us
  transfers between devices with their start and end apart: 27, of which 17 were waited for; matrix products, arithmetic and copies ran while one was open for 5% of the time, Pallas kernels for 1%

profile of v7, /device:TPU:1, one launch (start us, length us, event | category | flops | bytes accessed | tf_op | source)
XLA Modules:
  0.0 296.4 jit_solution(15239983511461480381)
XLA Ops:
  0.6 0.9 bitcast_convert_fusion
  1.6 10.2 %collective-permute-start = (bf16[400,128]{1,0:T(8,128)(2,1)S(1)}, bf16[400,128]{1,0:T(8,128)(2,1)S(1)}, u32[]{:S(2)}, u32[]{:S(2)}) collective-permute-start(bf16[400,128]{1,0:T(8,128)(2,1)S(1)} %bitcast_convert_fusion), channel_id=1, source_target_pairs={{0,0},{1,1},{2,2},{3,3},{4,64},{5,65},{6,66},{7,67},{8,128},{9,129... | collective-permute-start | bytes 307208 | tf_op jit(solution)/shard_map/ppermute | solution.py:65
  14.3 0.8 fusion.12
  16.4 1.4 broadcast_in_dim.29
  17.8 10.4 %all-to-all-start = ((bf16[16,400,128]{2,1,0:T(8,128)(2,1)}), bf16[16,400,128]{2,1,0:T(8,128)(2,1)S(1)}, u32[]{:S(2)}, u32[]{:S(2)}) async-start(bf16[16,400,128]{2,1,0:T(8,128)(2,1)} %broadcast_in_dim.29), calls=%async_computation | async-start | bytes 3276800 | tf_op jit(solution)/shard_map/all_to_all | solution.py:69
  28.3 5.9 %collective-permute-start.2 = (f32[408,128]{1,0:T(8,128)S(1)}, f32[408,128]{1,0:T(8,128)S(1)}, u32[]{:S(2)}, u32[]{:S(2)}) collective-permute-start(f32[408,128]{1,0:T(8,128)S(1)} %pad_maximum_fusion), channel_id=1, source_target_pairs={{0,0},{1,1},{2,2},{3,3},{4,64},{5,65},{6,66},{7,67},{8,128},{9,129... | collective-permute-start | bytes 626696 | tf_op jit(solution)/shard_map/ppermute | solution.py:65
  35.9 3.5 %collective-permute-start.1 = (bf16[64,128]{1,0:T(8,128)(2,1)S(1)}, bf16[64,128]{1,0:T(8,128)(2,1)S(1)}, u32[]{:S(2)}, u32[]{:S(2)}) collective-permute-start(bf16[64,128]{1,0:T(8,128)(2,1)S(1)} %pad_maximum_fusion.2), channel_id=1, source_target_pairs={{0,0},{1,1},{2,2},{3,3},{4,64},{5,65},{6,66},{7,67},{8,128},{9,129... | collective-permute-start | bytes 49160 | tf_op jit(solution)/shard_map/ppermute | solution.py:65
  39.4 10.1 %collective-permute-done.1 = bf16[64,128]{1,0:T(8,128)(2,1)S(1)} collective-permute-done((bf16[64,128]{1,0:T(8,128)(2,1)S(1)}, bf16[64,128]{1,0:T(8,128)(2,1)S(1)}, u32[]{:S(2)}, u32[]{:S(2)}) %collective-permute-start.1) | collective-permute-done | bytes 16416 | tf_op jit(solution)/shard_map/ppermute | solution.py:65
  49.7 1.9 collective-permute-start.3
  51.6 1.4 pad.26.rel
  53.0 2.2 collective-permute-done.3.other
  55.2 5.6 %edge_blocks.2 = (bf16[16,400,128]{2,1,0:T(8,128)(2,1)S(1)}, bf16[16,400,128]{2,1,0:T(8,128)(2,1)}, f32[400,128]{1,0:T(8,128)S(1)}, bf16[2560,128]{1,0:T(8,128)(2,1)}) custom-call(s32[128]{0:T(128)S(1)} %slice_bitcast_fusion.5.scal, s32[1]{0:T(128)} %bitcast.14.here, s32[32,128]{1,0:T(8,128)S(1)} %get-tuple-element.101.lists, ...), custom_call_target="tpu_custom_call" | custom-call | flops 2000000000 | bytes 10000000 | tf_op jit(solution)/shard_map/edge_blocks/pallas_call | solution.py:200
  60.8 1.1 copy-done
  61.9 2.0 collective-permute-start.4
  64.0 13.5 %all-to-all-start.1 = ((bf16[32,80,128]{2,1,0:T(8,128)(2,1)}), bf16[32,80,128]{2,1,0:T(8,128)(2,1)S(1)}, u32[]{:S(2)}, u32[]{:S(2)}) async-start(bf16[32,80,128]{2,1,0:T(8,128)(2,1)} %bitcast.16), calls=%async_computation.1 | async-start | bytes 1310720 | tf_op jit(solution)/shard_map/all_to_all | solution.py:69
  77.5 3.6 %add.59 = bf16[16,400,128]{2,1,0:T(8,128)(2,1)} add(bf16[16,400,128]{2,1,0:T(8,128)(2,1)} %copy-done, bf16[16,400,128]{2,1,0:T(8,128)(2,1)} %collective-permute-done.4) | non-fusion elementwise | flops 819200 | bytes 4915200 | tf_op jit(solution)/shard_map/add | solution.py:386
  81.1 8.7 %all-to-all-done.1 = bf16[32,80,128]{2,1,0:T(8,128)(2,1)S(1)} async-done(((bf16[32,80,128]{2,1,0:T(8,128)(2,1)}), bf16[32,80,128]{2,1,0:T(8,128)(2,1)S(1)}, u32[]{:S(2)}, u32[]{:S(2)}) %all-to-all-start.1) | async-done | bytes 655392 | tf_op jit(solution)/shard_map/all_to_all | solution.py:69
  89.8 0.8 copy-done.10
  90.6 3.7 %all-to-all-start.2 = ((bf16[16,400,128]{2,1,0:T(8,128)(2,1)}), bf16[16,400,128]{2,1,0:T(8,128)(2,1)S(1)}, u32[]{:S(2)}, u32[]{:S(2)}) async-start(bf16[16,400,128]{2,1,0:T(8,128)(2,1)} %add.59), calls=%async_computation.2 | async-start | bytes 3276800 | tf_op jit(solution)/shard_map/all_to_all | solution.py:69
  94.4 1.2 convert_reduce_fusion.1
  95.5 1.9 collective-permute-start.5
  97.5 3.1 %collective-permute-done.5 = f32[80,128]{1,0:T(8,128)S(1)} collective-permute-done((f32[80,128]{1,0:T(8,128)S(1)}, f32[80,128]{1,0:T(8,128)S(1)}, u32[]{:S(2)}, u32[]{:S(2)}) %collective-permute-start.5) | collective-permute-done | bytes 40992 | tf_op jit(solution)/shard_map/ppermute | solution.py:65
  100.6 6.1 %collective-permute-start.6 = (f32[80,128]{1,0:T(8,128)S(1)}, f32[80,128]{1,0:T(8,128)S(1)}, u32[]{:S(2)}, u32[]{:S(2)}) collective-permute-start(f32[80,128]{1,0:T(8,128)S(1)} %add.60), channel_id=1, source_target_pairs={{0,8},{1,9},{2,10},{3,11},{4,12},{5,13},{6,14},{7,15},{8,0},{9,1},... | collective-permute-start | bytes 122888 | tf_op jit(solution)/shard_map/ppermute | solution.py:65
  106.7 1.7 collective-permute-done.6
  108.4 7.0 %collective-permute-start.7 = (bf16[80,128]{1,0:T(8,128)(2,1)S(1)}, bf16[80,128]{1,0:T(8,128)(2,1)S(1)}, u32[]{:S(2)}, u32[]{:S(2)}) collective-permute-start(bf16[80,128]{1,0:T(8,128)(2,1)S(1)} %add_convert_fusion.1), channel_id=1, source_target_pairs={{0,16},{1,17},{2,18},{3,19},{4,20},{5,21},{6,22},{7,23},{8,24},{9,... | collective-permute-start | bytes 61448 | tf_op jit(solution)/shard_map/ppermute | solution.py:65
  115.4 1.5 collective-permute-done.7
  118.6 1.4 broadcast_in_dim.34
  119.9 6.3 %all-to-all-start.3 = ((bf16[16,400,128]{2,1,0:T(8,128)(2,1)}), bf16[16,400,128]{2,1,0:T(8,128)(2,1)}, u32[]{:S(2)}, u32[]{:S(2)}) async-start(bf16[16,400,128]{2,1,0:T(8,128)(2,1)} %broadcast_in_dim.34), calls=%async_computation.3 | async-start | bytes 3276800 | tf_op jit(solution)/shard_map/all_to_all | solution.py:69
  126.2 16.0 %collective-permute-start.9 = (bf16[80,128]{1,0:T(8,128)(2,1)S(1)}, bf16[80,128]{1,0:T(8,128)(2,1)S(1)}, u32[]{:S(2)}, u32[]{:S(2)}) collective-permute-start(bf16[80,128]{1,0:T(8,128)(2,1)S(1)} %convert_add_fusion.3), channel_id=1, source_target_pairs={{0,256},{1,257},{2,258},{3,259},{4,260},{5,261},{6,262},{7,263},{8... | collective-permute-start | bytes 61448 | tf_op jit(solution)/shard_map/ppermute | solution.py:65
  142.3 1.9 collective-permute-start.8
  144.2 4.7 %collective-permute-done.8 = bf16[432,128]{1,0:T(8,128)(2,1)S(1)} collective-permute-done((bf16[432,128]{1,0:T(8,128)(2,1)S(1)}, bf16[432,128]{1,0:T(8,128)(2,1)S(1)}, u32[]{:S(2)}, u32[]{:S(2)}) %collective-permute-start.8) | collective-permute-done | bytes 110624 | tf_op jit(solution)/shard_map/ppermute | solution.py:65
  149.0 7.1 %collective-permute-start.10 = (bf16[16,400,128]{2,1,0:T(8,128)(2,1)}, bf16[16,400,128]{2,1,0:T(8,128)(2,1)}, u32[]{:S(2)}, u32[]{:S(2)}) collective-permute-start(bf16[16,400,128]{2,1,0:T(8,128)(2,1)} %all-to-all-done.3.half), channel_id=1, source_target_pairs={{0,32},{1,33},{2,34},{3,35},{4,36},{5,37},{6,38},{7,39},{8,40},{9,... | collective-permute-start | bytes 4915208 | tf_op jit(solution)/shard_map/ppermute | solution.py:65
  156.1 0.9 broadcast_in_dim.35
  157.0 7.3 %all-to-all-start.4 = ((bf16[32,80,128]{2,1,0:T(8,128)(2,1)}), bf16[32,80,128]{2,1,0:T(8,128)(2,1)S(1)}, u32[]{:S(2)}, u32[]{:S(2)}) async-start(bf16[32,80,128]{2,1,0:T(8,128)(2,1)} %broadcast_in_dim.35), calls=%async_computation.4 | async-start | bytes 1310720 | tf_op jit(solution)/shard_map/all_to_all | solution.py:69
  164.4 5.1 %collective-permute-start.11 = (f32[408,128]{1,0:T(8,128)S(1)}, f32[408,128]{1,0:T(8,128)S(1)}, u32[]{:S(2)}, u32[]{:S(2)}) collective-permute-start(f32[408,128]{1,0:T(8,128)S(1)} %copy-done.9), channel_id=1, source_target_pairs={{0,0},{1,1},{2,2},{3,3},{4,64},{5,65},{6,66},{7,67},{8,128},{9,129... | collective-permute-start | bytes 626696 | tf_op jit(solution)/shard_map/ppermute | solution.py:65
  169.5 7.1 %all-to-all-done.4 = bf16[32,80,128]{2,1,0:T(8,128)(2,1)S(1)} async-done(((bf16[32,80,128]{2,1,0:T(8,128)(2,1)}), bf16[32,80,128]{2,1,0:T(8,128)(2,1)S(1)}, u32[]{:S(2)}, u32[]{:S(2)}) %all-to-all-start.4) | async-done | bytes 655392 | tf_op jit(solution)/shard_map/all_to_all | solution.py:69
  176.6 1.3 copy-done.1
  177.9 0.9 relation_update.2
  178.9 1.0 copy-done.4
  179.9 5.9 %edge_blocks.3 = (bf16[16,400,128]{2,1,0:T(8,128)(2,1)S(1)}, bf16[16,400,128]{2,1,0:T(8,128)(2,1)}, f32[400,128]{1,0:T(8,128)S(1)}, bf16[2560,128]{1,0:T(8,128)(2,1)}) custom-call(s32[128]{0:T(128)S(1)} %slice_bitcast_fusion.4.scal, s32[1]{0:T(128)} %bitcast.14.here, s32[32,128]{1,0:T(8,128)S(1)} %slice_convert_fusion.lists, ...), custom_call_target="tpu_custom_call" | custom-call | flops 2000000000 | bytes 10000000 | tf_op jit(solution)/shard_map/edge_blocks/pallas_call | solution.py:200
  185.9 3.2 %collective-permute-start.12 = (bf16[16,400,128]{2,1,0:T(8,128)(2,1)}, bf16[16,400,128]{2,1,0:T(8,128)(2,1)}, u32[]{:S(2)}, u32[]{:S(2)}) collective-permute-start(bf16[16,400,128]{2,1,0:T(8,128)(2,1)} %get-tuple-element.74), channel_id=1, source_target_pairs={{0,32},{1,33},{2,34},{3,35},{4,36},{5,37},{6,38},{7,39},{8,40},{9,... | collective-permute-start | bytes 4915208 | tf_op jit(solution)/shard_map/ppermute | solution.py:65
  189.0 13.9 %all-to-all-start.5 = ((bf16[32,80,128]{2,1,0:T(8,128)(2,1)}), bf16[32,80,128]{2,1,0:T(8,128)(2,1)S(1)}, u32[]{:S(2)}, u32[]{:S(2)}) async-start(bf16[32,80,128]{2,1,0:T(8,128)(2,1)} %bitcast.20), calls=%async_computation.5 | async-start | bytes 1310720 | tf_op jit(solution)/shard_map/all_to_all | solution.py:69
  203.0 3.0 %add.64 = bf16[16,400,128]{2,1,0:T(8,128)(2,1)} add(bf16[16,400,128]{2,1,0:T(8,128)(2,1)S(1)} %get-tuple-element.73, bf16[16,400,128]{2,1,0:T(8,128)(2,1)} %collective-permute-done.12) | non-fusion elementwise | flops 819200 | bytes 4915200 | tf_op jit(solution)/shard_map/add | solution.py:399
  206.0 9.2 %all-to-all-done.5 = bf16[32,80,128]{2,1,0:T(8,128)(2,1)S(1)} async-done(((bf16[32,80,128]{2,1,0:T(8,128)(2,1)}), bf16[32,80,128]{2,1,0:T(8,128)(2,1)S(1)}, u32[]{:S(2)}, u32[]{:S(2)}) %all-to-all-start.5) | async-done | bytes 655392 | tf_op jit(solution)/shard_map/all_to_all | solution.py:69
  215.3 3.7 %all-to-all-start.6 = ((bf16[16,400,128]{2,1,0:T(8,128)(2,1)}), bf16[16,400,128]{2,1,0:T(8,128)(2,1)S(1)}, u32[]{:S(2)}, u32[]{:S(2)}) async-start(bf16[16,400,128]{2,1,0:T(8,128)(2,1)} %add.64), calls=%async_computation.6 | async-start | bytes 3276800 | tf_op jit(solution)/shard_map/all_to_all | solution.py:69
  219.1 6.1 %collective-permute-start.13 = (f32[80,128]{1,0:T(8,128)S(1)}, f32[80,128]{1,0:T(8,128)S(1)}, u32[]{:S(2)}, u32[]{:S(2)}) collective-permute-start(f32[80,128]{1,0:T(8,128)S(1)} %convert_reduce_fusion), channel_id=1, source_target_pairs={{0,4},{1,5},{2,6},{3,7},{4,0},{5,1},{6,2},{7,3},{8,12},{9,13},{10,... | collective-permute-start | bytes 122888 | tf_op jit(solution)/shard_map/ppermute | solution.py:65
  225.2 1.7 collective-permute-done.13
  226.9 3.3 %collective-permute-start.14 = (f32[80,128]{1,0:T(8,128)S(1)}, f32[80,128]{1,0:T(8,128)S(1)}, u32[]{:S(2)}, u32[]{:S(2)}) collective-permute-start(f32[80,128]{1,0:T(8,128)S(1)} %add.65), channel_id=1, source_target_pairs={{0,8},{1,9},{2,10},{3,11},{4,12},{5,13},{6,14},{7,15},{8,0},{9,1},... | collective-permute-start | bytes 122888 | tf_op jit(solution)/shard_map/ppermute | solution.py:65
  230.2 2.6 collective-permute-done.14
  232.8 3.4 %collective-permute-start.15 = (bf16[80,128]{1,0:T(8,128)(2,1)S(1)}, bf16[80,128]{1,0:T(8,128)(2,1)S(1)}, u32[]{:S(2)}, u32[]{:S(2)}) collective-permute-start(bf16[80,128]{1,0:T(8,128)(2,1)S(1)} %add_convert_fusion), channel_id=1, source_target_pairs={{0,16},{1,17},{2,18},{3,19},{4,20},{5,21},{6,22},{7,23},{8,24},{9,... | collective-permute-start | bytes 61448 | tf_op jit(solution)/shard_map/ppermute | solution.py:65
  236.3 4.1 %collective-permute-start.16 = (bf16[400,128]{1,0:T(8,128)(2,1)S(1)}, bf16[400,128]{1,0:T(8,128)(2,1)S(1)}, u32[]{:S(2)}, u32[]{:S(2)}) collective-permute-start(bf16[400,128]{1,0:T(8,128)(2,1)S(1)} %convert_element_type.75), channel_id=1, source_target_pairs={{16,0},{17,1},{18,2},{19,3},{80,64},{81,65},{82,66},{83,67},{144,1... | collective-permute-start | bytes 307208 | tf_op jit(solution)/shard_map/ppermute | solution.py:65
  240.3 0.9 collective-permute-done.15
  241.3 12.3 %collective-permute-done.16.more = bf16[400,128]{1,0:T(8,128)(2,1)S(1)} collective-permute-done((bf16[400,128]{1,0:T(8,128)(2,1)S(1)}, bf16[400,128]{1,0:T(8,128)(2,1)S(1)}, u32[]{:S(2)}, u32[]{:S(2)}) %collective-permute-start.16) | collective-permute-done | bytes 102432 | tf_op jit(solution)/shard_map/ppermute | solution.py:65
  254.2 7.9 %collective-permute-start.17 = (bf16[80,128]{1,0:T(8,128)(2,1)S(1)}, bf16[80,128]{1,0:T(8,128)(2,1)S(1)}, u32[]{:S(2)}, u32[]{:S(2)}) collective-permute-start(bf16[80,128]{1,0:T(8,128)(2,1)S(1)} %convert_add_fusion.1), channel_id=1, source_target_pairs={{0,256},{1,257},{2,258},{3,259},{4,260},{5,261},{6,262},{7,263},{8... | collective-permute-start | bytes 61448 | tf_op jit(solution)/shard_map/ppermute | solution.py:65
  262.1 5.3 %collective-permute-done.17 = bf16[80,128]{1,0:T(8,128)(2,1)S(1)} collective-permute-done((bf16[80,128]{1,0:T(8,128)(2,1)S(1)}, bf16[80,128]{1,0:T(8,128)(2,1)S(1)}, u32[]{:S(2)}, u32[]{:S(2)}) %collective-permute-start.17) | collective-permute-done | bytes 20512 | tf_op jit(solution)/shard_map/ppermute | solution.py:65
  267.4 0.9 broadcast_in_dim.36
  268.4 9.7 %all-to-all-start.7 = ((bf16[32,80,128]{2,1,0:T(8,128)(2,1)}), bf16[32,80,128]{2,1,0:T(8,128)(2,1)S(1)}, u32[]{:S(2)}, u32[]{:S(2)}) async-start(bf16[32,80,128]{2,1,0:T(8,128)(2,1)} %broadcast_in_dim.36), calls=%async_computation.7 | async-start | bytes 1310720 | tf_op jit(solution)/shard_map/all_to_all | solution.py:69
  278.1 0.9 copy-done.7
  279.0 1.1 fold_pieces.1
  280.1 1.9 collective-permute-start.18
  282.0 8.3 %all-to-all-done.7 = bf16[32,80,128]{2,1,0:T(8,128)(2,1)S(1)} async-done(((bf16[32,80,128]{2,1,0:T(8,128)(2,1)}), bf16[32,80,128]{2,1,0:T(8,128)(2,1)S(1)}, u32[]{:S(2)}, u32[]{:S(2)}) %all-to-all-start.7) | async-done | bytes 655392 | tf_op jit(solution)/shard_map/all_to_all | solution.py:69
  290.4 1.3 copy-done.5
  291.7 2.4 relation_update.3
  294.7 1.8 last_update.1
  (80 shorter events, 8.8 us)
Async XLA Ops:
  1.6 14.1 %collective-permute-start = (bf16[400,128]{1,0:T(8,128)(2,1)S(1)}, bf16[400,128]{1,0:T(8,128)(2,1)S(1)}, u32[]{:S(2)}, u32[]{:S(2)}) collective-permute-start(bf16[400,128]{1,0:T(8,128)(2,1)S(1)} %bitcast_convert_fusion), channel_id=1, source_target_pairs={{0,0},{1,1},{2,2},{3,3},{4,64},{5,65},{6,66},{7,67},{8,128},{9,129... | collective-permute-start | bytes 307208 | tf_op jit(solution)/shard_map/ppermute | solution.py:65
  17.8 10.5 %copy-start.16 = (f32[128]{0:T(128)S(1)}, f32[128]{0:T(128)}, u32[]{:S(2)}) copy-start(f32[128]{0:T(128)} %param.11) | copy-start | bytes 1540
  17.8 10.5 %copy-start.11 = (f32[128,400]{0,1:T(8,128)S(1)}, f32[128,400]{0,1:T(8,128)}, u32[]{:S(2)}) copy-start(f32[128,400]{0,1:T(8,128)} %param.10) | copy-start | bytes 614404
  17.8 18.0 %copy-start.14 = (s32[2,10,128]{2,0,1:T(2,128)S(1)}, s32[2,10,128]{2,0,1:T(2,128)}, u32[]{:S(2)}) copy-start(s32[2,10,128]{2,0,1:T(2,128)} %param.18) | copy-start | bytes 30724
  17.8 18.0 %copy-start.15 = (s32[2,10,128]{2,0,1:T(2,128)S(1)}, s32[2,10,128]{2,0,1:T(2,128)}, u32[]{:S(2)}) copy-start(s32[2,10,128]{2,0,1:T(2,128)} %param.17) | copy-start | bytes 30724
  17.8 31.9 %all-to-all-start = ((bf16[16,400,128]{2,1,0:T(8,128)(2,1)}), bf16[16,400,128]{2,1,0:T(8,128)(2,1)S(1)}, u32[]{:S(2)}, u32[]{:S(2)}) async-start(bf16[16,400,128]{2,1,0:T(8,128)(2,1)} %broadcast_in_dim.29), calls=%async_computation | async-start | bytes 3276800 | tf_op jit(solution)/shard_map/all_to_all | solution.py:69
  28.3 21.2 %collective-permute-start.2 = (f32[408,128]{1,0:T(8,128)S(1)}, f32[408,128]{1,0:T(8,128)S(1)}, u32[]{:S(2)}, u32[]{:S(2)}) collective-permute-start(f32[408,128]{1,0:T(8,128)S(1)} %pad_maximum_fusion), channel_id=1, source_target_pairs={{0,0},{1,1},{2,2},{3,3},{4,64},{5,65},{6,66},{7,67},{8,128},{9,129... | collective-permute-start | bytes 626696 | tf_op jit(solution)/shard_map/ppermute | solution.py:65
  35.9 13.6 %collective-permute-start.1 = (bf16[64,128]{1,0:T(8,128)(2,1)S(1)}, bf16[64,128]{1,0:T(8,128)(2,1)S(1)}, u32[]{:S(2)}, u32[]{:S(2)}) collective-permute-start(bf16[64,128]{1,0:T(8,128)(2,1)S(1)} %pad_maximum_fusion.2), channel_id=1, source_target_pairs={{0,0},{1,1},{2,2},{3,3},{4,64},{5,65},{6,66},{7,67},{8,128},{9,129... | collective-permute-start | bytes 49160 | tf_op jit(solution)/shard_map/ppermute | solution.py:65
  49.7 5.5 %collective-permute-start.3 = (bf16[16,400,128]{2,1,0:T(8,128)(2,1)S(1)}, bf16[16,400,128]{2,1,0:T(8,128)(2,1)}, u32[]{:S(2)}, u32[]{:S(2)}) collective-permute-start(bf16[16,400,128]{2,1,0:T(8,128)(2,1)S(1)} %all-to-all-done.half), channel_id=1, source_target_pairs={{0,32},{1,33},{2,34},{3,35},{4,36},{5,37},{6,38},{7,39},{8,40},{9,... | collective-permute-start | bytes 4915208 | tf_op jit(solution)/shard_map/ppermute | solution.py:65
  60.8 1.2 copy-start
  61.9 15.6 %collective-permute-start.4 = (bf16[16,400,128]{2,1,0:T(8,128)(2,1)}, bf16[16,400,128]{2,1,0:T(8,128)(2,1)}, u32[]{:S(2)}, u32[]{:S(2)}) collective-permute-start(bf16[16,400,128]{2,1,0:T(8,128)(2,1)} %get-tuple-element.58), channel_id=1, source_target_pairs={{0,32},{1,33},{2,34},{3,35},{4,36},{5,37},{6,38},{7,39},{8,40},{9,... | collective-permute-start | bytes 4915208 | tf_op jit(solution)/shard_map/ppermute | solution.py:65
  64.0 25.8 %all-to-all-start.1 = ((bf16[32,80,128]{2,1,0:T(8,128)(2,1)}), bf16[32,80,128]{2,1,0:T(8,128)(2,1)S(1)}, u32[]{:S(2)}, u32[]{:S(2)}) async-start(bf16[32,80,128]{2,1,0:T(8,128)(2,1)} %bitcast.16), calls=%async_computation.1 | async-start | bytes 1310720 | tf_op jit(solution)/shard_map/all_to_all | solution.py:69
  89.8 0.8 copy-start.10
  90.6 26.7 %all-to-all-start.2 = ((bf16[16,400,128]{2,1,0:T(8,128)(2,1)}), bf16[16,400,128]{2,1,0:T(8,128)(2,1)S(1)}, u32[]{:S(2)}, u32[]{:S(2)}) async-start(bf16[16,400,128]{2,1,0:T(8,128)(2,1)} %add.59), calls=%async_computation.2 | async-start | bytes 3276800 | tf_op jit(solution)/shard_map/all_to_all | solution.py:69
  95.5 5.0 %collective-permute-start.5 = (f32[80,128]{1,0:T(8,128)S(1)}, f32[80,128]{1,0:T(8,128)S(1)}, u32[]{:S(2)}, u32[]{:S(2)}) collective-permute-start(f32[80,128]{1,0:T(8,128)S(1)} %convert_reduce_fusion.1), channel_id=1, source_target_pairs={{0,4},{1,5},{2,6},{3,7},{4,0},{5,1},{6,2},{7,3},{8,12},{9,13},{10,... | collective-permute-start | bytes 122888 | tf_op jit(solution)/shard_map/ppermute | solution.py:65
  100.6 7.8 %collective-permute-start.6 = (f32[80,128]{1,0:T(8,128)S(1)}, f32[80,128]{1,0:T(8,128)S(1)}, u32[]{:S(2)}, u32[]{:S(2)}) collective-permute-start(f32[80,128]{1,0:T(8,128)S(1)} %add.60), channel_id=1, source_target_pairs={{0,8},{1,9},{2,10},{3,11},{4,12},{5,13},{6,14},{7,15},{8,0},{9,1},... | collective-permute-start | bytes 122888 | tf_op jit(solution)/shard_map/ppermute | solution.py:65
  108.4 8.4 %collective-permute-start.7 = (bf16[80,128]{1,0:T(8,128)(2,1)S(1)}, bf16[80,128]{1,0:T(8,128)(2,1)S(1)}, u32[]{:S(2)}, u32[]{:S(2)}) collective-permute-start(bf16[80,128]{1,0:T(8,128)(2,1)S(1)} %add_convert_fusion.1), channel_id=1, source_target_pairs={{0,16},{1,17},{2,18},{3,19},{4,20},{5,21},{6,22},{7,23},{8,24},{9,... | collective-permute-start | bytes 61448 | tf_op jit(solution)/shard_map/ppermute | solution.py:65
  117.9 0.7 copy-start.8
  119.9 29.1 %all-to-all-start.3 = ((bf16[16,400,128]{2,1,0:T(8,128)(2,1)}), bf16[16,400,128]{2,1,0:T(8,128)(2,1)}, u32[]{:S(2)}, u32[]{:S(2)}) async-start(bf16[16,400,128]{2,1,0:T(8,128)(2,1)} %broadcast_in_dim.34), calls=%async_computation.3 | async-start | bytes 3276800 | tf_op jit(solution)/shard_map/all_to_all | solution.py:69
  126.2 38.1 %copy-start.9 = (f32[408,128]{1,0:T(8,128)S(1)}, f32[408,128]{1,0:T(8,128)}, u32[]{:S(2)}) copy-start(f32[408,128]{1,0:T(8,128)} %copy-done.8) | copy-start | bytes 626692
  126.2 18.0 %collective-permute-start.9 = (bf16[80,128]{1,0:T(8,128)(2,1)S(1)}, bf16[80,128]{1,0:T(8,128)(2,1)S(1)}, u32[]{:S(2)}, u32[]{:S(2)}) collective-permute-start(bf16[80,128]{1,0:T(8,128)(2,1)S(1)} %convert_add_fusion.3), channel_id=1, source_target_pairs={{0,256},{1,257},{2,258},{3,259},{4,260},{5,261},{6,262},{7,263},{8... | collective-permute-start | bytes 61448 | tf_op jit(solution)/shard_map/ppermute | solution.py:65
  142.3 6.7 %collective-permute-start.8 = (bf16[432,128]{1,0:T(8,128)(2,1)S(1)}, bf16[432,128]{1,0:T(8,128)(2,1)S(1)}, u32[]{:S(2)}, u32[]{:S(2)}) collective-permute-start(bf16[432,128]{1,0:T(8,128)(2,1)S(1)} %pad_maximum_fusion.1), channel_id=1, source_target_pairs={{0,16},{1,17},{2,18},{3,19},{64,80},{65,81},{66,82},{67,83},{128,1... | collective-permute-start | bytes 331784 | tf_op jit(solution)/shard_map/ppermute | solution.py:65
  149.0 30.9 %collective-permute-start.10 = (bf16[16,400,128]{2,1,0:T(8,128)(2,1)}, bf16[16,400,128]{2,1,0:T(8,128)(2,1)}, u32[]{:S(2)}, u32[]{:S(2)}) collective-permute-start(bf16[16,400,128]{2,1,0:T(8,128)(2,1)} %all-to-all-done.3.half), channel_id=1, source_target_pairs={{0,32},{1,33},{2,34},{3,35},{4,36},{5,37},{6,38},{7,39},{8,40},{9,... | collective-permute-start | bytes 4915208 | tf_op jit(solution)/shard_map/ppermute | solution.py:65
  157.0 19.6 %all-to-all-start.4 = ((bf16[32,80,128]{2,1,0:T(8,128)(2,1)}), bf16[32,80,128]{2,1,0:T(8,128)(2,1)S(1)}, u32[]{:S(2)}, u32[]{:S(2)}) async-start(bf16[32,80,128]{2,1,0:T(8,128)(2,1)} %broadcast_in_dim.35), calls=%async_computation.4 | async-start | bytes 1310720 | tf_op jit(solution)/shard_map/all_to_all | solution.py:69
  164.4 15.6 %collective-permute-start.11 = (f32[408,128]{1,0:T(8,128)S(1)}, f32[408,128]{1,0:T(8,128)S(1)}, u32[]{:S(2)}, u32[]{:S(2)}) collective-permute-start(f32[408,128]{1,0:T(8,128)S(1)} %copy-done.9), channel_id=1, source_target_pairs={{0,0},{1,1},{2,2},{3,3},{4,64},{5,65},{6,66},{7,67},{8,128},{9,129... | collective-permute-start | bytes 626696 | tf_op jit(solution)/shard_map/ppermute | solution.py:65
  176.6 1.3 copy-start.1
  178.9 1.0 copy-start.4
  179.9 5.9 %copy-start.2 = (f32[400,768]{1,0:T(8,128)}, f32[400,768]{1,0:T(8,128)S(1)}, u32[]{:S(2)}) copy-start(f32[400,768]{1,0:T(8,128)S(1)} %get-tuple-element.69.rel) | copy-start | bytes 3686404
  179.9 5.9 %copy-start.12 = (f32[408,128]{1,0:T(8,128)}, f32[408,128]{1,0:T(8,128)S(1)}, u32[]{:S(2)}) copy-start(f32[408,128]{1,0:T(8,128)S(1)} %collective-permute-done.11.kept) | copy-start | bytes 626692
  185.9 17.1 %collective-permute-start.12 = (bf16[16,400,128]{2,1,0:T(8,128)(2,1)}, bf16[16,400,128]{2,1,0:T(8,128)(2,1)}, u32[]{:S(2)}, u32[]{:S(2)}) collective-permute-start(bf16[16,400,128]{2,1,0:T(8,128)(2,1)} %get-tuple-element.74), channel_id=1, source_target_pairs={{0,32},{1,33},{2,34},{3,35},{4,36},{5,37},{6,38},{7,39},{8,40},{9,... | collective-permute-start | bytes 4915208 | tf_op jit(solution)/shard_map/ppermute | solution.py:65
  189.0 26.2 %all-to-all-start.5 = ((bf16[32,80,128]{2,1,0:T(8,128)(2,1)}), bf16[32,80,128]{2,1,0:T(8,128)(2,1)S(1)}, u32[]{:S(2)}, u32[]{:S(2)}) async-start(bf16[32,80,128]{2,1,0:T(8,128)(2,1)} %bitcast.20), calls=%async_computation.5 | async-start | bytes 1310720 | tf_op jit(solution)/shard_map/all_to_all | solution.py:69
  215.3 52.2 %all-to-all-start.6 = ((bf16[16,400,128]{2,1,0:T(8,128)(2,1)}), bf16[16,400,128]{2,1,0:T(8,128)(2,1)S(1)}, u32[]{:S(2)}, u32[]{:S(2)}) async-start(bf16[16,400,128]{2,1,0:T(8,128)(2,1)} %add.64), calls=%async_computation.6 | async-start | bytes 3276800 | tf_op jit(solution)/shard_map/all_to_all | solution.py:69
  219.1 7.8 %collective-permute-start.13 = (f32[80,128]{1,0:T(8,128)S(1)}, f32[80,128]{1,0:T(8,128)S(1)}, u32[]{:S(2)}, u32[]{:S(2)}) collective-permute-start(f32[80,128]{1,0:T(8,128)S(1)} %convert_reduce_fusion), channel_id=1, source_target_pairs={{0,4},{1,5},{2,6},{3,7},{4,0},{5,1},{6,2},{7,3},{8,12},{9,13},{10,... | collective-permute-start | bytes 122888 | tf_op jit(solution)/shard_map/ppermute | solution.py:65
  226.9 5.9 %collective-permute-start.14 = (f32[80,128]{1,0:T(8,128)S(1)}, f32[80,128]{1,0:T(8,128)S(1)}, u32[]{:S(2)}, u32[]{:S(2)}) collective-permute-start(f32[80,128]{1,0:T(8,128)S(1)} %add.65), channel_id=1, source_target_pairs={{0,8},{1,9},{2,10},{3,11},{4,12},{5,13},{6,14},{7,15},{8,0},{9,1},... | collective-permute-start | bytes 122888 | tf_op jit(solution)/shard_map/ppermute | solution.py:65
  232.8 8.4 %collective-permute-start.15 = (bf16[80,128]{1,0:T(8,128)(2,1)S(1)}, bf16[80,128]{1,0:T(8,128)(2,1)S(1)}, u32[]{:S(2)}, u32[]{:S(2)}) collective-permute-start(bf16[80,128]{1,0:T(8,128)(2,1)S(1)} %add_convert_fusion), channel_id=1, source_target_pairs={{0,16},{1,17},{2,18},{3,19},{4,20},{5,21},{6,22},{7,23},{8,24},{9,... | collective-permute-start | bytes 61448 | tf_op jit(solution)/shard_map/ppermute | solution.py:65
  236.3 17.3 %collective-permute-start.16 = (bf16[400,128]{1,0:T(8,128)(2,1)S(1)}, bf16[400,128]{1,0:T(8,128)(2,1)S(1)}, u32[]{:S(2)}, u32[]{:S(2)}) collective-permute-start(bf16[400,128]{1,0:T(8,128)(2,1)S(1)} %convert_element_type.75), channel_id=1, source_target_pairs={{16,0},{17,1},{18,2},{19,3},{80,64},{81,65},{82,66},{83,67},{144,1... | collective-permute-start | bytes 307208 | tf_op jit(solution)/shard_map/ppermute | solution.py:65
  253.5 0.6 copy-start.6
  254.2 13.2 %collective-permute-start.17 = (bf16[80,128]{1,0:T(8,128)(2,1)S(1)}, bf16[80,128]{1,0:T(8,128)(2,1)S(1)}, u32[]{:S(2)}, u32[]{:S(2)}) collective-permute-start(bf16[80,128]{1,0:T(8,128)(2,1)S(1)} %convert_add_fusion.1), channel_id=1, source_target_pairs={{0,256},{1,257},{2,258},{3,259},{4,260},{5,261},{6,262},{7,263},{8... | collective-permute-start | bytes 61448 | tf_op jit(solution)/shard_map/ppermute | solution.py:65
  268.4 22.0 %copy-start.3 = (f32[400,768]{1,0:T(8,128)S(1)}, f32[400,768]{1,0:T(8,128)}, u32[]{:S(2)}) copy-start(f32[400,768]{1,0:T(8,128)} %copy-done.2) | copy-start | bytes 3686404
  268.4 22.0 %all-to-all-start.7 = ((bf16[32,80,128]{2,1,0:T(8,128)(2,1)}), bf16[32,80,128]{2,1,0:T(8,128)(2,1)S(1)}, u32[]{:S(2)}, u32[]{:S(2)}) async-start(bf16[32,80,128]{2,1,0:T(8,128)(2,1)} %broadcast_in_dim.36), calls=%async_computation.7 | async-start | bytes 1310720 | tf_op jit(solution)/shard_map/all_to_all | solution.py:69
  278.1 0.9 copy-start.7
  280.1 13.9 %collective-permute-start.18 = (bf16[400,128]{1,0:T(8,128)(2,1)}, bf16[400,128]{1,0:T(8,128)(2,1)S(1)}, u32[]{:S(2)}, u32[]{:S(2)}) collective-permute-start(bf16[400,128]{1,0:T(8,128)(2,1)} %fold_pieces.1), channel_id=1, source_target_pairs={{0,0},{1,1},{2,2},{3,3},{4,64},{5,65},{6,66},{7,67},{8,128},{9,129... | collective-permute-start | bytes 307208 | tf_op jit(solution)/shard_map/ppermute | solution.py:65
  290.4 1.3 copy-start.5
  294.0 0.6 copy-start.13
